TPU v7x, 128 devices: a whole 4x4x4 slice. The times are simulated.
128 devices in a mesh: lat: 8 (over z, x_hi), lon: 16 (over x_lo, y, core).
Axes of the slice: x: 4 (x_hi: 2, x_lo: 2; x = x_hi * 2 + x_lo), y: 4, z: 4, core: 2. Of those that a mesh axis runs over, the one named last changes fastest.
Arguments:
- adjoint_displacement: float32 [2, 8, 5, 640, 640], P(None, 'lat', None, 'lon'), may hold values from -0.08 to 0.08, as said below
- adjoint_velocity: float32 [2, 8, 5, 640, 640], P(None, 'lat', None, 'lon'), may hold values from -8 to 8, as said below
- bulk_modulus_field: bfloat16 [8, 5, 640, 640], P('lat', None, 'lon'), may hold values from 0.5 to 2
- density: bfloat16 [8, 5, 640, 640], P('lat', None, 'lon'), may hold values from 1 to 3
- forward_displacement: bfloat16 [2, 2, 8, 5, 640, 640], P(None, None, 'lat', None, 'lon'), may hold values from -8 to 8, as said below
- adjoint_traces: float32 [2, 3, 131072], P(None, None, ('lat', 'lon')), may hold values from -1.5 to 1.5
- receiver_owner: int32 [131072], P(('lat', 'lon')), may hold values from 0 to 127, as said below
- receiver_point: int32 [131072], P(('lat', 'lon')), may hold values from 0 to 127999
Outputs:
- final_velocity: float32 [2, 8, 5, 640, 640], P(None, 'lat', None, 'lon')
- modulus_kernel: float32 [8, 5, 640, 640], P('lat', None, 'lon')
Inputs may be any that keep to these rules, and one draw needn't show every extreme that they name: `adjoint_displacement`: equal on all element points that lie on one grid point. `adjoint_velocity`: equal on all element points that lie on one grid point. `forward_displacement`: equal on all element points that lie on one grid point. `receiver_owner`: among the 1024 receivers of one device at most 32 name the same owner; one owner, drawn from the seed, is named by exactly 32 receivers of every device.
All inputs are finite; a program needn't handle non-finite values.
Results may differ from a plain program's by a relative error of at most 0.0003.
Values sent between devices are 32-bit elements; how exact they have to be, the bound alone decides.
No kernel may reach another device: no remote copies, remote signals or barrier semaphores. Data moves between devices by JAX's collectives and lax.ppermute only.
A program may use at most 320 MiB of HBM per device.

v0:
```python
import math

import jax
import jax.numpy as jnp
import numpy as np
from jax import lax
from jax.sharding import PartitionSpec as P

time_step = 0.05
highest = lax.Precision.HIGHEST


def with_halo(block, sides, width):
    for axis, dim in sides:
        count = lax.axis_size(axis)
        forward = [(i, i + 1) for i in range(count - 1)]
        backward = [(target, source) for source, target in forward]
        low = lax.ppermute(
            lax.slice_in_dim(block, block.shape[dim] - width, None, axis=dim), axis, forward
        )
        high = lax.ppermute(lax.slice_in_dim(block, 0, width, axis=dim), axis, backward)
        block = jnp.concatenate([low, block, high], axis=dim)
    return block


def gll_tables():
    root_value = math.sqrt(3.0 / 7.0)
    gll_points = np.array([-1.0, -root_value, 0.0, root_value, 1.0])
    gll_weights = np.array([0.1, 49.0 / 90.0, 32.0 / 45.0, 49.0 / 90.0, 0.1])
    legendre = (35.0 * gll_points**4 - 30.0 * gll_points**2 + 3.0) / 8.0
    derivative = np.zeros((5, 5))
    for point_a in range(5):
        for point_b in range(5):
            if point_a != point_b:
                derivative[point_a, point_b] = (
                    legendre[point_a]
                    / legendre[point_b]
                    / (gll_points[point_a] - gll_points[point_b])
                )
    derivative[0, 0] = -5.0
    derivative[4, 4] = 5.0
    weight_cube = (
        gll_weights[:, None, None] * gll_weights[None, :, None] * gll_weights[None, None, :]
    )
    return (
        jnp.asarray(derivative, jnp.float32),
        jnp.asarray(weight_cube.reshape(1, 1, 5, 1, 5, 5, 1), jnp.float32),
    )


def element_view(field):
    count, blocks_x, unused, rows_y, depth_all = field.shape
    return field.reshape(count, blocks_x, 5, rows_y // 5, 5, 5, depth_all // 5)


def gradients(view, derivative):
    along_x = jnp.einsum("ai,rxiyjkz->rxayjkz", derivative, view, precision=highest)
    along_y = jnp.einsum("bj,rxiyjkz->rxiybkz", derivative, view, precision=highest)
    along_z = jnp.einsum("ck,rxiyjkz->rxiyjcz", derivative, view, precision=highest)
    return (along_x, along_y, along_z)


def stiffness(field, modulus, derivative, weight_cube):
    grads = gradients(element_view(field), derivative)
    scaled = weight_cube * element_view(modulus[None])
    force = jnp.einsum("ai,rxayjkz->rxiyjkz", derivative, scaled * grads[0], precision=highest)
    force = force + jnp.einsum(
        "bj,rxiybkz->rxiyjkz", derivative, scaled * grads[1], precision=highest
    )
    force = force + jnp.einsum(
        "ck,rxiyjcz->rxiyjkz", derivative, scaled * grads[2], precision=highest
    )
    return (force.reshape(field.shape), grads)


def kernel_term(grads, forward, modulus, derivative):
    forward_grads = gradients(element_view(forward.astype(jnp.float32)), derivative)
    total = grads[0] * forward_grads[0] + grads[1] * forward_grads[1] + grads[2] * forward_grads[2]
    summed = jnp.sum(total, axis=0) * element_view(modulus[None])[0]
    return summed.reshape(modulus.shape)


def local_mass(density, weight_cube):
    return (weight_cube * element_view(density.astype(jnp.float32)[None]))[0].reshape(density.shape)


def fold_faces(extended, axis_pos, blocks):
    length = extended.shape[axis_pos]
    outer_shape = extended.shape[:axis_pos]
    inner_shape = extended.shape[axis_pos + 1 :]
    interior = lax.slice_in_dim(extended, 1, length - 1, axis=axis_pos)
    split_view = interior.reshape(outer_shape + (blocks, 5) + inner_shape)
    below_rim = lax.slice_in_dim(extended, 0, 1, axis=axis_pos)
    above_rim = lax.slice_in_dim(extended, length - 1, length, axis=axis_pos)
    low_face = lax.index_in_dim(split_view, 0, axis_pos + 1, keepdims=False)
    high_face = lax.index_in_dim(split_view, 4, axis_pos + 1, keepdims=False)
    from_below = jnp.concatenate(
        [below_rim, lax.slice_in_dim(high_face, 0, blocks - 1, axis=axis_pos)], axis_pos
    )
    from_above = jnp.concatenate(
        [lax.slice_in_dim(low_face, 1, blocks, axis=axis_pos), above_rim], axis_pos
    )
    middle = lax.slice_in_dim(split_view, 1, 4, axis=axis_pos + 1)
    joined = jnp.concatenate(
        [
            jnp.expand_dims(low_face + from_below, axis_pos + 1),
            middle,
            jnp.expand_dims(high_face + from_above, axis_pos + 1),
        ],
        axis_pos + 1,
    )
    return joined.reshape(outer_shape + (blocks * 5,) + inner_shape)


def fold_depth(field):
    leading_shape = field.shape[:-1]
    depth = field.shape[-1] // 5
    split_view = field.reshape(leading_shape + (5, depth))
    low_face = split_view[..., 0, :]
    high_face = split_view[..., 4, :]
    zero_line = jnp.zeros(leading_shape + (1,), field.dtype)
    from_below = jnp.concatenate([zero_line, high_face[..., :-1]], -1)
    from_above = jnp.concatenate([low_face[..., 1:], zero_line], -1)
    joined = jnp.concatenate(
        [
            (low_face + from_below)[..., None, :],
            split_view[..., 1:4, :],
            (high_face + from_above)[..., None, :],
        ],
        -2,
    )
    return joined.reshape(field.shape)


def assemble(field):
    count, blocks_x, unused, rows_y, depth_all = field.shape
    merged = field.reshape(count, blocks_x * 5, rows_y, depth_all)
    extended = with_halo(merged, (("lat", 1),), 1)
    merged = fold_faces(extended, 1, blocks_x)
    extended = with_halo(merged, (("lon", 2),), 1)
    merged = fold_faces(extended, 2, rows_y // 5)
    return fold_depth(merged).reshape(field.shape)


def fill_slots(flat_traces, receiver_owner, receiver_point, devices, capacity):
    owner_table = (receiver_owner[:, None] == jnp.arange(devices, dtype=jnp.int32)[None, :]).astype(
        jnp.int32
    )
    earlier = jnp.cumsum(owner_table, axis=0) - owner_table
    order_rank = jnp.sum(earlier * owner_table, axis=1)
    slot_index = receiver_owner * capacity + order_rank
    send_values = (
        jnp.zeros((flat_traces.shape[0], devices * capacity), jnp.float32)
        .at[:, slot_index]
        .set(flat_traces)
    )
    send_points = (
        jnp.zeros((1, devices * capacity), jnp.int32).at[:, slot_index].set(receiver_point[None, :])
    )
    return (send_values, send_points)


def deliver(adjoint_traces, receiver_owner, receiver_point):
    run_count, time_count, receivers = adjoint_traces.shape
    lat_count = lax.axis_size("lat")
    lon_count = lax.axis_size("lon")
    devices = lat_count * lon_count
    capacity = 4 * receivers // devices
    trace_rows = run_count * time_count
    flat_traces = adjoint_traces.reshape(trace_rows, receivers)
    send_values, send_points = fill_slots(
        flat_traces, receiver_owner, receiver_point, devices, capacity
    )
    got_values, got_points = (
        lax.all_to_all(
            send_values.reshape(trace_rows, devices, capacity),
            ("lat", "lon"),
            split_axis=1,
            concat_axis=1,
            tiled=True,
        ),
        lax.all_to_all(
            send_points.reshape(1, devices, capacity),
            ("lat", "lon"),
            split_axis=1,
            concat_axis=1,
            tiled=True,
        ),
    )
    return (got_values.reshape(trace_rows, -1), got_points.reshape(-1))


def on_device(
    adjoint_displacement,
    adjoint_velocity,
    bulk_modulus_field,
    density,
    forward_displacement,
    adjoint_traces,
    receiver_owner,
    receiver_point,
):
    derivative, weight_cube = gll_tables()
    modulus = bulk_modulus_field.astype(jnp.float32)
    run_count = adjoint_displacement.shape[0]
    step_count = forward_displacement.shape[0]
    point_count = modulus.size
    values, targets = deliver(adjoint_traces, receiver_owner, receiver_point)
    sources = jnp.zeros((values.shape[0], point_count), jnp.float32).at[:, targets].add(values)
    sources = sources.reshape((run_count, step_count + 1) + modulus.shape)
    mass = assemble(local_mass(density, weight_cube)[None])[0]
    force, unused = stiffness(adjoint_displacement, modulus, derivative, weight_cube)
    acceleration = assemble(sources[:, 0] - force) / mass
    displacement = adjoint_displacement
    velocity = adjoint_velocity
    kernel = jnp.zeros(modulus.shape, jnp.float32)
    for step_index in range(step_count):
        displacement = (
            displacement + time_step * velocity + 0.5 * time_step * time_step * acceleration
        )
        velocity = velocity + 0.5 * time_step * acceleration
        force, grads = stiffness(displacement, modulus, derivative, weight_cube)
        acceleration = assemble(sources[:, step_index + 1] - force) / mass
        velocity = velocity + 0.5 * time_step * acceleration
        kernel = kernel - time_step * kernel_term(
            grads, forward_displacement[step_index], modulus, derivative
        )
    return (velocity, kernel)


def solution(mesh):
    placed = (
        P(None, "lat", None, "lon", None),
        P(None, "lat", None, "lon", None),
        P("lat", None, "lon", None),
        P("lat", None, "lon", None),
        P(None, None, "lat", None, "lon", None),
        P(None, None, ("lat", "lon")),
        P(("lat", "lon")),
        P(("lat", "lon")),
    )
    return jax.shard_map(
        on_device,
        mesh=mesh,
        in_specs=placed,
        out_specs=(P(None, "lat", None, "lon", None), P("lat", None, "lon", None)),
        check_vma=False,
    )
```

profile of v0, /device:TPU:25, one launch (start us, length us, event | category | flops | bytes accessed | tf_op | source)
XLA Modules:
  0.0 397.9 jit_solution(4779614800566991630)
XLA Ops:
  2.3 4.5 %scatter_custom_fusion = s32[4096]{0:T(1024)S(1)} fusion(s32[1024]{0:T(1024)S(1)} %compare_select_fusion.1, s32[1024]{0:T(1024)} %param.17, s32[]{:T(128)} %constant.11.clone.1), kind=kCustom, calls=%fused_computation.197 | custom fusion | bytes 16896 | tf_op jit(solution)/shard_map/scatter | solution.py:158
  7.5 10.6 %all-to-all-start = ((s32[1,128,32]{2,0,1:T(1,128)}), s32[1,128,32]{2,0,1:T(1,128)S(1)}, u32[]{:S(2)}, u32[]{:S(2)}) async-start(s32[1,128,32]{2,0,1:T(1,128)} %bitcast.5), calls=%async_computation | async-start | bytes 131072 | tf_op jit(solution)/shard_map/all_to_all | solution.py:182
  19.2 5.3 %collective-permute-start.4 = (f32[1,1,40,640]{3,2,1,0:T(8,128)}, f32[1,1,40,640]{3,2,1,0:T(8,128)}, u32[]{:S(2)}, u32[]{:S(2)}) collective-permute-start(f32[1,1,40,640]{3,2,1,0:T(8,128)} %get-tuple-element.61), channel_id=1, source_target_pairs={{0,16},{16,32},{32,48},{48,64},{64,80},{80,96},{96,112},{1,17},{17... | collective-permute-start | bytes 307208 | tf_op jit(solution)/shard_map/ppermute | solution.py:18
  26.1 2.6 fusion.114
  28.7 2.8 fusion.47
  31.5 3.2 fusion.49
  36.7 2.0 fusion.117
  38.7 2.0 fusion.73
  43.3 2.0 fusion.70
  52.5 2.7 bitcast_add_fusion.4
  59.3 3.6 scatter_custom_fusion.1
  66.7 11.7 %all-to-all-start.1 = ((f32[128,1,192]{2,1,0:T(1,128)}), f32[128,1,192]{2,1,0:T(1,128)S(1)}, u32[]{:S(2)}, u32[]{:S(2)}) async-start(f32[128,1,192]{2,1,0:T(1,128)} %reshape.540), calls=%async_computation.1 | async-start | bytes 262144 | tf_op jit(solution)/shard_map/all_to_all | solution.py:175
  79.8 5.1 %sort = (s32[4096]{0:T(1024)S(1)}, s32[4096]{0:T(1024)S(1)}) sort(s32[4096]{0:T(1024)S(1)} %bitcast.617, s32[4096]{0:T(1024)S(1)} %iota.8), dimensions={0}, to_apply=%compare | sort | flops 49152 | bytes 65536 | tf_op jit(solution)/shard_map/scatter-add | solution.py:209
  92.2 82.6 %scatter_custom_fusion.2 = f32[6,128000]{0,1:T(8,128)} fusion(s32[4096]{0:T(1024)S(1)} %get-tuple-element.10, f32[]{:T(128)} %constant.10.clone.1, f32[4096,6]{1,0:T(8,128)} %copy.451, s32[4096]{0:T(1024)S(1)} %broadcast_clamp_fusion), kind=kCustom, calls=%fused_computation.4 | custom fusion | flops 24576 | bytes 3072512 | tf_op jit(solution)/shard_map/scatter-add | solution.py:209
  174.8 34.6 %copy.452 = f32[6,128000]{1,0:T(8,128)} copy(f32[6,128000]{0,1:T(8,128)} %scatter_custom_fusion.2) | data formatting | bytes 6144000 | tf_op jit(solution)/shard_map/scatter-add | solution.py:209
  209.4 2.8 copy.613
  215.0 3.6 collective-permute-start
  222.8 4.5 %collective-permute-start.6 = (f32[1,5,1,640]{3,2,1,0:T(1,128)S(1)}, f32[1,5,1,640]{3,2,1,0:T(1,128)S(1)}, u32[]{:S(2)}, u32[]{:S(2)}) collective-permute-start(f32[1,5,1,640]{3,2,1,0:T(1,128)S(1)} %get-tuple-element.57), channel_id=1, source_target_pairs={{0,1},{1,2},{2,3},{3,4},{4,5},{5,6},{6,7},{7,8},{8,9},{9,10},{10,1... | collective-permute-start | bytes 38408 | tf_op jit(solution)/shard_map/ppermute | solution.py:18
  229.6 5.0 %collective-permute-done.7 = f32[1,5,1,640]{3,2,1,0:T(1,128)S(1)} collective-permute-done((f32[1,5,1,640]{3,2,1,0:T(1,128)S(1)}, f32[1,5,1,640]{3,2,1,0:T(1,128)S(1)}, u32[]{:S(2)}, u32[]{:S(2)}) %collective-permute-start.7) | collective-permute-done | bytes 12832 | tf_op jit(solution)/shard_map/ppermute | solution.py:21
  244.7 2.4 collective-permute-start.3
  247.3 4.6 %collective-permute-done.3 = f32[2,5,1,640]{3,2,1,0:T(1,128)S(1)} collective-permute-done((f32[2,5,1,640]{3,2,1,0:T(1,128)S(1)}, f32[2,5,1,640]{3,2,1,0:T(1,128)S(1)}, u32[]{:S(2)}, u32[]{:S(2)}) %collective-permute-start.3) | collective-permute-done | bytes 25632 | tf_op jit(solution)/shard_map/ppermute | solution.py:21
  253.4 2.0 reshape_reshape.25
  258.4 2.1 reshape.519
  260.5 2.4 fusion.68
  267.9 2.0 fusion.41
  274.6 2.9 bitcast_add_fusion.2
  280.8 3.4 fusion.10
  285.2 2.1 reduce_sum.33
  287.3 2.5 reshape.466
  292.8 6.4 %collective-permute-start.8 = (f32[2,1,40,640]{3,2,0,1:T(8,128)S(1)}, f32[2,1,40,640]{3,2,0,1:T(8,128)S(1)}, u32[]{:S(2)}, u32[]{:S(2)}) collective-permute-start(f32[2,1,40,640]{3,2,0,1:T(8,128)S(1)} %get-tuple-element.41), channel_id=1, source_target_pairs={{0,16},{16,32},{32,48},{48,64},{64,80},{80,96},{96,112},{1,17},{17... | collective-permute-start | bytes 614408 | tf_op jit(solution)/shard_map/ppermute | solution.py:18
  302.2 6.2 %collective-permute-done.9 = f32[2,1,40,640]{3,2,0,1:T(8,128)S(1)} collective-permute-done((f32[2,1,40,640]{3,2,0,1:T(8,128)S(1)}, f32[2,1,40,640]{3,2,0,1:T(8,128)S(1)}, u32[]{:S(2)}, u32[]{:S(2)}) %collective-permute-start.9) | collective-permute-done | bytes 204832 | tf_op jit(solution)/shard_map/ppermute | solution.py:21
  311.0 2.4 collective-permute-start.11
  313.7 4.6 %collective-permute-done.11 = f32[2,5,1,640]{3,2,1,0:T(1,128)S(1)} collective-permute-done((f32[2,5,1,640]{3,2,1,0:T(1,128)S(1)}, f32[2,5,1,640]{3,2,1,0:T(1,128)S(1)}, u32[]{:S(2)}, u32[]{:S(2)}) %collective-permute-start.11) | collective-permute-done | bytes 25632 | tf_op jit(solution)/shard_map/ppermute | solution.py:21
  319.7 2.0 reshape_reshape.28
  324.7 2.0 reshape.521
  327.7 3.0 multiply_add_fusion
  335.5 2.0 fusion.33
  342.3 3.1 bitcast_add_fusion
  348.6 3.4 fusion.7
  353.1 2.5 reshape.473
  355.6 2.6 bitcast_subtract_fusion
  361.2 5.5 %collective-permute-start.12 = (f32[2,1,40,640]{3,2,0,1:T(8,128)S(1)}, f32[2,1,40,640]{3,2,0,1:T(8,128)S(1)}, u32[]{:S(2)}, u32[]{:S(2)}) collective-permute-start(f32[2,1,40,640]{3,2,0,1:T(8,128)S(1)} %get-tuple-element.35), channel_id=1, source_target_pairs={{0,16},{16,32},{32,48},{48,64},{64,80},{80,96},{96,112},{1,17},{17... | collective-permute-start | bytes 614408 | tf_op jit(solution)/shard_map/ppermute | solution.py:18
  369.4 5.3 %collective-permute-done.13 = f32[2,1,40,640]{3,2,0,1:T(8,128)S(1)} collective-permute-done((f32[2,1,40,640]{3,2,0,1:T(8,128)S(1)}, f32[2,1,40,640]{3,2,0,1:T(8,128)S(1)}, u32[]{:S(2)}, u32[]{:S(2)}) %collective-permute-start.13) | collective-permute-done | bytes 204832 | tf_op jit(solution)/shard_map/ppermute | solution.py:21
  375.1 2.7 collective-permute-start.14
  380.2 5.1 %collective-permute-done.15 = f32[2,5,1,640]{3,2,1,0:T(1,128)S(1)} collective-permute-done((f32[2,5,1,640]{3,2,1,0:T(1,128)S(1)}, f32[2,5,1,640]{3,2,1,0:T(1,128)S(1)}, u32[]{:S(2)}, u32[]{:S(2)}) %collective-permute-start.15) | collective-permute-done | bytes 25632 | tf_op jit(solution)/shard_map/ppermute | solution.py:21
  386.9 2.0 reshape_reshape.30
  392.0 2.9 reshape.523
  394.9 2.9 fusion.67
  (253 shorter events, 111.5 us)
Async XLA Ops:
  0.6 1.3 copy-start.33
  1.5 16.6 %copy-start.31 = (f32[5,5,5]{2,1,0:T(8,128)S(1)}, f32[5,5,5]{2,1,0:T(8,128)}, u32[]{:S(2)}) copy-start(f32[5,5,5]{2,1,0:T(8,128)} %constant.56) | copy-start | bytes 1504
  1.9 16.5 %copy-start.27 = (bf16[1,5,40,640]{3,2,1,0:T(8,128)(2,1)S(1)}, bf16[1,5,40,640]{3,2,1,0:T(8,128)(2,1)}, u32[]{:S(2)}) copy-start(bf16[1,5,40,640]{3,2,1,0:T(8,128)(2,1)} %param.13) | copy-start | bytes 768004
  7.5 59.2 %all-to-all-start = ((s32[1,128,32]{2,0,1:T(1,128)}), s32[1,128,32]{2,0,1:T(1,128)S(1)}, u32[]{:S(2)}, u32[]{:S(2)}) async-start(s32[1,128,32]{2,0,1:T(1,128)} %bitcast.5), calls=%async_computation | async-start | bytes 131072 | tf_op jit(solution)/shard_map/all_to_all | solution.py:182
  18.2 7.7 %copy-start.8 = (f32[2,1,5,40,640]{4,3,2,1,0:T(8,128)S(1)}, f32[2,1,5,40,640]{4,3,2,1,0:T(8,128)}, u32[]{:S(2)}) copy-start(f32[2,1,5,40,640]{4,3,2,1,0:T(8,128)} %param.10) | copy-start | bytes 3072004
  18.5 7.6 %copy-start.23 = (f32[5,5,1,1,1,1]{1,0,5,4,3,2:T(8,128)S(1)}, f32[5,5,1,1,1,1]{1,0,5,4,3,2:T(8,128)}, u32[]{:S(2)}) copy-start(f32[5,5,1,1,1,1]{1,0,5,4,3,2:T(8,128)} %constant.57) | copy-start | bytes 304
  19.2 202.3 %collective-permute-start.4 = (f32[1,1,40,640]{3,2,1,0:T(8,128)}, f32[1,1,40,640]{3,2,1,0:T(8,128)}, u32[]{:S(2)}, u32[]{:S(2)}) collective-permute-start(f32[1,1,40,640]{3,2,1,0:T(8,128)} %get-tuple-element.61), channel_id=1, source_target_pairs={{0,16},{16,32},{32,48},{48,64},{64,80},{80,96},{96,112},{1,17},{17... | collective-permute-start | bytes 307208 | tf_op jit(solution)/shard_map/ppermute | solution.py:18
  24.4 197.0 %collective-permute-start.5 = (f32[1,1,40,640]{3,2,1,0:T(8,128)}, f32[1,1,40,640]{3,2,1,0:T(8,128)}, u32[]{:S(2)}, u32[]{:S(2)}) collective-permute-start(f32[1,1,40,640]{3,2,1,0:T(8,128)} %get-tuple-element.62), channel_id=1, source_target_pairs={{16,0},{32,16},{48,32},{64,48},{80,64},{96,80},{112,96},{17,1},{33... | collective-permute-start | bytes 307208 | tf_op jit(solution)/shard_map/ppermute | solution.py:21
  36.7 4.0 %copy-start.3 = (bf16[2,5,8,5,5,128]{5,4,3,2,1,0:T(8,128)(2,1)}, bf16[2,5,8,5,5,128]{5,4,3,2,1,0:T(8,128)(2,1)S(1)}, u32[]{:S(2)}) copy-start(bf16[2,5,8,5,5,128]{5,4,3,2,1,0:T(8,128)(2,1)S(1)} %reshape.476) | copy-start | bytes 1536004
  41.3 4.0 copy-start.1
  43.3 2.0 copy-start.29
  43.3 2.3 copy-start.32
  45.6 1.4 copy-start.12
  45.6 1.9 copy-start.13
  50.7 1.7 copy-start.14
  52.5 2.7 copy-start.28
  63.8 2.6 copy-start.24
  66.7 20.0 %all-to-all-start.1 = ((f32[128,1,192]{2,1,0:T(1,128)}), f32[128,1,192]{2,1,0:T(1,128)S(1)}, u32[]{:S(2)}, u32[]{:S(2)}) async-start(f32[128,1,192]{2,1,0:T(1,128)} %reshape.540), calls=%async_computation.1 | async-start | bytes 262144 | tf_op jit(solution)/shard_map/all_to_all | solution.py:175
  212.1 7.8 %copy-start = (f32[1,6,200,640]{3,2,1,0:T(8,128)}, f32[1,6,200,640]{3,2,1,0:T(8,128)S(1)}, u32[]{:S(2)}) copy-start(f32[1,6,200,640]{3,2,1,0:T(8,128)S(1)} %copy.613) | copy-start | bytes 9216004
  212.2 2.0 copy-start.21
  215.0 25.7 %collective-permute-start = (f32[2,1,40,640]{3,2,0,1:T(8,128)}, f32[2,1,40,640]{3,2,0,1:T(8,128)}, u32[]{:S(2)}, u32[]{:S(2)}) collective-permute-start(f32[2,1,40,640]{3,2,0,1:T(8,128)} %get-tuple-element.47), channel_id=1, source_target_pairs={{0,16},{16,32},{32,48},{48,64},{64,80},{80,96},{96,112},{1,17},{17... | collective-permute-start | bytes 614408 | tf_op jit(solution)/shard_map/ppermute | solution.py:18
  218.6 22.1 %collective-permute-start.1 = (f32[2,1,40,640]{3,2,0,1:T(8,128)}, f32[2,1,40,640]{3,2,0,1:T(8,128)}, u32[]{:S(2)}, u32[]{:S(2)}) collective-permute-start(f32[2,1,40,640]{3,2,0,1:T(8,128)} %get-tuple-element.48), channel_id=1, source_target_pairs={{16,0},{32,16},{48,32},{64,48},{80,64},{96,80},{112,96},{17,1},{33... | collective-permute-start | bytes 614408 | tf_op jit(solution)/shard_map/ppermute | solution.py:21
  222.8 6.6 %collective-permute-start.6 = (f32[1,5,1,640]{3,2,1,0:T(1,128)S(1)}, f32[1,5,1,640]{3,2,1,0:T(1,128)S(1)}, u32[]{:S(2)}, u32[]{:S(2)}) collective-permute-start(f32[1,5,1,640]{3,2,1,0:T(1,128)S(1)} %get-tuple-element.57), channel_id=1, source_target_pairs={{0,1},{1,2},{2,3},{3,4},{4,5},{5,6},{6,7},{7,8},{8,9},{9,10},{10,1... | collective-permute-start | bytes 38408 | tf_op jit(solution)/shard_map/ppermute | solution.py:18
  227.5 7.1 %collective-permute-start.7 = (f32[1,5,1,640]{3,2,1,0:T(1,128)S(1)}, f32[1,5,1,640]{3,2,1,0:T(1,128)S(1)}, u32[]{:S(2)}, u32[]{:S(2)}) collective-permute-start(f32[1,5,1,640]{3,2,1,0:T(1,128)S(1)} %get-tuple-element.58), channel_id=1, source_target_pairs={{1,0},{2,1},{3,2},{4,3},{5,4},{6,5},{7,6},{8,7},{9,8},{10,9},{11,1... | collective-permute-start | bytes 38408 | tf_op jit(solution)/shard_map/ppermute | solution.py:21
  240.7 19.7 %copy-start.9 = (f32[5,40,640]{2,1,0:T(8,128)}, f32[5,40,640]{2,1,0:T(8,128)S(1)}, u32[]{:S(2)}) copy-start(f32[5,40,640]{2,1,0:T(8,128)S(1)} %div.54) | copy-start | bytes 1536004
  242.6 4.5 %collective-permute-start.2 = (f32[2,5,1,640]{3,2,1,0:T(1,128)S(1)}, f32[2,5,1,640]{3,2,1,0:T(1,128)S(1)}, u32[]{:S(2)}, u32[]{:S(2)}) collective-permute-start(f32[2,5,1,640]{3,2,1,0:T(1,128)S(1)} %get-tuple-element.43), channel_id=1, source_target_pairs={{0,1},{1,2},{2,3},{3,4},{4,5},{5,6},{6,7},{7,8},{8,9},{9,10},{10,1... | collective-permute-start | bytes 76808 | tf_op jit(solution)/shard_map/ppermute | solution.py:18
  244.7 7.3 %collective-permute-start.3 = (f32[2,5,1,640]{3,2,1,0:T(1,128)S(1)}, f32[2,5,1,640]{3,2,1,0:T(1,128)S(1)}, u32[]{:S(2)}, u32[]{:S(2)}) collective-permute-start(f32[2,5,1,640]{3,2,1,0:T(1,128)S(1)} %get-tuple-element.44), channel_id=1, source_target_pairs={{1,0},{2,1},{3,2},{4,3},{5,4},{6,5},{7,6},{8,7},{9,8},{10,9},{11,1... | collective-permute-start | bytes 76808 | tf_op jit(solution)/shard_map/ppermute | solution.py:21
  258.4 2.1 copy-start.7
  277.6 1.8 copy-start.18
  279.0 1.8 copy-start.17
  291.1 9.5 %copy-start.22 = (f32[2,1,5,40,640]{4,3,2,0,1:T(8,128)S(1)}, f32[2,1,5,40,640]{4,3,2,0,1:T(8,128)}, u32[]{:S(2)}) copy-start(f32[2,1,5,40,640]{4,3,2,0,1:T(8,128)} %reshape.466) | copy-start | bytes 3072004
  292.8 9.4 %collective-permute-start.8 = (f32[2,1,40,640]{3,2,0,1:T(8,128)S(1)}, f32[2,1,40,640]{3,2,0,1:T(8,128)S(1)}, u32[]{:S(2)}, u32[]{:S(2)}) collective-permute-start(f32[2,1,40,640]{3,2,0,1:T(8,128)S(1)} %get-tuple-element.41), channel_id=1, source_target_pairs={{0,16},{16,32},{32,48},{48,64},{64,80},{80,96},{96,112},{1,17},{17... | collective-permute-start | bytes 614408 | tf_op jit(solution)/shard_map/ppermute | solution.py:18
  299.2 9.3 %collective-permute-start.9 = (f32[2,1,40,640]{3,2,0,1:T(8,128)S(1)}, f32[2,1,40,640]{3,2,0,1:T(8,128)S(1)}, u32[]{:S(2)}, u32[]{:S(2)}) collective-permute-start(f32[2,1,40,640]{3,2,0,1:T(8,128)S(1)} %get-tuple-element.42), channel_id=1, source_target_pairs={{16,0},{32,16},{48,32},{64,48},{80,64},{96,80},{112,96},{17,1},{33... | collective-permute-start | bytes 614408 | tf_op jit(solution)/shard_map/ppermute | solution.py:21
  308.9 4.5 %collective-permute-start.10 = (f32[2,5,1,640]{3,2,1,0:T(1,128)S(1)}, f32[2,5,1,640]{3,2,1,0:T(1,128)S(1)}, u32[]{:S(2)}, u32[]{:S(2)}) collective-permute-start(f32[2,5,1,640]{3,2,1,0:T(1,128)S(1)} %get-tuple-element.37), channel_id=1, source_target_pairs={{0,1},{1,2},{2,3},{3,4},{4,5},{5,6},{6,7},{7,8},{8,9},{9,10},{10,1... | collective-permute-start | bytes 76808 | tf_op jit(solution)/shard_map/ppermute | solution.py:18
  311.0 7.3 %collective-permute-start.11 = (f32[2,5,1,640]{3,2,1,0:T(1,128)S(1)}, f32[2,5,1,640]{3,2,1,0:T(1,128)S(1)}, u32[]{:S(2)}, u32[]{:S(2)}) collective-permute-start(f32[2,5,1,640]{3,2,1,0:T(1,128)S(1)} %get-tuple-element.38), channel_id=1, source_target_pairs={{1,0},{2,1},{3,2},{4,3},{5,4},{6,5},{7,6},{8,7},{9,8},{10,9},{11,1... | collective-permute-start | bytes 76808 | tf_op jit(solution)/shard_map/ppermute | solution.py:21
  324.7 3.1 copy-start.10
  345.4 1.8 copy-start.16
  346.9 1.8 copy-start.15
  359.4 8.6 %copy-start.20 = (f32[2,1,5,40,640]{4,3,2,0,1:T(8,128)S(1)}, f32[2,1,5,40,640]{4,3,2,0,1:T(8,128)}, u32[]{:S(2)}) copy-start(f32[2,1,5,40,640]{4,3,2,0,1:T(8,128)} %bitcast_subtract_fusion) | copy-start | bytes 3072004
  361.1 7.2 %copy-start.25 = (f32[1,5,40,640]{3,2,1,0:T(8,128)S(1)}, f32[1,5,40,640]{3,2,1,0:T(8,128)}, u32[]{:S(2)}) copy-start(f32[1,5,40,640]{3,2,1,0:T(8,128)} %reduce_sum.33) | copy-start | bytes 1536004
  361.2 7.2 %copy-start.26 = (f32[1,5,40,640]{3,2,1,0:T(8,128)S(1)}, f32[1,5,40,640]{3,2,1,0:T(8,128)}, u32[]{:S(2)}) copy-start(f32[1,5,40,640]{3,2,1,0:T(8,128)} %reduce_sum.35) | copy-start | bytes 1536004
  361.2 7.2 %copy-start.30 = (bf16[1,5,40,640]{3,2,1,0:T(8,128)(2,1)S(1)}, bf16[1,5,40,640]{3,2,1,0:T(8,128)(2,1)}, u32[]{:S(2)}) copy-start(bf16[1,5,40,640]{3,2,1,0:T(8,128)(2,1)} %param.12) | copy-start | bytes 768004
  361.2 8.2 %collective-permute-start.12 = (f32[2,1,40,640]{3,2,0,1:T(8,128)S(1)}, f32[2,1,40,640]{3,2,0,1:T(8,128)S(1)}, u32[]{:S(2)}, u32[]{:S(2)}) collective-permute-start(f32[2,1,40,640]{3,2,0,1:T(8,128)S(1)} %get-tuple-element.35), channel_id=1, source_target_pairs={{0,16},{16,32},{32,48},{48,64},{64,80},{80,96},{96,112},{1,17},{17... | collective-permute-start | bytes 614408 | tf_op jit(solution)/shard_map/ppermute | solution.py:18
  366.7 8.0 %collective-permute-start.13 = (f32[2,1,40,640]{3,2,0,1:T(8,128)S(1)}, f32[2,1,40,640]{3,2,0,1:T(8,128)S(1)}, u32[]{:S(2)}, u32[]{:S(2)}) collective-permute-start(f32[2,1,40,640]{3,2,0,1:T(8,128)S(1)} %get-tuple-element.36), channel_id=1, source_target_pairs={{16,0},{32,16},{48,32},{64,48},{80,64},{96,80},{112,96},{17,1},{33... | collective-permute-start | bytes 614408 | tf_op jit(solution)/shard_map/ppermute | solution.py:21
  375.1 4.8 %collective-permute-start.14 = (f32[2,5,1,640]{3,2,1,0:T(1,128)S(1)}, f32[2,5,1,640]{3,2,1,0:T(1,128)S(1)}, u32[]{:S(2)}, u32[]{:S(2)}) collective-permute-start(f32[2,5,1,640]{3,2,1,0:T(1,128)S(1)} %get-tuple-element.31), channel_id=1, source_target_pairs={{0,1},{1,2},{2,3},{3,4},{4,5},{5,6},{6,7},{7,8},{8,9},{9,10},{10,1... | collective-permute-start | bytes 76808 | tf_op jit(solution)/shard_map/ppermute | solution.py:18
  378.0 7.3 %collective-permute-start.15 = (f32[2,5,1,640]{3,2,1,0:T(1,128)S(1)}, f32[2,5,1,640]{3,2,1,0:T(1,128)S(1)}, u32[]{:S(2)}, u32[]{:S(2)}) collective-permute-start(f32[2,5,1,640]{3,2,1,0:T(1,128)S(1)} %get-tuple-element.32), channel_id=1, source_target_pairs={{1,0},{2,1},{3,2},{4,3},{5,4},{6,5},{7,6},{8,7},{9,8},{10,9},{11,1... | collective-permute-start | bytes 76808 | tf_op jit(solution)/shard_map/ppermute | solution.py:21
  392.0 2.9 copy-start.6
  392.0 2.9 copy-start.11
  (5 other events, 5.6 us)
where the time goes:
time: 403 us; the launch traced here: 398 us
  other arithmetic  129 us (32%)
  local copies, waits for them, and re-layouts  113 us (28%)
  starting transfers between devices  68 us (17%)
  matrix products  52.7 us (13%)
  waiting for transfers between devices  32.6 us (8%)
    scatter-add x3, other arithmetic, on_device(): jnp.zeros((values.shape[0], point_count), jnp.float32).at[:, targets]  87.8 us
    scatter-add x2, local copies, waits for them, and re-layouts, on_device(): jnp.zeros((values.shape[0], point_count), jnp.float32).at[:, targets]  34.6 us
    ppermute x8, starting transfers between devices, with_halo(): lax.ppermute(lax.slice_in_dim(block, block.shape[dim] - width, None, axis...  31.8 us
    ppermute x8, waiting for transfers between devices, with_halo(): lax.ppermute(lax.slice_in_dim(block, 0, width, axis=dim), axis, backward)  30.8 us
    dot_general x5, matrix products, gradients(): jnp.einsum('ai,rxiyjkz->rxayjkz', derivative, view, precision=highest)  14 us
    ppermute x8, starting transfers between devices, with_halo(): lax.ppermute(lax.slice_in_dim(block, 0, width, axis=dim), axis, backward)  14 us
    all_to_all x1, starting transfers between devices, deliver(): lax.all_to_all(send_values.reshape(trace_rows, devices, capacity), ('lat'...  11.7 us
    reshape x9, local copies, waits for them, and re-layouts, stiffness(): return (force.reshape(field.shape), grads)  11.3 us
  transfers between devices with their start and end apart: 18, of which 7 were waited for; matrix products, arithmetic and copies ran while one was open for 47% of the time, Pallas kernels for 0%

commit v1 on v0

v1 whole, which is shorter than its diff:
```python
import functools
import math

import jax
import jax.numpy as jnp
import numpy as np
from jax import lax
from jax.experimental import pallas as pl
from jax.experimental.pallas import tpu as pltpu
from jax.sharding import PartitionSpec as P

time_step = 0.05
f32 = jnp.float32
bf16 = jnp.bfloat16
points = 125
padded = 128
slots = 32
face_tiles = 18
VMEM = pl.BlockSpec(memory_space=pltpu.VMEM)
SMEM = pl.BlockSpec(memory_space=pltpu.SMEM)


def gll_tables():
    root_value = math.sqrt(3.0 / 7.0)
    gll_points = np.array([-1.0, -root_value, 0.0, root_value, 1.0])
    gll_weights = np.array([0.1, 49.0 / 90.0, 32.0 / 45.0, 49.0 / 90.0, 0.1])
    legendre = (35.0 * gll_points**4 - 30.0 * gll_points**2 + 3.0) / 8.0
    derivative = np.zeros((5, 5))
    for a in range(5):
        for b in range(5):
            if a != b:
                derivative[a, b] = legendre[a] / legendre[b] / (gll_points[a] - gll_points[b])
    derivative[0, 0] = -5.0
    derivative[4, 4] = 5.0
    return derivative, gll_weights


derivative, gll_weights = gll_tables()
transposed = derivative.T


def weight(i, j, k):
    return float(gll_weights[i] * gll_weights[j] * gll_weights[k])


def apply5(matrix, u):
    odd = (u[0] - u[4], u[1] - u[3])
    even = (u[0] + u[4], u[1] + u[3])
    out = [None] * 5
    for a in (0, 1):
        p = float(0.5 * (matrix[a, 0] - matrix[a, 4])) * odd[0]
        p = p + float(0.5 * (matrix[a, 1] - matrix[a, 3])) * odd[1]
        m = float(0.5 * (matrix[a, 0] + matrix[a, 4])) * even[0]
        m = m + float(0.5 * (matrix[a, 1] + matrix[a, 3])) * even[1]
        m = m + float(matrix[a, 2]) * u[2]
        out[a] = p + m
        out[4 - a] = p - m
    out[2] = float(matrix[2, 0]) * odd[0] + float(matrix[2, 1]) * odd[1]
    return out


directions = ((5, 1, 25), (25, 1, 5), (25, 5, 1))


def for_lines(body):
    for direction, (outer, inner, step) in enumerate(directions):

        def block(t, carry, direction=direction, outer=outer, inner=inner, step=step):
            for line in range(5):
                base = t * outer + line * inner
                body(direction, [base + step * n for n in range(5)])
            return carry

        lax.fori_loop(0, 5, block, 0)


def sublane():
    return lax.broadcasted_iota(jnp.int32, (8, 128), 0)


def lane():
    return lax.broadcasted_iota(jnp.int32, (8, 128), 1)


def row_of(tile, index):
    return jnp.broadcast_to(tile[index : index + 1, :], (8, 128))


def column_of(tile, index):
    return jnp.broadcast_to(tile[:, index : index + 1], (8, 128))


def at(i, j, k):
    return (i * 5 + j) * 5 + k


def to_tiles(plane, put, wide):
    for i in range(5):
        rows = plane(i)
        for k in range(5):
            wide[i, k] = rows[:, k * 128 : (k + 1) * 128]
        for j in range(5):
            for k in range(5):
                put(at(i, j, k), wide[i, k, pl.ds(j, 8, stride=5), :])


def from_tiles(tile, put_plane, wide):
    for i in range(5):
        for j in range(5):
            for k in range(5):
                wide[i, k, pl.ds(j, 8, stride=5), :] = tile(i, j, k)
        for k in range(5):
            put_plane(i, k, wide[i, k])


def subtract_stiffness(d, f, e, wm):
    def line(direction, index):
        g = apply5(derivative, [d[e, n] for n in index])
        r = apply5(transposed, [g[a] * wm[index[a]] for a in range(5)])
        for a in range(5):
            f[e, index[a]] = f[e, index[a]] - r[a]

    for_lines(line)


def fold(get, put):
    sub, ln = sublane(), lane()
    for i in range(5):
        v = [[get(at(i, j, k)) for k in range(5)] for j in range(5)]
        for k in range(5):
            v[0][k] = v[0][k] + jnp.where(sub == 0, 0.0, pltpu.roll(v[4][k], 1, 0))
        for j in range(5):
            v[j][0] = v[j][0] + jnp.where(ln == 0, 0.0, pltpu.roll(v[j][4], 1, 1))
        for j in range(5):
            for k in range(5):
                if (j, k) == (0, 4) or j == 0 or k == 0:
                    put(at(i, j, k), v[j][k])


def emit_faces(get, c, face_low, face_high, row_low, row_high):
    sub, ln = sublane(), lane()
    for i, face in ((0, face_low), (4, face_high)):
        last_row = jnp.zeros((8, 128), f32)
        last_column = jnp.zeros((8, 128), f32)
        for k in range(5):
            last_row = jnp.where(sub == k, row_of(get(at(i, 4, k)), 7), last_row)
        for j in range(4):
            last_column = jnp.where(ln == j, column_of(get(at(i, j, 4)), 127), last_column)
            for k in range(4):
                face[c, j * 4 + k] = get(at(i, j, k))
        face[c, 16] = last_row
        face[c, 17] = last_column
    for i in range(5):
        low = jnp.zeros((8, 128), f32)
        high = jnp.zeros((8, 128), f32)
        for k in range(5):
            low = jnp.where(sub == k, row_of(get(at(i, 0, k)), 0), low)
            high = jnp.where(sub == k, row_of(get(at(i, 4, k)), 7), high)
        row_low[c, i] = low
        row_high[c, i] = high


def complete(get, i, c, flags, from_below, from_above, from_left, from_right):
    sub, ln = sublane(), lane()
    v = [[get(at(i, j, k)) for k in range(5)] for j in range(5)]
    if i in (0, 4):
        face = from_below if i == 0 else from_above
        keep = flags[0 if i == 0 else 1] > 0
        for j in range(4):
            for k in range(4):
                v[j][k] = v[j][k] + jnp.where(keep, face[c, j * 4 + k], 0.0)
        last_row, last_column = face[c, 16], face[c, 17]
        for k in range(5):
            v[4][k] = v[4][k] + jnp.where((sub == 7) & keep, row_of(last_row, k), 0.0)
        for j in range(4):
            v[j][4] = v[j][4] + jnp.where((ln == 127) & keep, column_of(last_column, j), 0.0)
    left, right = from_left[c, i], from_right[c, i]
    for k in range(5):
        v[0][k] = v[0][k] + jnp.where((sub == 0) & (flags[2] > 0), row_of(left, k), 0.0)
        v[4][k] = v[4][k] + jnp.where((sub == 7) & (flags[3] > 0), row_of(right, k), 0.0)
    for k in range(5):
        v[4][k] = jnp.where(sub == 7, v[4][k], pltpu.roll(v[0][k], 7, 0))
    for j in range(5):
        v[j][4] = jnp.where(ln == 127, v[j][4], pltpu.roll(v[j][0], 127, 1))
    return v


def pack_kernel(traces, owner, point, out):
    devices = out.shape[0] // 2
    receivers = owner.shape[1]
    p = point[...]
    hi = p >> 7
    lo = p & 127

    def divide(x, by):
        return jnp.floor((x.astype(f32) + 0.5) * (1.0 / by)).astype(jnp.int32)

    t = divide(hi, 5)
    k = hi - 5 * t
    i = divide(t, 40)
    row = t - 40 * i
    ey = divide(row, 5)
    j = row - 5 * ey
    place = ((((i * 5 + j) * 5 + k) * 8 + ey) * 128 + lo).astype(f32)
    rows = [traces[0, 0:1, :], traces[1, 0:1, :], place, traces[0, 1:2, :]]
    rows += [traces[1, 1:2, :], traces[0, 2:3, :], traces[1, 2:3, :], jnp.zeros((1, receivers), f32)]
    owned = lax.broadcasted_iota(jnp.int32, (devices, receivers), 0) == owner[...]
    owned = jnp.where(owned, 1.0, 0.0)
    before = lax.broadcasted_iota(jnp.int32, (128, 128), 0) < lax.broadcasted_iota(jnp.int32, (128, 128), 1)
    before = jnp.where(before, 1.0, 0.0).astype(bf16)
    carry = jnp.zeros((devices, 1), f32)
    ranks = []
    for chunk in range(receivers // 128):
        part = owned[:, chunk * 128 : (chunk + 1) * 128]
        earlier = jnp.dot(part.astype(bf16), before, preferred_element_type=f32) + carry
        ranks.append(jnp.sum(part * earlier, axis=0, keepdims=True))
        carry = carry + jnp.sum(part, axis=1, keepdims=True)
    rank = jnp.concatenate(ranks, axis=1).astype(jnp.int32)
    chosen = lax.broadcasted_iota(jnp.int32, (slots, receivers), 0) == rank
    owned = owned.astype(bf16)
    total = jnp.zeros((devices, 256), f32)
    left = rows
    for _ in range(3):
        pieces = [v.astype(bf16) for v in left]
        left = [v - q.astype(f32) for v, q in zip(left, pieces)]
        table = jnp.concatenate([jnp.where(chosen, q.astype(f32), 0.0) for q in pieces], axis=0)
        total = total + lax.dot_general(
            owned, table.astype(bf16), (((1,), (1,)), ((), ())), preferred_element_type=f32
        )
    out[pl.ds(0, devices, stride=2), :] = total[:, :128]
    out[pl.ds(1, devices, stride=2), :] = total[:, 128:]


def scatter(places, values, hi_rows, lo_rows, piece_rows, left_side, right_side, store):
    place = places.astype(jnp.int32)
    hi_rows[...] = place >> 7
    lo_rows[...] = place & 127
    count = len(values)
    for c, v in enumerate(values):
        upper = v.astype(bf16).astype(f32)
        piece_rows[2 * c] = upper
        piece_rows[2 * c + 1] = v - upper
    index = lax.broadcasted_iota(jnp.int32, (128, 128), 0)

    def fill(r, carry):
        where = pl.ds(pl.multiple_of(r * 128, 128), 128)
        hi = hi_rows[pl.ds(r, 1), :]
        lo = lo_rows[pl.ds(r, 1), :]
        for m in range(8):
            left_side[m * 128 : (m + 1) * 128, where] = jnp.where(index + m * 128 == hi, 1.0, 0.0).astype(bf16)
        same = index == lo
        for n in range(2 * count):
            right_side[n * 128 : (n + 1) * 128, where] = jnp.where(same, piece_rows[n, pl.ds(r, 1), :], 0.0).astype(bf16)
        return carry

    lax.fori_loop(0, slots, fill, 0)

    def tile(m, carry):
        rows = pl.ds(pl.multiple_of(m * 256, 256), 256)
        for c in range(count):
            both = lax.dot_general(
                left_side[rows, :],
                right_side[c * 256 : (c + 1) * 256, :],
                (((1,), (1,)), ((), ())),
                preferred_element_type=f32,
            )
            store(m, c, both[:, :128] + both[:, 128:])
        return carry

    lax.fori_loop(0, 4, tile, 0)


def start_kernel(d0, v0, modulus, density, d_out, v_out, wm, mass, kd, wide):
    def put_event(e, carry):
        for source, target in ((d0, d_out), (v0, v_out)):

            def put_field(n, value, target=target):
                target[e, n] = value

            to_tiles(lambda i, source=source: source[e, i], put_field, wide)
        return carry

    lax.fori_loop(0, 2, put_event, 0)
    for source, target in ((modulus, wm), (density, mass)):

        def put_weighted(n, value, target=target):
            target[n] = value * weight(n // 25, n // 5 % 5, n % 5)

        to_tiles(lambda i, source=source: source[i].astype(f32), put_weighted, wide)

    def put(n, value):
        mass[n] = value

    fold(lambda n: mass[n], put)

    def clear(n, carry):
        kd[0, n] = jnp.zeros((8, 128), f32)
        kd[1, n] = jnp.zeros((8, 128), f32)
        return carry

    lax.fori_loop(0, points, clear, 0)

    def event(e, carry):
        subtract_stiffness(d_out, kd, e, wm)
        return carry

    lax.fori_loop(0, 2, event, 0)


def first_force_kernel(got, kd, mass, f, face_low, face_high, row_low, row_high, sums, hi_rows, lo_rows, piece_rows, left_side, right_side):
    devices = got.shape[0] // 2
    first = got[pl.ds(0, devices, stride=2), :].T

    def store(m, c, value):
        sums[c, pl.ds(m * 32, 32)] = value.reshape(32, 8, 128)

    scatter(first[64:96], [first[0:32], first[32:64]], hi_rows, lo_rows, piece_rows, left_side, right_side, store)

    def event(e, carry):
        def get(n):
            return kd[e, n] + sums[e, n]

        def copy(n, c):
            f[e, n] = get(n)
            return c

        lax.fori_loop(0, points, copy, 0)

        def put(n, value):
            f[e, n] = value

        fold(lambda n: f[e, n], put)
        emit_faces(lambda n: f[e, n], e, face_low, face_high, row_low, row_high)
        return carry

    lax.fori_loop(0, 2, event, 0)
    emit_faces(lambda n: mass[n], 2, face_low, face_high, row_low, row_high)


def later_sources_kernel(got, s1, s2, hi_rows, lo_rows, piece_rows, left_side, right_side):
    devices = got.shape[0] // 2
    first = got[pl.ds(0, devices, stride=2), :].T
    second = got[pl.ds(1, devices, stride=2), :].T

    def store(m, c, value):
        target = s1 if c < 2 else s2
        target[c % 2, pl.ds(m * 32, 32)] = value.reshape(32, 8, 128)

    values = [first[96:128], second[0:32], second[32:64], second[64:96]]
    scatter(first[64:96], values, hi_rows, lo_rows, piece_rows, left_side, right_side, store)


def rows_kernel(flags, from_below, from_above, row_low, row_high, low_out, high_out):
    sub, ln = sublane(), lane()
    for c in range(row_low.shape[0]):
        for i in range(5):
            low, high = row_low[c, i], row_high[c, i]
            if i in (0, 4):
                face = from_below if i == 0 else from_above
                keep = flags[0 if i == 0 else 1] > 0
                extra = jnp.zeros((8, 128), f32)
                for k in range(4):
                    extra = jnp.where(sub == k, row_of(face[c, k], 0), extra)
                corner = jnp.broadcast_to(face[c, 17][0:1, 0:1], (8, 128))
                extra = jnp.where((sub == 4) & (ln == 127), corner, extra)
                low = low + jnp.where(keep, extra, 0.0)
                high = high + jnp.where(keep, face[c, 16], 0.0)
            low_out[c, i] = low
            high_out[c, i] = high


def step_kernel(first, *refs):
    if first:
        flags, f, below, above, left, right, d, q, source, wm, mass = refs[:11]
        d_out, q_out, inverse, f_out, face_low, face_high, row_low, row_high = refs[11:]
        for i in range(5):
            v = complete(lambda n: mass[n], i, 2, flags, below, above, left, right)
            for j in range(5):
                for k in range(5):
                    inverse[at(i, j, k)] = 1.0 / v[j][k]
    else:
        flags, f, below, above, left, right, d, q, source, wm, inverse = refs[:11]
        d_out, q_out, f_out, face_low, face_high, row_low, row_high = refs[11:]
    share = 0.5 * time_step if first else time_step

    def event(e, carry):
        for i in range(5):
            v = complete(lambda n: f[e, n], i, e, flags, below, above, left, right)
            for j in range(5):
                for k in range(5):
                    n = at(i, j, k)
                    q_new = q[e, n] + share * (v[j][k] * inverse[n])
                    q_out[e, n] = q_new
                    d_out[e, n] = d[e, n] + time_step * q_new

        def copy(n, c):
            f_out[e, n] = source[e, n]
            return c

        lax.fori_loop(0, points, copy, 0)
        subtract_stiffness(d_out, f_out, e, wm)

        def put(n, value):
            f_out[e, n] = value

        fold(lambda n: f_out[e, n], put)
        emit_faces(lambda n: f_out[e, n], e, face_low, face_high, row_low, row_high)
        return carry

    lax.fori_loop(0, 2, event, 0)


def last_kernel(flags, f, below, above, left, right, q, inverse, velocity, wide):
    def event(e, carry):
        for i in range(5):
            v = complete(lambda n: f[e, n], i, e, flags, below, above, left, right)
            for j in range(5):
                for k in range(5):
                    n = at(i, j, k)
                    wide[i, k, pl.ds(j, 8, stride=5), :] = q[e, n] + 0.5 * time_step * (v[j][k] * inverse[n])
            for k in range(5):
                velocity[e, i, :, k * 128 : (k + 1) * 128] = wide[i, k]
        return carry

    lax.fori_loop(0, 2, event, 0)


def correlate(d, forward, total, wide, tiles):
    def event(e, carry):
        def put(n, value):
            tiles[n] = value

        to_tiles(lambda i: forward[e, i].astype(f32), put, wide)

        def line(direction, index):
            g = apply5(derivative, [d[e, n] for n in index])
            h = apply5(derivative, [tiles[n] for n in index])
            for a in range(5):
                total[index[a]] = total[index[a]] + g[a] * h[a]

        for_lines(line)
        return carry

    lax.fori_loop(0, 2, event, 0)


def first_kernel_term(d, forward, total, wide, tiles):
    def clear(n, carry):
        total[n] = jnp.zeros((8, 128), f32)
        return carry

    lax.fori_loop(0, points, clear, 0)
    correlate(d, forward, total, wide, tiles)


def last_kernel_term(d, forward, before, wm, out, total, wide, tiles):
    def copy(n, carry):
        total[n] = before[n]
        return carry

    lax.fori_loop(0, points, copy, 0)
    correlate(d, forward, total, wide, tiles)

    def tile(i, j, k):
        return total[at(i, j, k)] * wm[at(i, j, k)] * (-time_step / weight(i, j, k))

    def put_plane(i, k, rows):
        out[i, :, k * 128 : (k + 1) * 128] = rows

    from_tiles(tile, put_plane, wide)


def call(kernel, name, out_shapes, args, scratch=(), specs=None, flops=10**6, moved=4 * 10**6):
    return pl.pallas_call(
        kernel,
        name=name,
        out_shape=[jax.ShapeDtypeStruct(s, f32) for s in out_shapes],
        in_specs=specs or [VMEM] * len(args),
        out_specs=[VMEM] * len(out_shapes),
        scratch_shapes=list(scratch),
        compiler_params=pltpu.CompilerParams(vmem_limit_bytes=56 * 2**20),
        cost_estimate=pl.CostEstimate(flops=flops, bytes_accessed=moved, transcendentals=0),
    )(*args)


def swap(low, high, axis):
    count = lax.axis_size(axis)
    up = [(n, (n + 1) % count) for n in range(count)]
    down = [(b, a) for a, b in up]
    return lax.ppermute(high, axis, up), lax.ppermute(low, axis, down)


def on_device(d0, v0, modulus, density, forward, traces, owner, point):
    lat, lon = lax.axis_index("lat"), lax.axis_index("lon")
    lat_count, lon_count = lax.axis_size("lat"), lax.axis_size("lon")
    devices = lat_count * lon_count
    flags = jnp.stack([lat > 0, lat < lat_count - 1, lon > 0, lon < lon_count - 1]).astype(jnp.int32)
    field = (2, points, 8, 128)
    one = (points, 8, 128)
    wide_field = (2, padded, 8, 128)
    native = d0.shape
    d0, v0 = d0.reshape(2, 5, 40, 640), v0.reshape(2, 5, 40, 640)
    kernel_shape = modulus.shape
    modulus, density = modulus.reshape(5, 40, 640), density.reshape(5, 40, 640)
    forward = forward.reshape(2, 2, 5, 40, 640)
    receivers = owner.shape[0]

    def faces(channels):
        return [(channels, face_tiles, 8, 128)] * 2 + [(channels, 5, 8, 128)] * 2

    (packed,) = call(
        pack_kernel, "pack", [(2 * devices, 128)], (traces, owner.reshape(1, receivers), point.reshape(1, receivers))
    )
    got = lax.all_to_all(packed.reshape(devices, 2, 128), ("lat", "lon"), 0, 0, tiled=True)
    got = got.reshape(2 * devices, 128)
    wide = pltpu.VMEM((5, 5, 40, 128), f32)
    tiles = pltpu.VMEM(one, f32)
    d, q, wm, mass, kd = call(
        start_kernel, "start", [field, field, one, one, field], (d0, v0, modulus, density), [wide], flops=10**8
    )

    def scatter_scratch(count):
        return [
            pltpu.VMEM((slots, devices), jnp.int32),
            pltpu.VMEM((slots, devices), jnp.int32),
            pltpu.VMEM((2 * count, slots, devices), f32),
            pltpu.VMEM((1024, slots * devices), bf16),
            pltpu.VMEM((256 * count, slots * devices), bf16),
        ]

    f, *edges = call(
        first_force_kernel,
        "first_force",
        [field] + faces(3),
        (got, kd, mass),
        [pltpu.VMEM(wide_field, f32)] + scatter_scratch(2),
        flops=4 * 10**9,
    )
    s1, s2 = call(
        later_sources_kernel, "later_sources", [wide_field, wide_field], (got,), scatter_scratch(4), flops=8 * 10**9
    )

    def exchange(edges):
        face_low, face_high, row_low, row_high = edges
        below, above = swap(face_low, face_high, "lat")
        low, high = call(
            rows_kernel,
            "rows",
            [row_low.shape] * 2,
            (flags, below, above, row_low, row_high),
            specs=[SMEM] + [VMEM] * 4,
            moved=4 * 10**5,
        )
        left, right = swap(low, high, "lon")
        return below, above, left, right

    specs = [SMEM] + [VMEM] * 10
    received = exchange(edges)
    d, q, inverse, f, *edges = call(
        functools.partial(step_kernel, True),
        "first_step",
        [field, field, one, field] + faces(2),
        (flags, f, *received, d, q, s1, wm, mass),
        specs=specs,
        flops=10**8,
    )
    (term,) = call(first_kernel_term, "first_term", [one], (d, forward[0]), [wide, tiles], flops=10**8)
    received = exchange(edges)
    d, q, f, *edges = call(
        functools.partial(step_kernel, False),
        "second_step",
        [field, field, field] + faces(2),
        (flags, f, *received, d, q, s2, wm, inverse),
        specs=specs,
        flops=10**8,
    )
    (kernel,) = call(
        last_kernel_term, "last_term", [(5, 40, 640)], (d, forward[1], term, wm), [tiles, wide, tiles], flops=10**8
    )
    received = exchange(edges)
    (velocity,) = call(
        last_kernel, "last", [(2, 5, 40, 640)], (flags, f, *received, q, inverse), [wide], [SMEM] + [VMEM] * 7
    )
    return velocity.reshape(native), kernel.reshape(kernel_shape)


def solution(mesh):
    placed = (
        P(None, "lat", None, "lon", None),
        P(None, "lat", None, "lon", None),
        P("lat", None, "lon", None),
        P("lat", None, "lon", None),
        P(None, None, "lat", None, "lon", None),
        P(None, None, ("lat", "lon")),
        P(("lat", "lon")),
        P(("lat", "lon")),
    )
    return jax.shard_map(
        on_device,
        mesh=mesh,
        in_specs=placed,
        out_specs=(P(None, "lat", None, "lon", None), P("lat", None, "lon", None)),
        check_vma=False,
    )
```

time: 403 us -> 141 us (0.35)
  the two profiles are of different devices: /device:TPU:25 before, /device:TPU:0 now
where the time goes in v1:
time: 141 us
  Pallas kernels  73 us (52%)
  starting transfers between devices  39.7 us (28%)
  waiting for transfers between devices  19.8 us (14%)
  local copies, waits for them, and re-layouts  7.02 us (5%)
    pallas_call x12, Pallas kernels, call(): pl.pallas_call(kernel, name=name, out_shape=[jax.ShapeDtypeStruct(s, f32)...  73 us
    ppermute x12, starting transfers between devices, swap(): return (lax.ppermute(high, axis, up), lax.ppermute(low, axis, down))  28.5 us
    ppermute x12, waiting for transfers between devices, swap(): return (lax.ppermute(high, axis, up), lax.ppermute(low, axis, down))  16.7 us
    all_to_all x1, starting transfers between devices, on_device(): lax.all_to_all(packed.reshape(devices, 2, 128), ('lat', 'lon'), 0, 0, til...  11.1 us
    unnamed x29, local copies, waits for them, and re-layouts  5.97 us
    all_to_all x1, waiting for transfers between devices, on_device(): lax.all_to_all(packed.reshape(devices, 2, 128), ('lat', 'lon'), 0, 0, til...  3.11 us
  transfers between devices with their start and end apart: 13, of which 8 were waited for; matrix products, arithmetic and copies ran while one was open for 1% of the time, Pallas kernels for 23%

profile of v1, /device:TPU:0, one launch (start us, length us, event | category | flops | bytes accessed | tf_op | source)
XLA Modules:
  0.0 140.8 jit_solution(10717855123988637795)
XLA Ops:
  0.6 1.4 copy.10.traces
  2.0 2.2 %pack.1 = f32[256,128]{1,0:T(8,128)} custom-call(f32[2,3,1024]{2,1,0:T(4,128)} %copy.10.traces, s32[1,1024]{1,0:T(1,128)} %bitcast.31, s32[1,1024]{1,0:T(1,128)} %bitcast.32), custom_call_target="tpu_custom_call" | custom-call | flops 1000000 | bytes 4000000 | tf_op jit(solution)/shard_map/pack/pallas_call | solution.py:474
  4.2 11.1 %all-to-all-start = ((f32[128,2,128]{2,1,0:T(2,128)}), f32[128,2,128]{2,1,0:T(2,128)S(1)}, u32[]{:S(2)}, u32[]{:S(2)}) async-start(f32[128,2,128]{2,1,0:T(2,128)} %bitcast.25), calls=%async_computation | async-start | bytes 262144 | tf_op jit(solution)/shard_map/all_to_all | solution.py:514
  15.3 6.3 %start.1 = (f32[2,125,8,128]{3,2,1,0:T(8,128)}, f32[2,125,8,128]{3,2,1,0:T(8,128)}, f32[125,8,128]{2,1,0:T(8,128)}, f32[125,8,128]{2,1,0:T(8,128)}, f32[2,125,8,128]{3,2,1,0:T(8,128)}) custom-call(f32[2,5,40,640]{3,2,1,0:T(8,128)} %bitcast.21, f32[2,5,40,640]{3,2,1,0:T(8,128)} %bitcast.22, bf16[5,40,640]{2,1,0:T(8,128)(2,1)} %bitcast.27, ...), custom_call_target="tpu_custom_call" | custom-call | flops 100000000 | bytes 4000000 | tf_op jit(solution)/shard_map/start/pallas_call | solution.py:474
  21.6 3.1 %all-to-all-done = f32[128,2,128]{2,1,0:T(2,128)S(1)} async-done(((f32[128,2,128]{2,1,0:T(2,128)}), f32[128,2,128]{2,1,0:T(2,128)S(1)}, u32[]{:S(2)}, u32[]{:S(2)}) %all-to-all-start) | async-done | bytes 131104 | tf_op jit(solution)/shard_map/all_to_all | solution.py:514
  24.8 0.7 copy-done.7
  25.4 13.7 %first_force.1 = (f32[2,125,8,128]{3,2,1,0:T(8,128)}, f32[3,18,8,128]{3,2,1,0:T(8,128)}, f32[3,18,8,128]{3,2,1,0:T(8,128)}, f32[3,5,8,128]{3,2,1,0:T(8,128)}, f32[3,5,8,128]{3,2,1,0:T(8,128)}) custom-call(f32[256,128]{1,0:T(8,128)} %bitcast.29, f32[2,125,8,128]{3,2,1,0:T(8,128)} %get-tuple-element.35.kd, f32[125,8,128]{2,1,0:T(8,128)} %get-tuple-element.36.mass.refs_10_), custom_call_target="tpu_custom_call" | custom-call | flops 4000000000 | bytes 4000000 | tf_op jit(solution)/shard_map/first_force/pallas_call | solution.py:474
  39.1 1.2 collective-permute-start
  40.3 4.4 %collective-permute-start.1 = (f32[3,18,8,128]{3,2,1,0:T(8,128)}, f32[3,18,8,128]{3,2,1,0:T(8,128)S(1)}, u32[]{:S(2)}, u32[]{:S(2)}) collective-permute-start(f32[3,18,8,128]{3,2,1,0:T(8,128)} %get-tuple-element.39), channel_id=1, source_target_pairs={{16,0},{32,16},{48,32},{64,48},{80,64},{96,80},{112,96},{0,112},{1... | collective-permute-start | bytes 663560 | tf_op jit(solution)/shard_map/ppermute | solution.py:490
  44.7 0.6 add_convert_fusion.flags.refs_0_
  45.3 5.9 %collective-permute-done.from_below.refs_2_ = f32[3,18,8,128]{3,2,1,0:T(8,128)S(1)} collective-permute-done((f32[3,18,8,128]{3,2,1,0:T(8,128)}, f32[3,18,8,128]{3,2,1,0:T(8,128)S(1)}, u32[]{:S(2)}, u32[]{:S(2)}) %collective-permute-start) | collective-permute-done | bytes 221216 | tf_op jit(solution)/shard_map/ppermute | solution.py:490
  51.2 1.6 %collective-permute-done.1.from_above.refs_3_ = f32[3,18,8,128]{3,2,1,0:T(8,128)S(1)} collective-permute-done((f32[3,18,8,128]{3,2,1,0:T(8,128)}, f32[3,18,8,128]{3,2,1,0:T(8,128)S(1)}, u32[]{:S(2)}, u32[]{:S(2)}) %collective-permute-start.1) | collective-permute-done | bytes 221216 | tf_op jit(solution)/shard_map/ppermute | solution.py:490
  52.8 0.7 copy-done.2
  53.5 1.8 %rows.3 = (f32[3,5,8,128]{3,2,1,0:T(8,128)}, f32[3,5,8,128]{3,2,1,0:T(8,128)}) custom-call(s32[4]{0:T(128)} %add_convert_fusion.flags.refs_0_, f32[3,18,8,128]{3,2,1,0:T(8,128)} %copy-done.1, f32[3,18,8,128]{3,2,1,0:T(8,128)} %copy-done.2, f32[3,5,8,128]{3,2,1,0:T(8,128)} %get-tuple-element.40.row_low, f32[3,5,8,128]{3,2,1,0:T(8,128)} %get-tuple-element.41.row_high), custom_call_target="tpu_custom_call" | custom-call | flops 1000000 | bytes 400000 | tf_op jit(solution)/shard_map/rows/pallas_call | solution.py:474
  55.3 3.9 %collective-permute-start.3 = (f32[3,5,8,128]{3,2,1,0:T(8,128)}, f32[3,5,8,128]{3,2,1,0:T(8,128)S(1)}, u32[]{:S(2)}, u32[]{:S(2)}) collective-permute-start(f32[3,5,8,128]{3,2,1,0:T(8,128)} %get-tuple-element.43), channel_id=1, source_target_pairs={{1,0},{2,1},{3,2},{4,3},{5,4},{6,5},{7,6},{8,7},{9,8},{10,9},{11,1... | collective-permute-start | bytes 184328 | tf_op jit(solution)/shard_map/ppermute | solution.py:490
  59.1 16.4 %later_sources.1 = (f32[2,128,8,128]{3,2,1,0:T(8,128)}, f32[2,128,8,128]{3,2,1,0:T(8,128)}) custom-call(f32[256,128]{1,0:T(8,128)} %bitcast.30), custom_call_target="tpu_custom_call" | custom-call | flops 8000000000 | bytes 4000000 | tf_op jit(solution)/shard_map/later_sources/pallas_call | solution.py:474
  75.5 0.6 copy-done.8
  76.1 0.0 copy-done.9
  76.1 8.5 %first_step.1 = (f32[2,125,8,128]{3,2,1,0:T(8,128)}, f32[2,125,8,128]{3,2,1,0:T(8,128)}, f32[125,8,128]{2,1,0:T(8,128)}, f32[2,125,8,128]{3,2,1,0:T(8,128)}, f32...) custom-call(s32[4]{0:T(128)} %add_convert_fusion.flags.refs_0_, ...), custom_call_target="tpu_custom_call" | custom-call | flops 100000000 | bytes 4000000 | tf_op jit(solution)/shard_map/first_step/pallas_call | solution.py:474
  84.6 1.7 %collective-permute-start.4 = (f32[2,18,8,128]{3,2,1,0:T(8,128)}, f32[2,18,8,128]{3,2,1,0:T(8,128)S(1)}, u32[]{:S(2)}, u32[]{:S(2)}) collective-permute-start(f32[2,18,8,128]{3,2,1,0:T(8,128)} %get-tuple-element.49), channel_id=1, source_target_pairs={{0,16},{16,32},{32,48},{48,64},{64,80},{80,96},{96,112},{112,0},{1... | collective-permute-start | bytes 442376 | tf_op jit(solution)/shard_map/ppermute | solution.py:490
  86.3 3.9 %collective-permute-start.5 = (f32[2,18,8,128]{3,2,1,0:T(8,128)}, f32[2,18,8,128]{3,2,1,0:T(8,128)S(1)}, u32[]{:S(2)}, u32[]{:S(2)}) collective-permute-start(f32[2,18,8,128]{3,2,1,0:T(8,128)} %get-tuple-element.50), channel_id=1, source_target_pairs={{16,0},{32,16},{48,32},{64,48},{80,64},{96,80},{112,96},{0,112},{1... | collective-permute-start | bytes 442376 | tf_op jit(solution)/shard_map/ppermute | solution.py:490
  90.3 3.3 %collective-permute-done.4.from_below.refs_2_ = f32[2,18,8,128]{3,2,1,0:T(8,128)S(1)} collective-permute-done((f32[2,18,8,128]{3,2,1,0:T(8,128)}, f32[2,18,8,128]{3,2,1,0:T(8,128)S(1)}, u32[]{:S(2)}, u32[]{:S(2)}) %collective-permute-start.4) | collective-permute-done | bytes 147488 | tf_op jit(solution)/shard_map/ppermute | solution.py:490
  93.6 0.0 collective-permute-done.5.from_above.refs_3_
  93.6 0.7 copy-done.5
  94.3 0.0 copy-done.6
  94.3 1.7 %rows.4 = (f32[2,5,8,128]{3,2,1,0:T(8,128)}, f32[2,5,8,128]{3,2,1,0:T(8,128)}) custom-call(s32[4]{0:T(128)} %add_convert_fusion.flags.refs_0_, f32[2,18,8,128]{3,2,1,0:T(8,128)} %copy-done.5, f32[2,18,8,128]{3,2,1,0:T(8,128)} %copy-done.6, f32[2,5,8,128]{3,2,1,0:T(8,128)} %get-tuple-element.51.row_low, f32[2,5,8,128]{3,2,1,0:T(8,128)} %get-tuple-element.52.row_high), custom_call_target="tpu_custom_call" | custom-call | flops 1000000 | bytes 400000 | tf_op jit(solution)/shard_map/rows/pallas_call | solution.py:474
  96.0 0.0 collective-permute-start.6
  96.0 3.9 %collective-permute-start.7 = (f32[2,5,8,128]{3,2,1,0:T(8,128)}, f32[2,5,8,128]{3,2,1,0:T(8,128)S(1)}, u32[]{:S(2)}, u32[]{:S(2)}) collective-permute-start(f32[2,5,8,128]{3,2,1,0:T(8,128)} %get-tuple-element.54), channel_id=1, source_target_pairs={{1,0},{2,1},{3,2},{4,3},{5,4},{6,5},{7,6},{8,7},{9,8},{10,9},{11,1... | collective-permute-start | bytes 122888 | tf_op jit(solution)/shard_map/ppermute | solution.py:490
  99.8 1.9 %collective-permute-done.6.refs_4_ = f32[2,5,8,128]{3,2,1,0:T(8,128)S(1)} collective-permute-done((f32[2,5,8,128]{3,2,1,0:T(8,128)}, f32[2,5,8,128]{3,2,1,0:T(8,128)S(1)}, u32[]{:S(2)}, u32[]{:S(2)}) %collective-permute-start.6) | collective-permute-done | bytes 40992 | tf_op jit(solution)/shard_map/ppermute | solution.py:490
  101.7 0.1 collective-permute-done.7.refs_5_
  101.8 0.5 copy-done.12
  102.3 0.1 copy-done.13
  102.4 8.3 %second_step.1 = (f32[2,125,8,128]{3,2,1,0:T(8,128)}, f32[2,125,8,128]{3,2,1,0:T(8,128)}, f32[2,125,8,128]{3,2,1,0:T(8,128)}, f32[2,18,8,128]{3,2,1,0:T(8,128)},...) custom-call(s32[4]{0:T(128)} %add_convert_fusion.flags.refs_0_, ...), custom_call_target="tpu_custom_call" | custom-call | flops 100000000 | bytes 4000000 | tf_op jit(solution)/shard_map/second_step/pallas_call | solution.py:474
  110.7 2.7 %collective-permute-start.8 = (f32[2,18,8,128]{3,2,1,0:T(8,128)}, f32[2,18,8,128]{3,2,1,0:T(8,128)S(1)}, u32[]{:S(2)}, u32[]{:S(2)}) collective-permute-start(f32[2,18,8,128]{3,2,1,0:T(8,128)} %get-tuple-element.60), channel_id=1, source_target_pairs={{0,16},{16,32},{32,48},{48,64},{64,80},{80,96},{96,112},{112,0},{1... | collective-permute-start | bytes 442376 | tf_op jit(solution)/shard_map/ppermute | solution.py:490
  113.4 2.9 %collective-permute-start.9 = (f32[2,18,8,128]{3,2,1,0:T(8,128)}, f32[2,18,8,128]{3,2,1,0:T(8,128)S(1)}, u32[]{:S(2)}, u32[]{:S(2)}) collective-permute-start(f32[2,18,8,128]{3,2,1,0:T(8,128)} %get-tuple-element.61), channel_id=1, source_target_pairs={{16,0},{32,16},{48,32},{64,48},{80,64},{96,80},{112,96},{0,112},{1... | collective-permute-start | bytes 442376 | tf_op jit(solution)/shard_map/ppermute | solution.py:490
  116.4 3.6 %collective-permute-done.8.from_below.below = f32[2,18,8,128]{3,2,1,0:T(8,128)S(1)} collective-permute-done((f32[2,18,8,128]{3,2,1,0:T(8,128)}, f32[2,18,8,128]{3,2,1,0:T(8,128)S(1)}, u32[]{:S(2)}, u32[]{:S(2)}) %collective-permute-start.8) | collective-permute-done | bytes 147488 | tf_op jit(solution)/shard_map/ppermute | solution.py:490
  119.9 0.3 collective-permute-done.9.from_above.above
  120.3 0.3 copy-done.3
  120.6 0.4 copy-done.4
  120.9 1.7 %rows.5 = (f32[2,5,8,128]{3,2,1,0:T(8,128)}, f32[2,5,8,128]{3,2,1,0:T(8,128)}) custom-call(s32[4]{0:T(128)} %add_convert_fusion.flags.refs_0_, f32[2,18,8,128]{3,2,1,0:T(8,128)} %copy-done.3, f32[2,18,8,128]{3,2,1,0:T(8,128)} %copy-done.4, f32[2,5,8,128]{3,2,1,0:T(8,128)} %get-tuple-element.62.row_low, f32[2,5,8,128]{3,2,1,0:T(8,128)} %get-tuple-element.63.row_high), custom_call_target="tpu_custom_call" | custom-call | flops 1000000 | bytes 400000 | tf_op jit(solution)/shard_map/rows/pallas_call | solution.py:474
  122.6 0.0 collective-permute-start.10
  122.6 3.9 %collective-permute-start.11 = (f32[2,5,8,128]{3,2,1,0:T(8,128)}, f32[2,5,8,128]{3,2,1,0:T(8,128)S(1)}, u32[]{:S(2)}, u32[]{:S(2)}) collective-permute-start(f32[2,5,8,128]{3,2,1,0:T(8,128)} %get-tuple-element.65), channel_id=1, source_target_pairs={{1,0},{2,1},{3,2},{4,3},{5,4},{6,5},{7,6},{8,7},{9,8},{10,9},{11,1... | collective-permute-start | bytes 122888 | tf_op jit(solution)/shard_map/ppermute | solution.py:490
  126.5 1.1 slice_bitcast_fusion
  127.5 4.5 %first_term.1.before = f32[125,8,128]{2,1,0:T(8,128)} custom-call(f32[2,125,8,128]{3,2,1,0:T(8,128)} %get-tuple-element.55.refs_6_.d, bf16[2,5,40,640]{3,2,1,0:T(8,128)(2,1)} %get-tuple-element.70.forward), custom_call_target="tpu_custom_call" | custom-call | flops 100000000 | bytes 4000000 | tf_op jit(solution)/shard_map/first_term/pallas_call | solution.py:474
  132.0 4.9 %last_term.1 = f32[5,40,640]{2,1,0:T(8,128)} custom-call(f32[2,125,8,128]{3,2,1,0:T(8,128)} %get-tuple-element.67.d, bf16[2,5,40,640]{3,2,1,0:T(8,128)(2,1)} %get-tuple-element.71.forward, f32[125,8,128]{2,1,0:T(8,128)} %first_term.1.before, f32[125,8,128]{2,1,0:T(8,128)} %get-tuple-element.47.refs_9_.wm), custom_call_target="tpu_custom_call" | custom-call | flops 100000000 | bytes 4000000 | tf_op jit(solution)/shard_map/last_term/pallas_call | solution.py:474
  136.9 0.6 copy-done.10
  137.5 0.0 copy-done.11
  137.5 3.2 %last.1 = f32[2,5,40,640]{3,2,1,0:T(8,128)} custom-call(s32[4]{0:T(128)} %add_convert_fusion.flags.refs_0_, f32[2,125,8,128]{3,2,1,0:T(8,128)} %get-tuple-element.59.f, f32[2,18,8,128]{3,2,1,0:T(8,128)} %copy-done.3, f32[2,18,8,128]{3,2,1,0:T(8,128)} %copy-done.4, f32[2,5,8,128]{3,2,1,0:T(8,128)} %copy-done.10, f32[2,5,8,128]{3,2,1,0:T(8,128)} %copy-done.11, ...), custom_call_target="tpu_custom_call" | custom-call | flops 1000000 | bytes 4000000 | tf_op jit(solution)/shard_map/last/pallas_call | solution.py:474
  (21 shorter events, 0.0 us)
Async XLA Ops:
  4.2 20.6 %all-to-all-start = ((f32[128,2,128]{2,1,0:T(2,128)}), f32[128,2,128]{2,1,0:T(2,128)S(1)}, u32[]{:S(2)}, u32[]{:S(2)}) async-start(f32[128,2,128]{2,1,0:T(2,128)} %bitcast.25), calls=%async_computation | async-start | bytes 262144 | tf_op jit(solution)/shard_map/all_to_all | solution.py:514
  24.8 0.7 copy-start.7
  39.1 12.1 %collective-permute-start = (f32[3,18,8,128]{3,2,1,0:T(8,128)}, f32[3,18,8,128]{3,2,1,0:T(8,128)S(1)}, u32[]{:S(2)}, u32[]{:S(2)}) collective-permute-start(f32[3,18,8,128]{3,2,1,0:T(8,128)} %get-tuple-element.38), channel_id=1, source_target_pairs={{0,16},{16,32},{32,48},{48,64},{64,80},{80,96},{96,112},{112,0},{1... | collective-permute-start | bytes 663560 | tf_op jit(solution)/shard_map/ppermute | solution.py:490
  40.3 12.5 %collective-permute-start.1 = (f32[3,18,8,128]{3,2,1,0:T(8,128)}, f32[3,18,8,128]{3,2,1,0:T(8,128)S(1)}, u32[]{:S(2)}, u32[]{:S(2)}) collective-permute-start(f32[3,18,8,128]{3,2,1,0:T(8,128)} %get-tuple-element.39), channel_id=1, source_target_pairs={{16,0},{32,16},{48,32},{64,48},{80,64},{96,80},{112,96},{0,112},{1... | collective-permute-start | bytes 663560 | tf_op jit(solution)/shard_map/ppermute | solution.py:490
  51.2 1.6 %copy-start.1 = (f32[3,18,8,128]{3,2,1,0:T(8,128)}, f32[3,18,8,128]{3,2,1,0:T(8,128)S(1)}, u32[]{:S(2)}) copy-start(f32[3,18,8,128]{3,2,1,0:T(8,128)S(1)} %collective-permute-done.from_below.refs_2_) | copy-start | bytes 663556
  52.8 0.7 copy-start.2
  55.3 20.2 %collective-permute-start.2 = (f32[3,5,8,128]{3,2,1,0:T(8,128)}, f32[3,5,8,128]{3,2,1,0:T(8,128)S(1)}, u32[]{:S(2)}, u32[]{:S(2)}) collective-permute-start(f32[3,5,8,128]{3,2,1,0:T(8,128)} %get-tuple-element.42), channel_id=1, source_target_pairs={{0,1},{1,2},{2,3},{3,4},{4,5},{5,6},{6,7},{7,8},{8,9},{9,10},{10,1... | collective-permute-start | bytes 184328 | tf_op jit(solution)/shard_map/ppermute | solution.py:490
  55.3 20.2 %collective-permute-start.3 = (f32[3,5,8,128]{3,2,1,0:T(8,128)}, f32[3,5,8,128]{3,2,1,0:T(8,128)S(1)}, u32[]{:S(2)}, u32[]{:S(2)}) collective-permute-start(f32[3,5,8,128]{3,2,1,0:T(8,128)} %get-tuple-element.43), channel_id=1, source_target_pairs={{1,0},{2,1},{3,2},{4,3},{5,4},{6,5},{7,6},{8,7},{9,8},{10,9},{11,1... | collective-permute-start | bytes 184328 | tf_op jit(solution)/shard_map/ppermute | solution.py:490
  75.5 0.6 copy-start.8
  75.5 0.6 copy-start.9
  84.6 9.0 %collective-permute-start.4 = (f32[2,18,8,128]{3,2,1,0:T(8,128)}, f32[2,18,8,128]{3,2,1,0:T(8,128)S(1)}, u32[]{:S(2)}, u32[]{:S(2)}) collective-permute-start(f32[2,18,8,128]{3,2,1,0:T(8,128)} %get-tuple-element.49), channel_id=1, source_target_pairs={{0,16},{16,32},{32,48},{48,64},{64,80},{80,96},{96,112},{112,0},{1... | collective-permute-start | bytes 442376 | tf_op jit(solution)/shard_map/ppermute | solution.py:490
  86.3 7.3 %collective-permute-start.5 = (f32[2,18,8,128]{3,2,1,0:T(8,128)}, f32[2,18,8,128]{3,2,1,0:T(8,128)S(1)}, u32[]{:S(2)}, u32[]{:S(2)}) collective-permute-start(f32[2,18,8,128]{3,2,1,0:T(8,128)} %get-tuple-element.50), channel_id=1, source_target_pairs={{16,0},{32,16},{48,32},{64,48},{80,64},{96,80},{112,96},{0,112},{1... | collective-permute-start | bytes 442376 | tf_op jit(solution)/shard_map/ppermute | solution.py:490
  93.6 0.7 copy-start.5
  93.6 0.7 copy-start.6
  96.0 5.7 %collective-permute-start.6 = (f32[2,5,8,128]{3,2,1,0:T(8,128)}, f32[2,5,8,128]{3,2,1,0:T(8,128)S(1)}, u32[]{:S(2)}, u32[]{:S(2)}) collective-permute-start(f32[2,5,8,128]{3,2,1,0:T(8,128)} %get-tuple-element.53), channel_id=1, source_target_pairs={{0,1},{1,2},{2,3},{3,4},{4,5},{5,6},{6,7},{7,8},{8,9},{9,10},{10,1... | collective-permute-start | bytes 122888 | tf_op jit(solution)/shard_map/ppermute | solution.py:490
  96.0 5.8 %collective-permute-start.7 = (f32[2,5,8,128]{3,2,1,0:T(8,128)}, f32[2,5,8,128]{3,2,1,0:T(8,128)S(1)}, u32[]{:S(2)}, u32[]{:S(2)}) collective-permute-start(f32[2,5,8,128]{3,2,1,0:T(8,128)} %get-tuple-element.54), channel_id=1, source_target_pairs={{1,0},{2,1},{3,2},{4,3},{5,4},{6,5},{7,6},{8,7},{9,8},{10,9},{11,1... | collective-permute-start | bytes 122888 | tf_op jit(solution)/shard_map/ppermute | solution.py:490
  101.7 0.6 copy-start.12
  101.8 0.6 copy-start.13
  102.4 24.0 %copy-start = (bf16[2,2,1,5,40,640]{5,4,3,2,1,0:T(8,128)(2,1)S(1)}, bf16[2,2,1,5,40,640]{5,4,3,2,1,0:T(8,128)(2,1)}, u32[]{:S(2)}) copy-start(bf16[2,2,1,5,40,640]{5,4,3,2,1,0:T(8,128)(2,1)} %param.12) | copy-start | bytes 3072004
  110.7 9.2 %collective-permute-start.8 = (f32[2,18,8,128]{3,2,1,0:T(8,128)}, f32[2,18,8,128]{3,2,1,0:T(8,128)S(1)}, u32[]{:S(2)}, u32[]{:S(2)}) collective-permute-start(f32[2,18,8,128]{3,2,1,0:T(8,128)} %get-tuple-element.60), channel_id=1, source_target_pairs={{0,16},{16,32},{32,48},{48,64},{64,80},{80,96},{96,112},{112,0},{1... | collective-permute-start | bytes 442376 | tf_op jit(solution)/shard_map/ppermute | solution.py:490
  113.4 6.9 %collective-permute-start.9 = (f32[2,18,8,128]{3,2,1,0:T(8,128)}, f32[2,18,8,128]{3,2,1,0:T(8,128)S(1)}, u32[]{:S(2)}, u32[]{:S(2)}) collective-permute-start(f32[2,18,8,128]{3,2,1,0:T(8,128)} %get-tuple-element.61), channel_id=1, source_target_pairs={{16,0},{32,16},{48,32},{64,48},{80,64},{96,80},{112,96},{0,112},{1... | collective-permute-start | bytes 442376 | tf_op jit(solution)/shard_map/ppermute | solution.py:490
  119.9 0.7 copy-start.3
  120.3 0.7 copy-start.4
  122.6 14.3 %collective-permute-start.10 = (f32[2,5,8,128]{3,2,1,0:T(8,128)}, f32[2,5,8,128]{3,2,1,0:T(8,128)S(1)}, u32[]{:S(2)}, u32[]{:S(2)}) collective-permute-start(f32[2,5,8,128]{3,2,1,0:T(8,128)} %get-tuple-element.64), channel_id=1, source_target_pairs={{0,1},{1,2},{2,3},{3,4},{4,5},{5,6},{6,7},{7,8},{8,9},{9,10},{10,1... | collective-permute-start | bytes 122888 | tf_op jit(solution)/shard_map/ppermute | solution.py:490
  122.6 14.3 %collective-permute-start.11 = (f32[2,5,8,128]{3,2,1,0:T(8,128)}, f32[2,5,8,128]{3,2,1,0:T(8,128)S(1)}, u32[]{:S(2)}, u32[]{:S(2)}) collective-permute-start(f32[2,5,8,128]{3,2,1,0:T(8,128)} %get-tuple-element.65), channel_id=1, source_target_pairs={{1,0},{2,1},{3,2},{4,3},{5,4},{6,5},{7,6},{8,7},{9,8},{10,9},{11,1... | collective-permute-start | bytes 122888 | tf_op jit(solution)/shard_map/ppermute | solution.py:490
  136.9 0.6 copy-start.10
  136.9 0.6 copy-start.11

commit v2 on v1

--- a/solution.py
+++ b/solution.py
@@ -16,8 +16,11 @@
 padded = 128
 slots = 32
 face_tiles = 18
+kept_tiles = 12288
 VMEM = pl.BlockSpec(memory_space=pltpu.VMEM)
 SMEM = pl.BlockSpec(memory_space=pltpu.SMEM)
+HBM = pl.BlockSpec(memory_space=pltpu.HBM)
+ANY = pl.BlockSpec(memory_space=pl.ANY)
 
 
 def gll_tables():
@@ -62,16 +65,12 @@
 directions = ((5, 1, 25), (25, 1, 5), (25, 5, 1))
 
 
-def for_lines(body):
-    for direction, (outer, inner, step) in enumerate(directions):
-
-        def block(t, carry, direction=direction, outer=outer, inner=inner, step=step):
+def for_lines(body, directions):
+    for outer, inner, step in directions:
+        for t in range(5):
             for line in range(5):
                 base = t * outer + line * inner
-                body(direction, [base + step * n for n in range(5)])
-            return carry
-
-        lax.fori_loop(0, 5, block, 0)
+                body([base + step * n for n in range(5)])
 
 
 def sublane():
@@ -113,17 +112,18 @@
             put_plane(i, k, wide[i, k])
 
 
-def subtract_stiffness(d, f, e, wm):
-    def line(direction, index):
+def force(d, f, e, wm, source):
+    def line(index, before):
         g = apply5(derivative, [d[e, n] for n in index])
         r = apply5(transposed, [g[a] * wm[index[a]] for a in range(5)])
         for a in range(5):
-            f[e, index[a]] = f[e, index[a]] - r[a]
-
-    for_lines(line)
-
-
-def fold(get, put):
+            f[e, index[a]] = before(index[a]) - r[a]
+
+    for_lines(lambda index: line(index, source), directions[:1])
+    for_lines(lambda index: line(index, lambda n: f[e, n]), directions[1:])
+
+
+def fold(get, put, every=False):
     sub, ln = sublane(), lane()
     for i in range(5):
         v = [[get(at(i, j, k)) for k in range(5)] for j in range(5)]
@@ -133,11 +133,12 @@
             v[j][0] = v[j][0] + jnp.where(ln == 0, 0.0, pltpu.roll(v[j][4], 1, 1))
         for j in range(5):
             for k in range(5):
-                if (j, k) == (0, 4) or j == 0 or k == 0:
+                if every or j == 0 or k == 0:
                     put(at(i, j, k), v[j][k])
 
 
 def emit_faces(get, c, face_low, face_high, row_low, row_high):
+    lead = () if c is None else (c,)
     sub, ln = sublane(), lane()
     for i, face in ((0, face_low), (4, face_high)):
         last_row = jnp.zeros((8, 128), f32)
@@ -147,20 +148,20 @@
         for j in range(4):
             last_column = jnp.where(ln == j, column_of(get(at(i, j, 4)), 127), last_column)
             for k in range(4):
-                face[c, j * 4 + k] = get(at(i, j, k))
-        face[c, 16] = last_row
-        face[c, 17] = last_column
+                face[lead + (j * 4 + k,)] = get(at(i, j, k))
+        face[lead + (16,)] = last_row
+        face[lead + (17,)] = last_column
     for i in range(5):
         low = jnp.zeros((8, 128), f32)
         high = jnp.zeros((8, 128), f32)
         for k in range(5):
             low = jnp.where(sub == k, row_of(get(at(i, 0, k)), 0), low)
             high = jnp.where(sub == k, row_of(get(at(i, 4, k)), 7), high)
-        row_low[c, i] = low
-        row_high[c, i] = high
-
-
-def complete(get, i, c, flags, from_below, from_above, from_left, from_right):
+        row_low[lead + (i,)] = low
+        row_high[lead + (i,)] = high
+
+
+def complete(get, i, c, flags, from_below, from_above, from_even, from_odd):
     sub, ln = sublane(), lane()
     v = [[get(at(i, j, k)) for k in range(5)] for j in range(5)]
     if i in (0, 4):
@@ -174,7 +175,8 @@
             v[4][k] = v[4][k] + jnp.where((sub == 7) & keep, row_of(last_row, k), 0.0)
         for j in range(4):
             v[j][4] = v[j][4] + jnp.where((ln == 127) & keep, column_of(last_column, j), 0.0)
-    left, right = from_left[c, i], from_right[c, i]
+    left = jnp.where(flags[4] > 0, from_odd[c, i], from_even[c, i])
+    right = jnp.where(flags[4] > 0, from_even[c, i], from_odd[c, i])
     for k in range(5):
         v[0][k] = v[0][k] + jnp.where((sub == 0) & (flags[2] > 0), row_of(left, k), 0.0)
         v[4][k] = v[4][k] + jnp.where((sub == 7) & (flags[3] > 0), row_of(right, k), 0.0)
@@ -185,7 +187,13 @@
     return v
 
 
-def pack_kernel(traces, owner, point, out):
+def pack_kernel(traces_in, owner_in, point_in, out, traces, owner, point, sems):
+    pairs = ((traces_in, traces), (owner_in, owner), (point_in, point))
+    copies = [pltpu.make_async_copy(a, b, sems.at[n]) for n, (a, b) in enumerate(pairs)]
+    for copy in copies:
+        copy.start()
+    for copy in copies:
+        copy.wait()
     devices = out.shape[0] // 2
     receivers = owner.shape[1]
     p = point[...]
@@ -202,8 +210,8 @@
     ey = divide(row, 5)
     j = row - 5 * ey
     place = ((((i * 5 + j) * 5 + k) * 8 + ey) * 128 + lo).astype(f32)
-    rows = [traces[0, 0:1, :], traces[1, 0:1, :], place, traces[0, 1:2, :]]
-    rows += [traces[1, 1:2, :], traces[0, 2:3, :], traces[1, 2:3, :], jnp.zeros((1, receivers), f32)]
+    rows = [traces[0, 0:1, :], traces[0, 1:2, :], place, traces[1, 0:1, :]]
+    rows += [traces[1, 1:2, :], traces[2, 0:1, :], traces[2, 1:2, :], jnp.zeros((1, receivers), f32)]
     owned = lax.broadcasted_iota(jnp.int32, (devices, receivers), 0) == owner[...]
     owned = jnp.where(owned, 1.0, 0.0)
     before = lax.broadcasted_iota(jnp.int32, (128, 128), 0) < lax.broadcasted_iota(jnp.int32, (128, 128), 1)
@@ -233,124 +241,153 @@
 
 def scatter(places, values, hi_rows, lo_rows, piece_rows, left_side, right_side, store):
     place = places.astype(jnp.int32)
-    hi_rows[...] = place >> 7
-    lo_rows[...] = place & 127
+    hi_rows[...] = (place >> 7).astype(f32)
+    lo_rows[...] = (place & 127).astype(f32)
     count = len(values)
     for c, v in enumerate(values):
         upper = v.astype(bf16).astype(f32)
         piece_rows[2 * c] = upper
         piece_rows[2 * c + 1] = v - upper
-    index = lax.broadcasted_iota(jnp.int32, (128, 128), 0)
-
-    def fill(r, carry):
-        where = pl.ds(pl.multiple_of(r * 128, 128), 128)
-        hi = hi_rows[pl.ds(r, 1), :]
-        lo = lo_rows[pl.ds(r, 1), :]
-        for m in range(8):
-            left_side[m * 128 : (m + 1) * 128, where] = jnp.where(index + m * 128 == hi, 1.0, 0.0).astype(bf16)
-        same = index == lo
-        for n in range(2 * count):
-            right_side[n * 128 : (n + 1) * 128, where] = jnp.where(same, piece_rows[n, pl.ds(r, 1), :], 0.0).astype(bf16)
-        return carry
-
-    lax.fori_loop(0, slots, fill, 0)
-
-    def tile(m, carry):
-        rows = pl.ds(pl.multiple_of(m * 256, 256), 256)
+    index = [lax.broadcasted_iota(jnp.int32, (16, 128), 0).astype(f32) + 16.0 * g for g in range(8)]
+    index = [x.astype(bf16) for x in index]
+    one, zero = jnp.ones((16, 128), bf16), jnp.zeros((16, 128), bf16)
+
+    def fill_right(r):
+        where = slice(r * 128, r * 128 + 128)
+        lo = jnp.broadcast_to(lo_rows[r : r + 1, :], (16, 128)).astype(bf16)
+        pieces = [jnp.broadcast_to(piece_rows[n, r : r + 1, :], (16, 128)).astype(bf16) for n in range(2 * count)]
+        for g in range(8):
+            same = index[g] == lo
+            for n in range(2 * count):
+                at_row = n * 128 + g * 16
+                right_side[at_row : at_row + 16, where] = jnp.where(same, pieces[n], zero)
+
+    def fill_left(r, m):
+        where = slice(r * 128, r * 128 + 128)
+        hi = jnp.broadcast_to(hi_rows[r : r + 1, :], (16, 128))
+        part = (hi - 128.0 * m).astype(bf16)
+        for g in range(8):
+            left_side[m * 128 + g * 16 : m * 128 + g * 16 + 16, where] = jnp.where(index[g] == part, one, zero)
+
+    def fill_tile(m):
+        for r in range(slots):
+            fill_left(r, 2 * m)
+            fill_left(r, 2 * m + 1)
+
+    for r in range(slots):
+        fill_right(r)
+    fill_tile(0)
+    for m in range(4):
+        if m < 3:
+            fill_tile(m + 1)
         for c in range(count):
             both = lax.dot_general(
-                left_side[rows, :],
-                right_side[c * 256 : (c + 1) * 256, :],
+                left_side[m * 256 : m * 256 + 256, :],
+                right_side[c * 256 : c * 256 + 256, :],
                 (((1,), (1,)), ((), ())),
                 preferred_element_type=f32,
             )
-            store(m, c, both[:, :128] + both[:, 128:])
-        return carry
-
-    lax.fori_loop(0, 4, tile, 0)
-
-
-def start_kernel(d0, v0, modulus, density, d_out, v_out, wm, mass, kd, wide):
-    def put_event(e, carry):
-        for source, target in ((d0, d_out), (v0, v_out)):
-
-            def put_field(n, value, target=target):
-                target[e, n] = value
-
-            to_tiles(lambda i, source=source: source[e, i], put_field, wide)
-        return carry
-
-    lax.fori_loop(0, 2, put_event, 0)
-    for source, target in ((modulus, wm), (density, mass)):
-
-        def put_weighted(n, value, target=target):
+            store(c, m, both[:, :128] + both[:, 128:])
+
+
+def start_kernel(d_in, v_in, k_in, m_in, d_out, v_out, wm_out, mass_out, kept, *scratch):
+    d0, v0, modulus, density, d, v, wm, mass, kd, edges, wide, sems = scratch
+    copies = []
+
+    def copy(source, target):
+        copies.append(pltpu.make_async_copy(source, target, sems.at[len(copies)]))
+        copies[-1].start()
+        return copies[-1]
+
+    loads = [copy(k_in, modulus), copy(d_in.at[0], d0.at[0]), copy(d_in.at[1], d0.at[1])]
+    loads += [copy(m_in, density), copy(v_in, v0)]
+
+    def weighted(target):
+        def put(n, value):
             target[n] = value * weight(n // 25, n // 5 % 5, n % 5)
 
-        to_tiles(lambda i, source=source: source[i].astype(f32), put_weighted, wide)
-
-    def put(n, value):
+        return put
+
+    loads[0].wait()
+    to_tiles(lambda i: modulus[i].astype(f32), weighted(wm), wide)
+    copy(wm, wm_out)
+    for e in range(2):
+
+        def put_d(n, value, e=e):
+            d[e, n] = value
+
+        loads[1 + e].wait()
+        to_tiles(lambda i, e=e: d0[e, i], put_d, wide)
+        copy(d.at[e], d_out.at[e])
+        force(d, kd, e, wm, lambda n: 0.0)
+        copy(kd.at[e], kept.at[e * points : e * points + points])
+    loads[3].wait()
+    to_tiles(lambda i: density[i].astype(f32), weighted(mass), wide)
+
+    def put_mass(n, value):
         mass[n] = value
 
-    fold(lambda n: mass[n], put)
-
-    def clear(n, carry):
-        kd[0, n] = jnp.zeros((8, 128), f32)
-        kd[1, n] = jnp.zeros((8, 128), f32)
-        return carry
-
-    lax.fori_loop(0, points, clear, 0)
-
-    def event(e, carry):
-        subtract_stiffness(d_out, kd, e, wm)
-        return carry
-
-    lax.fori_loop(0, 2, event, 0)
-
-
-def first_force_kernel(got, kd, mass, f, face_low, face_high, row_low, row_high, sums, hi_rows, lo_rows, piece_rows, left_side, right_side):
+    fold(lambda n: mass[n], put_mass)
+    copy(mass, mass_out)
+    low, high, row_low, row_high = edges.at[0:18], edges.at[18:36], edges.at[36:41], edges.at[41:46]
+    emit_faces(lambda n: mass[n], None, low, high, row_low, row_high)
+    copy(edges, kept.at[2 * points : 2 * points + 46])
+    loads[4].wait()
+    for e in range(2):
+
+        def put_v(n, value, e=e):
+            v[e, n] = value
+
+        to_tiles(lambda i, e=e: v0[e, i], put_v, wide)
+        copy(v.at[e], v_out.at[e])
+    for pending in copies[len(loads) :]:
+        pending.wait()
+
+
+def first_force_kernel(got, kept, f, face_low, face_high, row_low, row_high, kd, sems, *scratch):
+    edges = kept.at[2 * points : 2 * points + 46]
+    pairs = ((kept.at[0:points], kd.at[0]), (kept.at[points : 2 * points], kd.at[1]))
+    pairs += ((edges.at[0:18], face_low.at[2]), (edges.at[18:36], face_high.at[2]))
+    pairs += ((edges.at[36:41], row_low.at[2]), (edges.at[41:46], row_high.at[2]))
+    copies = [pltpu.make_async_copy(a, b, sems.at[n]) for n, (a, b) in enumerate(pairs)]
+    for copy in copies:
+        copy.start()
     devices = got.shape[0] // 2
     first = got[pl.ds(0, devices, stride=2), :].T
 
-    def store(m, c, value):
-        sums[c, pl.ds(m * 32, 32)] = value.reshape(32, 8, 128)
-
-    scatter(first[64:96], [first[0:32], first[32:64]], hi_rows, lo_rows, piece_rows, left_side, right_side, store)
+    def store(c, m, value):
+        count = min(32, points - 32 * m)
+        f[c, 32 * m : 32 * m + count] = value.reshape(32, 8, 128)[:count]
+
+    scatter(first[64:96], [first[0:32], first[32:64]], *scratch, store)
+    for copy in copies:
+        copy.wait()
 
     def event(e, carry):
-        def get(n):
-            return kd[e, n] + sums[e, n]
-
-        def copy(n, c):
-            f[e, n] = get(n)
-            return c
-
-        lax.fori_loop(0, points, copy, 0)
-
         def put(n, value):
             f[e, n] = value
 
-        fold(lambda n: f[e, n], put)
+        fold(lambda n: f[e, n] + kd[e, n], put, every=True)
         emit_faces(lambda n: f[e, n], e, face_low, face_high, row_low, row_high)
         return carry
 
     lax.fori_loop(0, 2, event, 0)
-    emit_faces(lambda n: mass[n], 2, face_low, face_high, row_low, row_high)
-
-
-def later_sources_kernel(got, s1, s2, hi_rows, lo_rows, piece_rows, left_side, right_side):
+
+
+def source_kernel(step, got, order, s, token, *scratch):
     devices = got.shape[0] // 2
     first = got[pl.ds(0, devices, stride=2), :].T
     second = got[pl.ds(1, devices, stride=2), :].T
-
-    def store(m, c, value):
-        target = s1 if c < 2 else s2
-        target[c % 2, pl.ds(m * 32, 32)] = value.reshape(32, 8, 128)
-
-    values = [first[96:128], second[0:32], second[32:64], second[64:96]]
-    scatter(first[64:96], values, hi_rows, lo_rows, piece_rows, left_side, right_side, store)
-
-
-def rows_kernel(flags, from_below, from_above, row_low, row_high, low_out, high_out):
+    token[...] = jnp.zeros_like(token)
+
+    def store(c, m, value):
+        s[c, 32 * m : 32 * m + 32] = value.reshape(32, 8, 128)
+
+    values = [first[96:128], second[0:32]] if step == 1 else [second[32:64], second[64:96]]
+    scatter(first[64:96], values, *scratch, store)
+
+
+def rows_kernel(flags, from_below, from_above, row_low, row_high, order, even_out, odd_out):
     sub, ln = sublane(), lane()
     for c in range(row_low.shape[0]):
         for i in range(5):
@@ -365,8 +402,8 @@
                 extra = jnp.where((sub == 4) & (ln == 127), corner, extra)
                 low = low + jnp.where(keep, extra, 0.0)
                 high = high + jnp.where(keep, face[c, 16], 0.0)
-            low_out[c, i] = low
-            high_out[c, i] = high
+            even_out[c, i] = jnp.where(flags[4] > 0, high, low)
+            odd_out[c, i] = jnp.where(flags[4] > 0, low, high)
 
 
 def step_kernel(first, *refs):
@@ -393,12 +430,7 @@
                     q_out[e, n] = q_new
                     d_out[e, n] = d[e, n] + time_step * q_new
 
-        def copy(n, c):
-            f_out[e, n] = source[e, n]
-            return c
-
-        lax.fori_loop(0, points, copy, 0)
-        subtract_stiffness(d_out, f_out, e, wm)
+        force(d_out, f_out, e, wm, lambda n: source[e, n])
 
         def put(n, value):
             f_out[e, n] = value
@@ -425,41 +457,34 @@
     lax.fori_loop(0, 2, event, 0)
 
 
-def correlate(d, forward, total, wide, tiles):
+def correlate(d, forward, step, total, wide, tiles):
     def event(e, carry):
         def put(n, value):
             tiles[n] = value
 
-        to_tiles(lambda i: forward[e, i].astype(f32), put, wide)
-
-        def line(direction, index):
+        to_tiles(lambda i: forward[step, e, i].astype(f32), put, wide)
+
+        def line(index):
             g = apply5(derivative, [d[e, n] for n in index])
             h = apply5(derivative, [tiles[n] for n in index])
             for a in range(5):
                 total[index[a]] = total[index[a]] + g[a] * h[a]
 
-        for_lines(line)
+        for_lines(line, directions)
         return carry
 
     lax.fori_loop(0, 2, event, 0)
 
 
-def first_kernel_term(d, forward, total, wide, tiles):
+def term_kernel(d1, d2, forward, wm, out, token, total, wide, tiles):
     def clear(n, carry):
         total[n] = jnp.zeros((8, 128), f32)
         return carry
 
     lax.fori_loop(0, points, clear, 0)
-    correlate(d, forward, total, wide, tiles)
-
-
-def last_kernel_term(d, forward, before, wm, out, total, wide, tiles):
-    def copy(n, carry):
-        total[n] = before[n]
-        return carry
-
-    lax.fori_loop(0, points, copy, 0)
-    correlate(d, forward, total, wide, tiles)
+    correlate(d1, forward, 0, total, wide, tiles)
+    correlate(d2, forward, 1, total, wide, tiles)
+    token[...] = jnp.zeros_like(token)
 
     def tile(i, j, k):
         return total[at(i, j, k)] * wm[at(i, j, k)] * (-time_step / weight(i, j, k))
@@ -470,16 +495,17 @@
     from_tiles(tile, put_plane, wide)
 
 
-def call(kernel, name, out_shapes, args, scratch=(), specs=None, flops=10**6, moved=4 * 10**6):
+def call(kernel, name, out_shapes, args, scratch=(), specs=None, outs=None, flops=10**6, moved=4 * 10**6, vmem=16, **more):
     return pl.pallas_call(
         kernel,
         name=name,
-        out_shape=[jax.ShapeDtypeStruct(s, f32) for s in out_shapes],
+        out_shape=[s if hasattr(s, "dtype") else jax.ShapeDtypeStruct(s, f32) for s in out_shapes],
         in_specs=specs or [VMEM] * len(args),
-        out_specs=[VMEM] * len(out_shapes),
+        out_specs=outs or [VMEM] * len(out_shapes),
         scratch_shapes=list(scratch),
-        compiler_params=pltpu.CompilerParams(vmem_limit_bytes=56 * 2**20),
+        compiler_params=pltpu.CompilerParams(vmem_limit_bytes=vmem * 2**20),
         cost_estimate=pl.CostEstimate(flops=flops, bytes_accessed=moved, transcendentals=0),
+        **more,
     )(*args)
 
 
@@ -494,10 +520,12 @@
     lat, lon = lax.axis_index("lat"), lax.axis_index("lon")
     lat_count, lon_count = lax.axis_size("lat"), lax.axis_size("lon")
     devices = lat_count * lon_count
-    flags = jnp.stack([lat > 0, lat < lat_count - 1, lon > 0, lon < lon_count - 1]).astype(jnp.int32)
+    flags = [lat > 0, lat < lat_count - 1, lon > 0, lon < lon_count - 1, lon % 2 == 0]
+    flags = jnp.stack(flags).astype(jnp.int32)
     field = (2, points, 8, 128)
     one = (points, 8, 128)
     wide_field = (2, padded, 8, 128)
+    token = (8, 128)
     native = d0.shape
     d0, v0 = d0.reshape(2, 5, 40, 640), v0.reshape(2, 5, 40, 640)
     kernel_shape = modulus.shape
@@ -509,54 +537,91 @@
         return [(channels, face_tiles, 8, 128)] * 2 + [(channels, 5, 8, 128)] * 2
 
     (packed,) = call(
-        pack_kernel, "pack", [(2 * devices, 128)], (traces, owner.reshape(1, receivers), point.reshape(1, receivers))
+        pack_kernel,
+        "pack",
+        [(2 * devices, 128)],
+        (traces.transpose(1, 0, 2), owner.reshape(1, receivers), point.reshape(1, receivers)),
+        [
+            pltpu.VMEM((traces.shape[1], traces.shape[0], receivers), f32),
+            pltpu.VMEM((1, receivers), jnp.int32),
+            pltpu.VMEM((1, receivers), jnp.int32),
+            pltpu.SemaphoreType.DMA((3,)),
+        ],
+        [HBM] * 3,
+        vmem=56,
     )
     got = lax.all_to_all(packed.reshape(devices, 2, 128), ("lat", "lon"), 0, 0, tiled=True)
     got = got.reshape(2 * devices, 128)
     wide = pltpu.VMEM((5, 5, 40, 128), f32)
     tiles = pltpu.VMEM(one, f32)
-    d, q, wm, mass, kd = call(
-        start_kernel, "start", [field, field, one, one, field], (d0, v0, modulus, density), [wide], flops=10**8
-    )
-
-    def scatter_scratch(count):
-        return [
-            pltpu.VMEM((slots, devices), jnp.int32),
-            pltpu.VMEM((slots, devices), jnp.int32),
-            pltpu.VMEM((2 * count, slots, devices), f32),
-            pltpu.VMEM((1024, slots * devices), bf16),
-            pltpu.VMEM((256 * count, slots * devices), bf16),
+    d, q, wm, mass, kept = call(
+        start_kernel,
+        "start",
+        [field, field, one, one, (kept_tiles, 8, 128)],
+        (d0, v0, modulus, density),
+        [
+            pltpu.VMEM(d0.shape, f32),
+            pltpu.VMEM(v0.shape, f32),
+            pltpu.VMEM(modulus.shape, bf16),
+            pltpu.VMEM(density.shape, bf16),
         ]
-
+        + [pltpu.VMEM(s, f32) for s in (field, field, one, one, field, (46, 8, 128))]
+        + [wide, pltpu.SemaphoreType.DMA((16,))],
+        [HBM] * 4,
+        [HBM] * 5,
+        flops=10**8,
+        vmem=56,
+    )
+    scatter_scratch = [
+        pltpu.VMEM((slots, devices), f32),
+        pltpu.VMEM((slots, devices), f32),
+        pltpu.VMEM((4, slots, devices), f32),
+        pltpu.VMEM((1024, slots * devices), bf16),
+        pltpu.VMEM((512, slots * devices), bf16),
+    ]
     f, *edges = call(
         first_force_kernel,
         "first_force",
         [field] + faces(3),
-        (got, kd, mass),
-        [pltpu.VMEM(wide_field, f32)] + scatter_scratch(2),
+        (got, kept),
+        [pltpu.VMEM(field, f32), pltpu.SemaphoreType.DMA((6,))] + scatter_scratch,
+        [VMEM, HBM],
         flops=4 * 10**9,
-    )
-    s1, s2 = call(
-        later_sources_kernel, "later_sources", [wide_field, wide_field], (got,), scatter_scratch(4), flops=8 * 10**9
-    )
-
-    def exchange(edges):
+        vmem=18,
+    )
+
+    def source(step, order):
+        return call(
+            functools.partial(source_kernel, step),
+            "source",
+            [wide_field, token],
+            (got, order),
+            scatter_scratch,
+            [VMEM, ANY],
+            flops=4 * 10**9,
+            vmem=18,
+        )
+
+    def exchange(edges, order):
         face_low, face_high, row_low, row_high = edges
         below, above = swap(face_low, face_high, "lat")
-        low, high = call(
+        even, odd = call(
             rows_kernel,
             "rows",
             [row_low.shape] * 2,
-            (flags, below, above, row_low, row_high),
-            specs=[SMEM] + [VMEM] * 4,
+            (flags, below, above, row_low, row_high, order),
+            specs=[SMEM] + [VMEM] * 4 + [ANY],
             moved=4 * 10**5,
+            vmem=4,
         )
-        left, right = swap(low, high, "lon")
-        return below, above, left, right
+        pairs = [(n, n ^ 1) for n in range(lon_count)]
+        between = [(n, (n + 1 if n % 2 else n - 1) % lon_count) for n in range(lon_count)]
+        return below, above, lax.ppermute(even, "lon", pairs), lax.ppermute(odd, "lon", between)
 
     specs = [SMEM] + [VMEM] * 10
-    received = exchange(edges)
-    d, q, inverse, f, *edges = call(
+    s1, order = source(1, edges[2])
+    received = exchange(edges, order)
+    d1, q, inverse, f, *edges = call(
         functools.partial(step_kernel, True),
         "first_step",
         [field, field, one, field] + faces(2),
@@ -564,20 +629,20 @@
         specs=specs,
         flops=10**8,
     )
-    (term,) = call(first_kernel_term, "first_term", [one], (d, forward[0]), [wide, tiles], flops=10**8)
-    received = exchange(edges)
-    d, q, f, *edges = call(
+    s2, order = source(2, edges[2])
+    received = exchange(edges, order)
+    d2, q, f, *edges = call(
         functools.partial(step_kernel, False),
         "second_step",
         [field, field, field] + faces(2),
-        (flags, f, *received, d, q, s2, wm, inverse),
+        (flags, f, *received, d1, q, s2, wm, inverse),
         specs=specs,
         flops=10**8,
     )
-    (kernel,) = call(
-        last_kernel_term, "last_term", [(5, 40, 640)], (d, forward[1], term, wm), [tiles, wide, tiles], flops=10**8
-    )
-    received = exchange(edges)
+    kernel, order = call(
+        term_kernel, "term", [(5, 40, 640), token], (d1, d2, forward, wm), [tiles, wide, tiles], flops=10**8
+    )
+    received = exchange(edges, order)
     (velocity,) = call(
         last_kernel, "last", [(2, 5, 40, 640)], (flags, f, *received, q, inverse), [wide], [SMEM] + [VMEM] * 7
     )

time: 141 us -> 89.5 us (0.63)
  Pallas kernels: 73 us -> 34.2 us
  starting transfers between devices: 39.7 us -> 32.2 us
  local copies, waits for them, and re-layouts: 7.02 us -> 0.13 us
  waiting for transfers between devices: 19.8 us -> 21.9 us
    pallas_call x12, Pallas kernels: 73 us -> 34.2 us  [call(): pl.pallas_call(kernel, name=name, out_shape=[s if hasattr(s, 'dtype') els...]
    ppermute x0 -> x6, waiting for transfers between devices: none -> 13.6 us  [the longest x3 13 us: exchange(): lax.ppermute(odd, 'lon', between)]
    ppermute x12 -> x6, waiting for transfers between devices: 16.7 us -> 3.09 us  [swap(): return (lax.ppermute(high, axis, up), lax.ppermute(low, axis, down))]
    ppermute x12 -> x6, starting transfers between devices: 28.5 us -> 17.1 us  [swap(): return (lax.ppermute(high, axis, up), lax.ppermute(low, axis, down))]
    unnamed x29 -> x10, local copies, waits for them, and re-layouts: 5.97 us -> 0.02 us
    ppermute x0 -> x6, starting transfers between devices: none -> 3.91 us  [the longest x3 3.65 us: exchange(): lax.ppermute(odd, 'lon', between)]
    all_to_all x1, waiting for transfers between devices: 3.11 us -> 5.17 us  [on_device(): lax.all_to_all(packed.reshape(devices, 2, 128), ('lat', 'lon'), 0, 0, til...]
  transfers between devices with their start and end apart: 13 -> 13, of which waited for: 8 -> 7; matrix products, arithmetic and copies ran while one was open for 1% -> 0% of each run, Pallas kernels for 23% -> 20%
where the time goes in v2:
time: 89.5 us; the launch traced here: 89.3 us
  Pallas kernels  34.2 us (38%)
  starting transfers between devices  32.2 us (36%)
  waiting for transfers between devices  21.9 us (24%)
    pallas_call x12, Pallas kernels, call(): pl.pallas_call(kernel, name=name, out_shape=[s if hasattr(s, 'dtype') els...  34.2 us
    ppermute x6, starting transfers between devices, swap(): return (lax.ppermute(high, axis, up), lax.ppermute(low, axis, down))  17.1 us
    ppermute x3, waiting for transfers between devices, exchange(): lax.ppermute(odd, 'lon', between)  13 us
    all_to_all x1, starting transfers between devices, on_device(): lax.all_to_all(packed.reshape(devices, 2, 128), ('lat', 'lon'), 0, 0, til...  11.1 us
    all_to_all x1, waiting for transfers between devices, on_device(): lax.all_to_all(packed.reshape(devices, 2, 128), ('lat', 'lon'), 0, 0, til...  5.17 us
    ppermute x3, starting transfers between devices, exchange(): lax.ppermute(odd, 'lon', between)  3.65 us
    ppermute x6, waiting for transfers between devices, swap(): return (lax.ppermute(high, axis, up), lax.ppermute(low, axis, down))  3.09 us
  transfers between devices with their start and end apart: 13, of which 7 were waited for; matrix products, arithmetic and copies ran while one was open for 0% of the time, Pallas kernels for 20%

profile of v2, /device:TPU:0, one launch (start us, length us, event | category | flops | bytes accessed | tf_op | source)
XLA Modules:
  0.0 89.3 jit_solution(12724653886974969110)
XLA Ops:
  0.6 0.0 copy-start.1
  0.6 2.3 %pack.1 = f32[256,128]{1,0:T(8,128)} custom-call(f32[3,2,1024]{2,1,0:T(2,128)} %bitcast.29, s32[1,1024]{1,0:T(1,128)} %bitcast.30, s32[1,1024]{1,0:T(1,128)} %bitcast.31), custom_call_target="tpu_custom_call" | custom-call | flops 1000000 | bytes 4000000 | tf_op jit(solution)/shard_map/pack/pallas_call | solution.py:499
  2.9 11.1 %all-to-all-start = ((f32[128,2,128]{2,1,0:T(2,128)}), f32[128,2,128]{2,1,0:T(2,128)S(1)}, u32[]{:S(2)}, u32[]{:S(2)}) async-start(f32[128,2,128]{2,1,0:T(2,128)} %bitcast.26), calls=%async_computation | async-start | bytes 262144 | tf_op jit(solution)/shard_map/all_to_all | solution.py:553
  14.1 0.1 stack.23
  14.2 4.1 %start.1 = (f32[2,125,8,128]{3,2,1,0:T(8,128)}, f32[2,125,8,128]{3,2,1,0:T(8,128)}, f32[125,8,128]{2,1,0:T(8,128)}, f32[125,8,128]{2,1,0:T(8,128)}, f32[12288,8,128]{2,1,0:T(8,128)}) custom-call(f32[2,5,40,640]{3,2,1,0:T(8,128)} %bitcast.23, f32[2,5,40,640]{3,2,1,0:T(8,128)} %bitcast.24, bf16[5,40,640]{2,1,0:T(8,128)(2,1)} %bitcast.27, ...), custom_call_target="tpu_custom_call" | custom-call | flops 100000000 | bytes 4000000 | tf_op jit(solution)/shard_map/start/pallas_call | solution.py:499
  18.3 0.0 copy-start
  18.3 0.0 copy-start.2
  18.3 0.0 copy-start.4
  18.3 5.2 %all-to-all-done = f32[128,2,128]{2,1,0:T(2,128)S(1)} async-done(((f32[128,2,128]{2,1,0:T(2,128)}), f32[128,2,128]{2,1,0:T(2,128)S(1)}, u32[]{:S(2)}, u32[]{:S(2)}) %all-to-all-start) | async-done | bytes 131104 | tf_op jit(solution)/shard_map/all_to_all | solution.py:553
  23.5 5.1 %first_force.1 = (f32[2,125,8,128]{3,2,1,0:T(8,128)S(1)}, f32[3,18,8,128]{3,2,1,0:T(8,128)S(1)}, f32[3,18,8,128]{3,2,1,0:T(8,128)S(1)}, f32[3,5,8,128]{3,2,1,0:T(8,128)S(1)}, f32[3,5,8,128]{3,2,1,0:T(8,128)S(1)}) custom-call(f32[256,128]{1,0:T(8,128)S(1)} %bitcast.20, f32[12288,8,128]{2,1,0:T(8,128)} %get-tuple-element.39.kept), custom_call_target="tpu_custom_call" | custom-call | flops 4000000000 | bytes 4000000 | tf_op jit(solution)/shard_map/first_force/pallas_call | solution.py:499
  28.7 1.3 %collective-permute-start = (f32[3,18,8,128]{3,2,1,0:T(8,128)S(1)}, f32[3,18,8,128]{3,2,1,0:T(8,128)S(1)}, u32[]{:S(2)}, u32[]{:S(2)}) collective-permute-start(f32[3,18,8,128]{3,2,1,0:T(8,128)S(1)} %get-tuple-element.41), channel_id=1, source_target_pairs={{0,16},{16,32},{32,48},{48,64},{64,80},{80,96},{96,112},{112,0},{1... | collective-permute-start | bytes 663560 | tf_op jit(solution)/shard_map/ppermute | solution.py:516
  30.0 4.4 %collective-permute-start.1 = (f32[3,18,8,128]{3,2,1,0:T(8,128)S(1)}, f32[3,18,8,128]{3,2,1,0:T(8,128)S(1)}, u32[]{:S(2)}, u32[]{:S(2)}) collective-permute-start(f32[3,18,8,128]{3,2,1,0:T(8,128)S(1)} %get-tuple-element.42), channel_id=1, source_target_pairs={{16,0},{32,16},{48,32},{64,48},{80,64},{96,80},{112,96},{0,112},{1... | collective-permute-start | bytes 663560 | tf_op jit(solution)/shard_map/ppermute | solution.py:516
  34.4 4.8 %source.2 = (f32[2,128,8,128]{3,2,1,0:T(8,128)S(1)}, f32[8,128]{1,0:T(8,128)S(1)}) custom-call(f32[256,128]{1,0:T(8,128)S(1)} %bitcast.21, f32[3,5,8,128]{3,2,1,0:T(8,128)S(1)} %get-tuple-element.43.order.row_low), custom_call_target="tpu_custom_call" | custom-call | flops 4000000000 | bytes 4000000 | tf_op jit(solution)/shard_map/source/pallas_call | solution.py:499
  39.2 1.5 %collective-permute-done.from_below.refs_2_ = f32[3,18,8,128]{3,2,1,0:T(8,128)S(1)} collective-permute-done((f32[3,18,8,128]{3,2,1,0:T(8,128)S(1)}, f32[3,18,8,128]{3,2,1,0:T(8,128)S(1)}, u32[]{:S(2)}, u32[]{:S(2)}) %collective-permute-start) | collective-permute-done | bytes 221216 | tf_op jit(solution)/shard_map/ppermute | solution.py:516
  40.6 1.6 %collective-permute-done.1.from_above.refs_3_ = f32[3,18,8,128]{3,2,1,0:T(8,128)S(1)} collective-permute-done((f32[3,18,8,128]{3,2,1,0:T(8,128)S(1)}, f32[3,18,8,128]{3,2,1,0:T(8,128)S(1)}, u32[]{:S(2)}, u32[]{:S(2)}) %collective-permute-start.1) | collective-permute-done | bytes 221216 | tf_op jit(solution)/shard_map/ppermute | solution.py:516
  42.3 0.6 rows.3
  42.8 0.1 collective-permute-start.2
  42.9 1.7 %collective-permute-start.3 = (f32[3,5,8,128]{3,2,1,0:T(8,128)S(1)}, f32[3,5,8,128]{3,2,1,0:T(8,128)S(1)}, u32[]{:S(2)}, u32[]{:S(2)}) collective-permute-start(f32[3,5,8,128]{3,2,1,0:T(8,128)S(1)} %get-tuple-element.47), channel_id=1, source_target_pairs={{0,15},{1,2},{2,1},{3,4},{4,3},{5,6},{6,5},{7,8},{8,7},{9,10},{10,... | collective-permute-start | bytes 184328 | tf_op jit(solution)/shard_map/ppermute | solution.py:619
  44.6 0.0 collective-permute-done.2.refs_4_
  44.6 4.1 %collective-permute-done.3.refs_5_ = f32[3,5,8,128]{3,2,1,0:T(8,128)S(1)} collective-permute-done((f32[3,5,8,128]{3,2,1,0:T(8,128)S(1)}, f32[3,5,8,128]{3,2,1,0:T(8,128)S(1)}, u32[]{:S(2)}, u32[]{:S(2)}) %collective-permute-start.3) | collective-permute-done | bytes 61472 | tf_op jit(solution)/shard_map/ppermute | solution.py:619
  48.8 0.0 copy-done
  48.8 0.0 copy-done.2
  48.8 0.0 copy-done.4
  48.8 0.0 copy-done.3
  48.8 2.5 %first_step.1 = (f32[2,125,8,128]{3,2,1,0:T(8,128)S(1)}, f32[2,125,8,128]{3,2,1,0:T(8,128)S(1)}, f32[125,8,128]{2,1,0:T(8,128)S(1)}, f32[2,125,8,128]{3,2,1,0:T(...) custom-call(s32[5]{0:T(128)S(1)} %convert_element_type.3.flags.refs_, ...), custom_call_target="tpu_custom_call" | custom-call | flops 100000000 | bytes 4000000 | tf_op jit(solution)/shard_map/first_step/pallas_call | solution.py:499
  51.4 1.7 %collective-permute-start.4 = (f32[2,18,8,128]{3,2,1,0:T(8,128)S(1)}, f32[2,18,8,128]{3,2,1,0:T(8,128)S(1)}, u32[]{:S(2)}, u32[]{:S(2)}) collective-permute-start(f32[2,18,8,128]{3,2,1,0:T(8,128)S(1)} %get-tuple-element.54), channel_id=1, source_target_pairs={{0,16},{16,32},{32,48},{48,64},{64,80},{80,96},{96,112},{112,0},{1... | collective-permute-start | bytes 442376 | tf_op jit(solution)/shard_map/ppermute | solution.py:516
  53.1 4.0 %collective-permute-start.5 = (f32[2,18,8,128]{3,2,1,0:T(8,128)S(1)}, f32[2,18,8,128]{3,2,1,0:T(8,128)S(1)}, u32[]{:S(2)}, u32[]{:S(2)}) collective-permute-start(f32[2,18,8,128]{3,2,1,0:T(8,128)S(1)} %get-tuple-element.55), channel_id=1, source_target_pairs={{16,0},{32,16},{48,32},{64,48},{80,64},{96,80},{112,96},{0,112},{1... | collective-permute-start | bytes 442376 | tf_op jit(solution)/shard_map/ppermute | solution.py:516
  57.1 4.9 %source.3 = (f32[2,128,8,128]{3,2,1,0:T(8,128)S(1)}, f32[8,128]{1,0:T(8,128)S(1)}) custom-call(f32[256,128]{1,0:T(8,128)S(1)} %bitcast.22, f32[2,5,8,128]{3,2,1,0:T(8,128)S(1)} %get-tuple-element.56.order.row_low), custom_call_target="tpu_custom_call" | custom-call | flops 4000000000 | bytes 4000000 | tf_op jit(solution)/shard_map/source/pallas_call | solution.py:499
  61.9 0.0 collective-permute-done.4.from_below.refs_2_
  62.0 0.0 collective-permute-done.5.from_above.refs_3_
  62.0 0.6 rows.4
  62.6 0.1 collective-permute-start.6
  62.6 1.4 %collective-permute-start.7 = (f32[2,5,8,128]{3,2,1,0:T(8,128)S(1)}, f32[2,5,8,128]{3,2,1,0:T(8,128)S(1)}, u32[]{:S(2)}, u32[]{:S(2)}) collective-permute-start(f32[2,5,8,128]{3,2,1,0:T(8,128)S(1)} %get-tuple-element.60), channel_id=1, source_target_pairs={{0,15},{1,2},{2,1},{3,4},{4,3},{5,6},{6,5},{7,8},{8,7},{9,10},{10,... | collective-permute-start | bytes 122888 | tf_op jit(solution)/shard_map/ppermute | solution.py:619
  64.0 0.0 collective-permute-done.6.refs_4_
  64.0 4.5 %collective-permute-done.7.refs_5_ = f32[2,5,8,128]{3,2,1,0:T(8,128)S(1)} collective-permute-done((f32[2,5,8,128]{3,2,1,0:T(8,128)S(1)}, f32[2,5,8,128]{3,2,1,0:T(8,128)S(1)}, u32[]{:S(2)}, u32[]{:S(2)}) %collective-permute-start.7) | collective-permute-done | bytes 40992 | tf_op jit(solution)/shard_map/ppermute | solution.py:619
  68.5 2.4 %second_step.1 = (f32[2,125,8,128]{3,2,1,0:T(8,128)S(1)}, f32[2,125,8,128]{3,2,1,0:T(8,128)S(1)}, f32[2,125,8,128]{3,2,1,0:T(8,128)S(1)}, f32[2,18,8,128]{3,2,1,...) custom-call(s32[5]{0:T(128)S(1)} %convert_element_type.3.flags.refs_0_, ...), custom_call_target="tpu_custom_call" | custom-call | flops 100000000 | bytes 4000000 | tf_op jit(solution)/shard_map/second_step/pallas_call | solution.py:499
  70.9 1.0 %collective-permute-start.8 = (f32[2,18,8,128]{3,2,1,0:T(8,128)S(1)}, f32[2,18,8,128]{3,2,1,0:T(8,128)S(1)}, u32[]{:S(2)}, u32[]{:S(2)}) collective-permute-start(f32[2,18,8,128]{3,2,1,0:T(8,128)S(1)} %get-tuple-element.66), channel_id=1, source_target_pairs={{0,16},{16,32},{32,48},{48,64},{64,80},{80,96},{96,112},{112,0},{1... | collective-permute-start | bytes 442376 | tf_op jit(solution)/shard_map/ppermute | solution.py:516
  71.9 4.7 %collective-permute-start.9 = (f32[2,18,8,128]{3,2,1,0:T(8,128)S(1)}, f32[2,18,8,128]{3,2,1,0:T(8,128)S(1)}, u32[]{:S(2)}, u32[]{:S(2)}) collective-permute-start(f32[2,18,8,128]{3,2,1,0:T(8,128)S(1)} %get-tuple-element.67), channel_id=1, source_target_pairs={{16,0},{32,16},{48,32},{64,48},{80,64},{96,80},{112,96},{0,112},{1... | collective-permute-start | bytes 442376 | tf_op jit(solution)/shard_map/ppermute | solution.py:516
  76.6 0.0 copy-done.1
  76.6 4.5 %term.1 = (f32[5,40,640]{2,1,0:T(8,128)}, f32[8,128]{1,0:T(8,128)S(1)}) custom-call(f32[2,125,8,128]{3,2,1,0:T(8,128)S(1)} %get-tuple-element.61.refs_6_.d1, f32[2,125,8,128]{3,2,1,0:T(8,128)S(1)} %get-tuple-element.70.d2, bf16[2,2,5,40,640]{4,3,2,1,0:T(8,128)(2,1)S(1)} %bitcast.19, f32[125,8,128]{2,1,0:T(8,128)S(1)} %copy-done), custom_call_target="tpu_custom_call" | custom-call | flops 100000000 | bytes 4000000 | tf_op jit(solution)/shard_map/term/pallas_call | solution.py:499
  81.0 0.0 collective-permute-done.8.from_below.below
  81.1 0.0 collective-permute-done.9.from_above.above
  81.1 0.6 rows.5
  81.6 0.1 collective-permute-start.10
  81.7 0.6 collective-permute-start.11
  82.3 0.6 collective-permute-done.10.left
  82.9 4.4 %collective-permute-done.11.right = f32[2,5,8,128]{3,2,1,0:T(8,128)S(1)} collective-permute-done((f32[2,5,8,128]{3,2,1,0:T(8,128)S(1)}, f32[2,5,8,128]{3,2,1,0:T(8,128)S(1)}, u32[]{:S(2)}, u32[]{:S(2)}) %collective-permute-start.11) | collective-permute-done | bytes 40992 | tf_op jit(solution)/shard_map/ppermute | solution.py:619
  87.4 1.9 %last.1 = f32[2,5,40,640]{3,2,1,0:T(8,128)} custom-call(s32[5]{0:T(128)S(1)} %convert_element_type.3.flags.refs_0_, f32[2,125,8,128]{3,2,1,0:T(8,128)S(1)} %get-tuple-element.65.f, f32[2,18,8,128]{3,2,1,0:T(8,128)S(1)} %collective-permute-done.8.from_below.below, f32[2,18,8,128]{3,2,1,0:T(8,128)S(1)} %collective-permute-done.9.from_above.above, ...), custom_call_target="tpu_custom_call" | custom-call | flops 1000000 | bytes 4000000 | tf_op jit(solution)/shard_map/last/pallas_call | solution.py:499
  (2 shorter events, 0.0 us)
Async XLA Ops:
  0.6 76.0 %copy-start.1 = (bf16[2,2,1,5,40,640]{5,4,3,2,1,0:T(8,128)(2,1)S(1)}, bf16[2,2,1,5,40,640]{5,4,3,2,1,0:T(8,128)(2,1)}, u32[]{:S(2)}) copy-start(bf16[2,2,1,5,40,640]{5,4,3,2,1,0:T(8,128)(2,1)} %param.12) | copy-start | bytes 3072004
  2.9 20.6 %all-to-all-start = ((f32[128,2,128]{2,1,0:T(2,128)}), f32[128,2,128]{2,1,0:T(2,128)S(1)}, u32[]{:S(2)}, u32[]{:S(2)}) async-start(f32[128,2,128]{2,1,0:T(2,128)} %bitcast.26), calls=%async_computation | async-start | bytes 262144 | tf_op jit(solution)/shard_map/all_to_all | solution.py:553
  18.3 30.5 %copy-start = (f32[125,8,128]{2,1,0:T(8,128)S(1)}, f32[125,8,128]{2,1,0:T(8,128)}, u32[]{:S(2)}) copy-start(f32[125,8,128]{2,1,0:T(8,128)} %get-tuple-element.51.refs_9_.wm) | copy-start | bytes 1536004
  18.3 30.5 %copy-start.2 = (f32[2,125,8,128]{3,2,1,0:T(8,128)S(1)}, f32[2,125,8,128]{3,2,1,0:T(8,128)}, u32[]{:S(2)}) copy-start(f32[2,125,8,128]{3,2,1,0:T(8,128)} %get-tuple-element.48.refs_6_) | copy-start | bytes 3072004
  18.3 30.4 %copy-start.4 = (f32[125,8,128]{2,1,0:T(8,128)S(1)}, f32[125,8,128]{2,1,0:T(8,128)}, u32[]{:S(2)}) copy-start(f32[125,8,128]{2,1,0:T(8,128)} %get-tuple-element.52.refs_10_) | copy-start | bytes 1536004
  23.5 25.3 %copy-start.3 = (f32[2,125,8,128]{3,2,1,0:T(8,128)S(1)}, f32[2,125,8,128]{3,2,1,0:T(8,128)}, u32[]{:S(2)}) copy-start(f32[2,125,8,128]{3,2,1,0:T(8,128)} %get-tuple-element.49.refs_7_) | copy-start | bytes 3072004
  28.7 12.0 %collective-permute-start = (f32[3,18,8,128]{3,2,1,0:T(8,128)S(1)}, f32[3,18,8,128]{3,2,1,0:T(8,128)S(1)}, u32[]{:S(2)}, u32[]{:S(2)}) collective-permute-start(f32[3,18,8,128]{3,2,1,0:T(8,128)S(1)} %get-tuple-element.41), channel_id=1, source_target_pairs={{0,16},{16,32},{32,48},{48,64},{64,80},{80,96},{96,112},{112,0},{1... | collective-permute-start | bytes 663560 | tf_op jit(solution)/shard_map/ppermute | solution.py:516
  30.0 12.3 %collective-permute-start.1 = (f32[3,18,8,128]{3,2,1,0:T(8,128)S(1)}, f32[3,18,8,128]{3,2,1,0:T(8,128)S(1)}, u32[]{:S(2)}, u32[]{:S(2)}) collective-permute-start(f32[3,18,8,128]{3,2,1,0:T(8,128)S(1)} %get-tuple-element.42), channel_id=1, source_target_pairs={{16,0},{32,16},{48,32},{64,48},{80,64},{96,80},{112,96},{0,112},{1... | collective-permute-start | bytes 663560 | tf_op jit(solution)/shard_map/ppermute | solution.py:516
  42.8 1.8 %collective-permute-start.2 = (f32[3,5,8,128]{3,2,1,0:T(8,128)S(1)}, f32[3,5,8,128]{3,2,1,0:T(8,128)S(1)}, u32[]{:S(2)}, u32[]{:S(2)}) collective-permute-start(f32[3,5,8,128]{3,2,1,0:T(8,128)S(1)} %get-tuple-element.46), channel_id=1, source_target_pairs={{0,1},{1,0},{2,3},{3,2},{4,5},{5,4},{6,7},{7,6},{8,9},{9,8},{10,11... | collective-permute-start | bytes 184328 | tf_op jit(solution)/shard_map/ppermute | solution.py:619
  42.9 5.8 %collective-permute-start.3 = (f32[3,5,8,128]{3,2,1,0:T(8,128)S(1)}, f32[3,5,8,128]{3,2,1,0:T(8,128)S(1)}, u32[]{:S(2)}, u32[]{:S(2)}) collective-permute-start(f32[3,5,8,128]{3,2,1,0:T(8,128)S(1)} %get-tuple-element.47), channel_id=1, source_target_pairs={{0,15},{1,2},{2,1},{3,4},{4,3},{5,6},{6,5},{7,8},{8,7},{9,10},{10,... | collective-permute-start | bytes 184328 | tf_op jit(solution)/shard_map/ppermute | solution.py:619
  51.4 10.6 %collective-permute-start.4 = (f32[2,18,8,128]{3,2,1,0:T(8,128)S(1)}, f32[2,18,8,128]{3,2,1,0:T(8,128)S(1)}, u32[]{:S(2)}, u32[]{:S(2)}) collective-permute-start(f32[2,18,8,128]{3,2,1,0:T(8,128)S(1)} %get-tuple-element.54), channel_id=1, source_target_pairs={{0,16},{16,32},{32,48},{48,64},{64,80},{80,96},{96,112},{112,0},{1... | collective-permute-start | bytes 442376 | tf_op jit(solution)/shard_map/ppermute | solution.py:516
  53.1 8.9 %collective-permute-start.5 = (f32[2,18,8,128]{3,2,1,0:T(8,128)S(1)}, f32[2,18,8,128]{3,2,1,0:T(8,128)S(1)}, u32[]{:S(2)}, u32[]{:S(2)}) collective-permute-start(f32[2,18,8,128]{3,2,1,0:T(8,128)S(1)} %get-tuple-element.55), channel_id=1, source_target_pairs={{16,0},{32,16},{48,32},{64,48},{80,64},{96,80},{112,96},{0,112},{1... | collective-permute-start | bytes 442376 | tf_op jit(solution)/shard_map/ppermute | solution.py:516
  62.6 1.5 %collective-permute-start.6 = (f32[2,5,8,128]{3,2,1,0:T(8,128)S(1)}, f32[2,5,8,128]{3,2,1,0:T(8,128)S(1)}, u32[]{:S(2)}, u32[]{:S(2)}) collective-permute-start(f32[2,5,8,128]{3,2,1,0:T(8,128)S(1)} %get-tuple-element.59), channel_id=1, source_target_pairs={{0,1},{1,0},{2,3},{3,2},{4,5},{5,4},{6,7},{7,6},{8,9},{9,8},{10,11... | collective-permute-start | bytes 122888 | tf_op jit(solution)/shard_map/ppermute | solution.py:619
  62.6 5.8 %collective-permute-start.7 = (f32[2,5,8,128]{3,2,1,0:T(8,128)S(1)}, f32[2,5,8,128]{3,2,1,0:T(8,128)S(1)}, u32[]{:S(2)}, u32[]{:S(2)}) collective-permute-start(f32[2,5,8,128]{3,2,1,0:T(8,128)S(1)} %get-tuple-element.60), channel_id=1, source_target_pairs={{0,15},{1,2},{2,1},{3,4},{4,3},{5,6},{6,5},{7,8},{8,7},{9,10},{10,... | collective-permute-start | bytes 122888 | tf_op jit(solution)/shard_map/ppermute | solution.py:619
  70.9 10.2 %collective-permute-start.8 = (f32[2,18,8,128]{3,2,1,0:T(8,128)S(1)}, f32[2,18,8,128]{3,2,1,0:T(8,128)S(1)}, u32[]{:S(2)}, u32[]{:S(2)}) collective-permute-start(f32[2,18,8,128]{3,2,1,0:T(8,128)S(1)} %get-tuple-element.66), channel_id=1, source_target_pairs={{0,16},{16,32},{32,48},{48,64},{64,80},{80,96},{96,112},{112,0},{1... | collective-permute-start | bytes 442376 | tf_op jit(solution)/shard_map/ppermute | solution.py:516
  71.9 9.2 %collective-permute-start.9 = (f32[2,18,8,128]{3,2,1,0:T(8,128)S(1)}, f32[2,18,8,128]{3,2,1,0:T(8,128)S(1)}, u32[]{:S(2)}, u32[]{:S(2)}) collective-permute-start(f32[2,18,8,128]{3,2,1,0:T(8,128)S(1)} %get-tuple-element.67), channel_id=1, source_target_pairs={{16,0},{32,16},{48,32},{64,48},{80,64},{96,80},{112,96},{0,112},{1... | collective-permute-start | bytes 442376 | tf_op jit(solution)/shard_map/ppermute | solution.py:516
  81.6 1.3 %collective-permute-start.10 = (f32[2,5,8,128]{3,2,1,0:T(8,128)S(1)}, f32[2,5,8,128]{3,2,1,0:T(8,128)S(1)}, u32[]{:S(2)}, u32[]{:S(2)}) collective-permute-start(f32[2,5,8,128]{3,2,1,0:T(8,128)S(1)} %get-tuple-element.72), channel_id=1, source_target_pairs={{0,1},{1,0},{2,3},{3,2},{4,5},{5,4},{6,7},{7,6},{8,9},{9,8},{10,11... | collective-permute-start | bytes 122888 | tf_op jit(solution)/shard_map/ppermute | solution.py:619
  81.7 5.6 %collective-permute-start.11 = (f32[2,5,8,128]{3,2,1,0:T(8,128)S(1)}, f32[2,5,8,128]{3,2,1,0:T(8,128)S(1)}, u32[]{:S(2)}, u32[]{:S(2)}) collective-permute-start(f32[2,5,8,128]{3,2,1,0:T(8,128)S(1)} %get-tuple-element.73), channel_id=1, source_target_pairs={{0,15},{1,2},{2,1},{3,4},{4,3},{5,6},{6,5},{7,8},{8,7},{9,10},{10,... | collective-permute-start | bytes 122888 | tf_op jit(solution)/shard_map/ppermute | solution.py:619

commit v3 on v2

--- a/solution.py
+++ b/solution.py
@@ -137,7 +137,7 @@
                     put(at(i, j, k), v[j][k])
 
 
-def emit_faces(get, c, face_low, face_high, row_low, row_high):
+def emit_faces(get, c, face_low, face_high, row_low=None, row_high=None):
     lead = () if c is None else (c,)
     sub, ln = sublane(), lane()
     for i, face in ((0, face_low), (4, face_high)):
@@ -151,7 +151,7 @@
                 face[lead + (j * 4 + k,)] = get(at(i, j, k))
         face[lead + (16,)] = last_row
         face[lead + (17,)] = last_column
-    for i in range(5):
+    for i in range(5) if row_low is not None else ():
         low = jnp.zeros((8, 128), f32)
         high = jnp.zeros((8, 128), f32)
         for k in range(5):
@@ -161,7 +161,7 @@
         row_high[lead + (i,)] = high
 
 
-def complete(get, i, c, flags, from_below, from_above, from_even, from_odd):
+def complete(get, i, c, flags, from_below, from_above, left=None, right=None):
     sub, ln = sublane(), lane()
     v = [[get(at(i, j, k)) for k in range(5)] for j in range(5)]
     if i in (0, 4):
@@ -175,16 +175,33 @@
             v[4][k] = v[4][k] + jnp.where((sub == 7) & keep, row_of(last_row, k), 0.0)
         for j in range(4):
             v[j][4] = v[j][4] + jnp.where((ln == 127) & keep, column_of(last_column, j), 0.0)
-    left = jnp.where(flags[4] > 0, from_odd[c, i], from_even[c, i])
-    right = jnp.where(flags[4] > 0, from_even[c, i], from_odd[c, i])
-    for k in range(5):
-        v[0][k] = v[0][k] + jnp.where((sub == 0) & (flags[2] > 0), row_of(left, k), 0.0)
-        v[4][k] = v[4][k] + jnp.where((sub == 7) & (flags[3] > 0), row_of(right, k), 0.0)
+    if left is not None:
+        for k in range(5):
+            v[0][k] = v[0][k] + jnp.where((sub == 0) & (flags[2] > 0), row_of(left, k), 0.0)
+            v[4][k] = v[4][k] + jnp.where((sub == 7) & (flags[3] > 0), row_of(right, k), 0.0)
     for k in range(5):
         v[4][k] = jnp.where(sub == 7, v[4][k], pltpu.roll(v[0][k], 7, 0))
     for j in range(5):
         v[j][4] = jnp.where(ln == 127, v[j][4], pltpu.roll(v[j][0], 127, 1))
     return v
+
+
+def sides(flags, from_even, from_odd, *index):
+    even, odd = from_even[index], from_odd[index]
+    return jnp.where(flags[4] > 0, odd, even), jnp.where(flags[4] > 0, even, odd)
+
+
+def send_sides(flags, even_out, odd_out, index, low, high):
+    even_out[index] = jnp.where(flags[4] > 0, high, low)
+    odd_out[index] = jnp.where(flags[4] > 0, low, high)
+
+
+def stack_rows(rows, first=0, tile=None):
+    sub = sublane()
+    tile = jnp.zeros((8, 128), f32) if tile is None else tile
+    for n, (source, index) in enumerate(rows):
+        tile = jnp.where(sub == first + n, row_of(source, index), tile)
+    return tile
 
 
 def pack_kernel(traces_in, owner_in, point_in, out, traces, owner, point, sems):
@@ -290,8 +307,8 @@
             store(c, m, both[:, :128] + both[:, 128:])
 
 
-def start_kernel(d_in, v_in, k_in, m_in, d_out, v_out, wm_out, mass_out, kept, *scratch):
-    d0, v0, modulus, density, d, v, wm, mass, kd, edges, wide, sems = scratch
+def start_kernel(d_in, v_in, k_in, m_in, d_out, v_out, wm_out, mass_out, rim_out, kept, *scratch):
+    d0, v0, modulus, density, d, v, wm, mass, rim, kd, edges, wide, sems = scratch
     copies = []
 
     def copy(source, target):
@@ -311,6 +328,12 @@
     loads[0].wait()
     to_tiles(lambda i: modulus[i].astype(f32), weighted(wm), wide)
     copy(wm, wm_out)
+    for i in range(5):
+        for j in range(5):
+            tiles = [wm[at(i, j, k)] for k in range(5)]
+            rim[0, i * 5 + j] = stack_rows([(tile, 0) for tile in tiles])
+            rim[1, i * 5 + j] = stack_rows([(tile, 7) for tile in tiles])
+    copy(rim, rim_out)
     for e in range(2):
 
         def put_d(n, value, e=e):
@@ -387,7 +410,7 @@
     scatter(first[64:96], values, *scratch, store)
 
 
-def rows_kernel(flags, from_below, from_above, row_low, row_high, order, even_out, odd_out):
+def rows_kernel(flags, from_below, from_above, row_low, row_high, wm_rim, order, even_out, odd_out):
     sub, ln = sublane(), lane()
     for c in range(row_low.shape[0]):
         for i in range(5):
@@ -395,57 +418,150 @@
             if i in (0, 4):
                 face = from_below if i == 0 else from_above
                 keep = flags[0 if i == 0 else 1] > 0
-                extra = jnp.zeros((8, 128), f32)
-                for k in range(4):
-                    extra = jnp.where(sub == k, row_of(face[c, k], 0), extra)
+                extra = stack_rows([(face[c, k], 0) for k in range(4)])
                 corner = jnp.broadcast_to(face[c, 17][0:1, 0:1], (8, 128))
                 extra = jnp.where((sub == 4) & (ln == 127), corner, extra)
                 low = low + jnp.where(keep, extra, 0.0)
                 high = high + jnp.where(keep, face[c, 16], 0.0)
-            even_out[c, i] = jnp.where(flags[4] > 0, high, low)
-            odd_out[c, i] = jnp.where(flags[4] > 0, low, high)
-
-
-def step_kernel(first, *refs):
-    if first:
-        flags, f, below, above, left, right, d, q, source, wm, mass = refs[:11]
-        d_out, q_out, inverse, f_out, face_low, face_high, row_low, row_high = refs[11:]
-        for i in range(5):
-            v = complete(lambda n: mass[n], i, 2, flags, below, above, left, right)
-            for j in range(5):
-                for k in range(5):
-                    inverse[at(i, j, k)] = 1.0 / v[j][k]
-    else:
-        flags, f, below, above, left, right, d, q, source, wm, inverse = refs[:11]
-        d_out, q_out, f_out, face_low, face_high, row_low, row_high = refs[11:]
-    share = 0.5 * time_step if first else time_step
+            send_sides(flags, even_out, odd_out, c * 5 + i, low, high)
+    for n in range(25):
+        send_sides(flags, even_out, odd_out, 15 + n, wm_rim[0, n], wm_rim[1, n])
+
+
+def first_step_kernel(flags, f, below, above, even, odd, d, q, source, wm, mass, *refs):
+    d_out, q_out, inverse, f_out, face_low, face_high = refs
+    for i in range(5):
+        v = complete(lambda n: mass[n], i, 2, flags, below, above, *sides(flags, even, odd, 10 + i))
+        for j in range(5):
+            for k in range(5):
+                inverse[at(i, j, k)] = 1.0 / v[j][k]
 
     def event(e, carry):
         for i in range(5):
-            v = complete(lambda n: f[e, n], i, e, flags, below, above, left, right)
+            v = complete(lambda n: f[e, n], i, e, flags, below, above, *sides(flags, even, odd, e * 5 + i))
             for j in range(5):
                 for k in range(5):
                     n = at(i, j, k)
-                    q_new = q[e, n] + share * (v[j][k] * inverse[n])
+                    q_new = q[e, n] + 0.5 * time_step * (v[j][k] * inverse[n])
                     q_out[e, n] = q_new
                     d_out[e, n] = d[e, n] + time_step * q_new
-
         force(d_out, f_out, e, wm, lambda n: source[e, n])
 
         def put(n, value):
             f_out[e, n] = value
 
         fold(lambda n: f_out[e, n], put)
-        emit_faces(lambda n: f_out[e, n], e, face_low, face_high, row_low, row_high)
+        emit_faces(lambda n: f_out[e, n], e, face_low, face_high)
         return carry
 
     lax.fori_loop(0, 2, event, 0)
 
 
-def last_kernel(flags, f, below, above, left, right, q, inverse, velocity, wide):
+def advance_kernel(flags, f, below, above, d, q, inverse, source, d_out, q_out, even_out, odd_out):
     def event(e, carry):
         for i in range(5):
-            v = complete(lambda n: f[e, n], i, e, flags, below, above, left, right)
+            v = complete(lambda n: f[e, n], i, e, flags, below, above)
+            new = [[None] * 5 for _ in range(5)]
+            for j in range(5):
+                for k in range(5):
+                    n = at(i, j, k)
+                    q_new = q[e, n] + time_step * (v[j][k] * inverse[n])
+                    q_out[e, n] = q_new
+                    new[j][k] = d[e, n] + time_step * q_new
+                    d_out[e, n] = new[j][k]
+            for m in range(4):
+                low = stack_rows([(new[m + 1][k], 0) for k in range(5)])
+                high = stack_rows([(new[m][k], 7) for k in range(5)])
+                which = range(3) if m % 2 == 0 else range(3, 5)
+                if m < 2:
+                    low = stack_rows([(v[0][k], 0) for k in which], 5, low)
+                    high = stack_rows([(v[4][k], 7) for k in which], 5, high)
+                else:
+                    low = stack_rows([(source[e, at(i, 0, k)], 0) for k in which], 5, low)
+                    high = stack_rows([(source[e, at(i, 4, k)], 7) for k in which], 5, high)
+                send_sides(flags, even_out, odd_out, (e, i * 4 + m), low, high)
+        return carry
+
+    lax.fori_loop(0, 2, event, 0)
+
+
+def along_sublanes(matrix, tile):
+    sub = sublane()
+    total = None
+    for n in range(5):
+        weights = jnp.zeros((8, 128), f32)
+        for m in range(5):
+            weights = jnp.where(sub == m, float(matrix[m, n]), weights)
+        term = weights * row_of(tile, n)
+        total = term if total is None else total + term
+    return total
+
+
+def rim_force(u, wm, near):
+    out = []
+    gx = apply5(derivative, [u[i][near] for i in range(5)])
+    rx = apply5(transposed, [gx[i] * wm[i][near] for i in range(5)])
+    for i in range(5):
+        gy = apply5(derivative, u[i])
+        ry = apply5(transposed, [gy[j] * wm[i][j] for j in range(5)])[near]
+        gz = along_sublanes(derivative, u[i][near])
+        rz = along_sublanes(transposed, gz * wm[i][near])
+        out.append(rx[i] + ry + rz)
+    return out
+
+
+def second_step_kernel(flags, even, odd, wm_even, wm_odd, d, q, inverse, source, wm, *refs):
+    d_out, q_out, f_out, face_low, face_high = refs
+    sub = sublane()
+
+    def event(e, carry):
+        for i in range(5):
+            message = [sides(flags, even, odd, e, i * 4 + m) for m in range(4)]
+            for j in range(5):
+                for k in range(5):
+                    n = at(i, j, k)
+                    d_new, q_new = d[e, n], q[e, n]
+                    if j in (0, 4):
+                        side = 0 if j == 0 else 1
+                        row = row_of(message[0][side], 5 + k) if k < 3 else row_of(message[1][side], 2 + k)
+                        mine = (sub == (0 if j == 0 else 7)) & (flags[2 + side] > 0)
+                        change = time_step * (jnp.where(mine, row, 0.0) * inverse[n])
+                        q_new = q_new + change
+                        d_new = d_new + time_step * change
+                    d_out[e, n] = d_new
+                    q_out[e, n] = q_new
+        force(d_out, f_out, e, wm, lambda n: source[e, n])
+        for side in range(2):
+            j, edge = (0, 0) if side == 0 else (4, 7)
+            near = 4 - j
+            u, w, message = [], [], []
+            for i in range(5):
+                message.append([sides(flags, even, odd, e, i * 4 + m)[side] for m in range(4)])
+                shared = stack_rows([(d_out[e, at(i, j, k)], edge) for k in range(5)])
+                u.append(message[i] + [shared] if near == 4 else [shared] + message[i])
+                w.append([sides(flags, wm_even, wm_odd, 15 + i * 5 + m)[side] for m in range(5)])
+            r = rim_force(u, w, near)
+            mine = (sub == edge) & (flags[2 + side] > 0)
+            for i in range(5):
+                for k in range(5):
+                    row = row_of(message[i][2], 5 + k) if k < 3 else row_of(message[i][3], 2 + k)
+                    n = at(i, j, k)
+                    f_out[e, n] = f_out[e, n] + jnp.where(mine, row - row_of(r[i], k), 0.0)
+
+        def put(n, value):
+            f_out[e, n] = value
+
+        fold(lambda n: f_out[e, n], put)
+        emit_faces(lambda n: f_out[e, n], e, face_low, face_high)
+        return carry
+
+    lax.fori_loop(0, 2, event, 0)
+
+
+def last_kernel(flags, f, below, above, q, inverse, order, velocity, wide):
+    def event(e, carry):
+        for i in range(5):
+            v = complete(lambda n: f[e, n], i, e, flags, below, above)
             for j in range(5):
                 for k in range(5):
                     n = at(i, j, k)
@@ -534,7 +650,7 @@
     receivers = owner.shape[0]
 
     def faces(channels):
-        return [(channels, face_tiles, 8, 128)] * 2 + [(channels, 5, 8, 128)] * 2
+        return [(channels, face_tiles, 8, 128)] * 2
 
     (packed,) = call(
         pack_kernel,
@@ -554,10 +670,11 @@
     got = got.reshape(2 * devices, 128)
     wide = pltpu.VMEM((5, 5, 40, 128), f32)
     tiles = pltpu.VMEM(one, f32)
-    d, q, wm, mass, kept = call(
+    rim = (2, 25, 8, 128)
+    d, q, wm, mass, wm_rim, kept = call(
         start_kernel,
         "start",
-        [field, field, one, one, (kept_tiles, 8, 128)],
+        [field, field, one, one, rim, (kept_tiles, 8, 128)],
         (d0, v0, modulus, density),
         [
             pltpu.VMEM(d0.shape, f32),
@@ -565,10 +682,10 @@
             pltpu.VMEM(modulus.shape, bf16),
             pltpu.VMEM(density.shape, bf16),
         ]
-        + [pltpu.VMEM(s, f32) for s in (field, field, one, one, field, (46, 8, 128))]
+        + [pltpu.VMEM(s, f32) for s in (field, field, one, one, rim, field, (46, 8, 128))]
         + [wide, pltpu.SemaphoreType.DMA((16,))],
         [HBM] * 4,
-        [HBM] * 5,
+        [HBM] * 6,
         flops=10**8,
         vmem=56,
     )
@@ -582,7 +699,7 @@
     f, *edges = call(
         first_force_kernel,
         "first_force",
-        [field] + faces(3),
+        [field] + faces(3) + [(3, 5, 8, 128)] * 2,
         (got, kept),
         [pltpu.VMEM(field, f32), pltpu.SemaphoreType.DMA((6,))] + scatter_scratch,
         [VMEM, HBM],
@@ -602,49 +719,62 @@
             vmem=18,
         )
 
-    def exchange(edges, order):
-        face_low, face_high, row_low, row_high = edges
-        below, above = swap(face_low, face_high, "lat")
-        even, odd = call(
-            rows_kernel,
-            "rows",
-            [row_low.shape] * 2,
-            (flags, below, above, row_low, row_high, order),
-            specs=[SMEM] + [VMEM] * 4 + [ANY],
-            moved=4 * 10**5,
-            vmem=4,
-        )
+    def trade(even, odd):
         pairs = [(n, n ^ 1) for n in range(lon_count)]
         between = [(n, (n + 1 if n % 2 else n - 1) % lon_count) for n in range(lon_count)]
-        return below, above, lax.ppermute(even, "lon", pairs), lax.ppermute(odd, "lon", between)
-
-    specs = [SMEM] + [VMEM] * 10
-    s1, order = source(1, edges[2])
-    received = exchange(edges, order)
+        return lax.ppermute(even, "lon", pairs), lax.ppermute(odd, "lon", between)
+
+    face_low, face_high, row_low, row_high = edges
+    s1, order = source(1, row_low)
+    beside = swap(face_low, face_high, "lat")
+    first_message = call(
+        rows_kernel,
+        "rows",
+        [(40, 8, 128)] * 2,
+        (flags, *beside, row_low, row_high, wm_rim, order),
+        specs=[SMEM] + [VMEM] * 5 + [ANY],
+        moved=4 * 10**5,
+        vmem=4,
+    )
+    first_message = trade(*first_message)
     d1, q, inverse, f, *edges = call(
-        functools.partial(step_kernel, True),
+        first_step_kernel,
         "first_step",
         [field, field, one, field] + faces(2),
-        (flags, f, *received, d, q, s1, wm, mass),
-        specs=specs,
+        (flags, f, *beside, *first_message, d, q, s1, wm, mass),
+        specs=[SMEM] + [VMEM] * 10,
         flops=10**8,
     )
-    s2, order = source(2, edges[2])
-    received = exchange(edges, order)
+    s2, unused = source(2, edges[0])
+    beside = swap(*edges, "lat")
+    d2, q, *second_message = call(
+        advance_kernel,
+        "advance",
+        [field, field] + [(2, 20, 8, 128)] * 2,
+        (flags, f, *beside, d1, q, inverse, s2),
+        specs=[SMEM] + [VMEM] * 7,
+        flops=10**7,
+    )
+    second_message = trade(*second_message)
     d2, q, f, *edges = call(
-        functools.partial(step_kernel, False),
+        second_step_kernel,
         "second_step",
         [field, field, field] + faces(2),
-        (flags, f, *received, d1, q, s2, wm, inverse),
-        specs=specs,
+        (flags, *second_message, *first_message, d2, q, inverse, s2, wm),
+        specs=[SMEM] + [VMEM] * 9,
         flops=10**8,
     )
     kernel, order = call(
         term_kernel, "term", [(5, 40, 640), token], (d1, d2, forward, wm), [tiles, wide, tiles], flops=10**8
     )
-    received = exchange(edges, order)
+    beside = swap(*edges, "lat")
     (velocity,) = call(
-        last_kernel, "last", [(2, 5, 40, 640)], (flags, f, *received, q, inverse), [wide], [SMEM] + [VMEM] * 7
+        last_kernel,
+        "last",
+        [(2, 5, 40, 640)],
+        (flags, f, *beside, q, inverse, order),
+        [wide],
+        [SMEM] + [VMEM] * 5 + [ANY],
     )
     return velocity.reshape(native), kernel.reshape(kernel_shape)
 

time: 89.5 us -> 86.5 us (0.966)
  waiting for transfers between devices: 21.9 us -> 19.3 us
    ppermute x6 -> x4, waiting for transfers between devices: 13.6 us -> 11 us  [trade(): return (lax.ppermute(even, 'lon', pairs), lax.ppermute(odd, 'lon', between))]
    ppermute x6 -> x4, starting transfers between devices: 3.91 us -> 3.24 us  [trade(): return (lax.ppermute(even, 'lon', pairs), lax.ppermute(odd, 'lon', between))]
    pallas_call x12 -> x11, Pallas kernels: 34.2 us -> 34.6 us  [call(): pl.pallas_call(kernel, name=name, out_shape=[s if hasattr(s, 'dtype') els...]
  transfers between devices with their start and end apart: 13 -> 11, of which waited for: 7 -> 5; matrix products, arithmetic and copies ran while one was open for 0% -> 0% of each run, Pallas kernels for 20% -> 22%
where the time goes in v3:
time: 86.5 us; the launch traced here: 86.3 us
  Pallas kernels  34.6 us (40%)
  starting transfers between devices  31.5 us (36%)
  waiting for transfers between devices  19.3 us (22%)
    pallas_call x11, Pallas kernels, call(): pl.pallas_call(kernel, name=name, out_shape=[s if hasattr(s, 'dtype') els...  34.6 us
    ppermute x6, starting transfers between devices, swap(): return (lax.ppermute(high, axis, up), lax.ppermute(low, axis, down))  17.1 us
    all_to_all x1, starting transfers between devices, on_device(): lax.all_to_all(packed.reshape(devices, 2, 128), ('lat', 'lon'), 0, 0, til...  11.1 us
    ppermute x4, waiting for transfers between devices, trade(): return (lax.ppermute(even, 'lon', pairs), lax.ppermute(odd, 'lon', between))  11 us
    all_to_all x1, waiting for transfers between devices, on_device(): lax.all_to_all(packed.reshape(devices, 2, 128), ('lat', 'lon'), 0, 0, til...  5.16 us
    ppermute x4, starting transfers between devices, trade(): return (lax.ppermute(even, 'lon', pairs), lax.ppermute(odd, 'lon', between))  3.24 us
    ppermute x6, waiting for transfers between devices, swap(): return (lax.ppermute(high, axis, up), lax.ppermute(low, axis, down))  3.09 us
  transfers between devices with their start and end apart: 11, of which 5 were waited for; matrix products, arithmetic and copies ran while one was open for 0% of the time, Pallas kernels for 22%

profile of v3, /device:TPU:0, one launch (start us, length us, event | category | flops | bytes accessed | tf_op | source)
XLA Modules:
  0.0 86.3 jit_solution(12369875653764143560)
XLA Ops:
  0.6 0.0 copy-start.1
  0.6 2.3 %pack.1 = f32[256,128]{1,0:T(8,128)} custom-call(f32[3,2,1024]{2,1,0:T(2,128)} %bitcast.29, s32[1,1024]{1,0:T(1,128)} %bitcast.30, s32[1,1024]{1,0:T(1,128)} %bitcast.31), custom_call_target="tpu_custom_call" | custom-call | flops 1000000 | bytes 4000000 | tf_op jit(solution)/shard_map/pack/pallas_call | solution.py:615
  2.9 11.1 %all-to-all-start = ((f32[128,2,128]{2,1,0:T(2,128)}), f32[128,2,128]{2,1,0:T(2,128)S(1)}, u32[]{:S(2)}, u32[]{:S(2)}) async-start(f32[128,2,128]{2,1,0:T(2,128)} %bitcast.26), calls=%async_computation | async-start | bytes 262144 | tf_op jit(solution)/shard_map/all_to_all | solution.py:669
  14.1 0.1 stack.23
  14.2 4.1 %start.1 = (f32[2,125,8,128]{3,2,1,0:T(8,128)}, f32[2,125,8,128]{3,2,1,0:T(8,128)}, f32[125,8,128]{2,1,0:T(8,128)}, f32[125,8,128]{2,1,0:T(8,128)}, f32[2,25,8,128]{3,2,1,0:T(8,128)}, /*index=5*/f32[12288,8,128]{2,1,0:T(8,128)}) custom-call(f32[2,5,40,640]{3,2,1,0:T(8,128)} %bitcast.23, f32[2,5,40,640]{3,2,1,0:T(8,128)} %bitcast.24, ...), custom_call_target="tpu_custom_call" | custom-call | flops 100000000 | bytes 4000000 | tf_op jit(solution)/shard_map/start/pallas_call | solution.py:615
  18.3 0.0 copy-start.5
  18.3 0.0 copy-start
  18.3 0.0 copy-start.2
  18.3 0.0 copy-start.4
  18.3 5.2 %all-to-all-done = f32[128,2,128]{2,1,0:T(2,128)S(1)} async-done(((f32[128,2,128]{2,1,0:T(2,128)}), f32[128,2,128]{2,1,0:T(2,128)S(1)}, u32[]{:S(2)}, u32[]{:S(2)}) %all-to-all-start) | async-done | bytes 131104 | tf_op jit(solution)/shard_map/all_to_all | solution.py:669
  23.5 0.0 copy-start.3
  23.5 5.1 %first_force.1 = (f32[2,125,8,128]{3,2,1,0:T(8,128)S(1)}, f32[3,18,8,128]{3,2,1,0:T(8,128)S(1)}, f32[3,18,8,128]{3,2,1,0:T(8,128)S(1)}, f32[3,5,8,128]{3,2,1,0:T(8,128)S(1)}, f32[3,5,8,128]{3,2,1,0:T(8,128)S(1)}) custom-call(f32[256,128]{1,0:T(8,128)S(1)} %bitcast.20, f32[12288,8,128]{2,1,0:T(8,128)} %get-tuple-element.35.kept), custom_call_target="tpu_custom_call" | custom-call | flops 4000000000 | bytes 4000000 | tf_op jit(solution)/shard_map/first_force/pallas_call | solution.py:615
  28.6 1.3 %collective-permute-start = (f32[3,18,8,128]{3,2,1,0:T(8,128)S(1)}, f32[3,18,8,128]{3,2,1,0:T(8,128)S(1)}, u32[]{:S(2)}, u32[]{:S(2)}) collective-permute-start(f32[3,18,8,128]{3,2,1,0:T(8,128)S(1)} %get-tuple-element.37), channel_id=1, source_target_pairs={{0,16},{16,32},{32,48},{48,64},{64,80},{80,96},{96,112},{112,0},{1... | collective-permute-start | bytes 663560 | tf_op jit(solution)/shard_map/ppermute | solution.py:632
  29.9 4.4 %collective-permute-start.1 = (f32[3,18,8,128]{3,2,1,0:T(8,128)S(1)}, f32[3,18,8,128]{3,2,1,0:T(8,128)S(1)}, u32[]{:S(2)}, u32[]{:S(2)}) collective-permute-start(f32[3,18,8,128]{3,2,1,0:T(8,128)S(1)} %get-tuple-element.38), channel_id=1, source_target_pairs={{16,0},{32,16},{48,32},{64,48},{80,64},{96,80},{112,96},{0,112},{1... | collective-permute-start | bytes 663560 | tf_op jit(solution)/shard_map/ppermute | solution.py:632
  34.4 4.8 %source.2 = (f32[2,128,8,128]{3,2,1,0:T(8,128)S(1)}, f32[8,128]{1,0:T(8,128)S(1)}) custom-call(f32[256,128]{1,0:T(8,128)S(1)} %bitcast.21, f32[3,5,8,128]{3,2,1,0:T(8,128)S(1)} %get-tuple-element.39.order.row_low), custom_call_target="tpu_custom_call" | custom-call | flops 4000000000 | bytes 4000000 | tf_op jit(solution)/shard_map/source/pallas_call | solution.py:615
  39.2 1.5 %collective-permute-done.from_below.below = f32[3,18,8,128]{3,2,1,0:T(8,128)S(1)} collective-permute-done((f32[3,18,8,128]{3,2,1,0:T(8,128)S(1)}, f32[3,18,8,128]{3,2,1,0:T(8,128)S(1)}, u32[]{:S(2)}, u32[]{:S(2)}) %collective-permute-start) | collective-permute-done | bytes 221216 | tf_op jit(solution)/shard_map/ppermute | solution.py:632
  40.6 1.6 %collective-permute-done.1.from_above.above = f32[3,18,8,128]{3,2,1,0:T(8,128)S(1)} collective-permute-done((f32[3,18,8,128]{3,2,1,0:T(8,128)S(1)}, f32[3,18,8,128]{3,2,1,0:T(8,128)S(1)}, u32[]{:S(2)}, u32[]{:S(2)}) %collective-permute-start.1) | collective-permute-done | bytes 221216 | tf_op jit(solution)/shard_map/ppermute | solution.py:632
  42.2 0.0 copy-done.5
  42.2 0.6 rows.1
  42.8 0.1 collective-permute-start.2
  42.9 1.7 %collective-permute-start.3 = (f32[40,8,128]{2,1,0:T(8,128)S(1)}, f32[40,8,128]{2,1,0:T(8,128)S(1)}, u32[]{:S(2)}, u32[]{:S(2)}) collective-permute-start(f32[40,8,128]{2,1,0:T(8,128)S(1)} %get-tuple-element.44), channel_id=1, source_target_pairs={{0,15},{1,2},{2,1},{3,4},{4,3},{5,6},{6,5},{7,8},{8,7},{9,10},{10,... | collective-permute-start | bytes 491528 | tf_op jit(solution)/shard_map/ppermute | solution.py:725
  44.6 0.0 collective-permute-done.2.even.wm_even
  44.6 5.2 %collective-permute-done.3.odd.wm_odd = f32[40,8,128]{2,1,0:T(8,128)S(1)} collective-permute-done((f32[40,8,128]{2,1,0:T(8,128)S(1)}, f32[40,8,128]{2,1,0:T(8,128)S(1)}, u32[]{:S(2)}, u32[]{:S(2)}) %collective-permute-start.3) | collective-permute-done | bytes 163872 | tf_op jit(solution)/shard_map/ppermute | solution.py:725
  49.9 0.0 copy-done
  49.9 0.0 copy-done.2
  49.9 0.0 copy-done.4
  49.9 0.0 copy-done.3
  49.9 2.5 %first_step.1 = (f32[2,125,8,128]{3,2,1,0:T(8,128)S(1)}, f32[2,125,8,128]{3,2,1,0:T(8,128)S(1)}, f32[125,8,128]{2,1,0:T(8,128)S(1)}, f32[2,125,8,128]{3,2,1,0:T(...) custom-call(s32[5]{0:T(128)S(1)} %convert_element_type.3.flags, ...), custom_call_target="tpu_custom_call" | custom-call | flops 100000000 | bytes 4000000 | tf_op jit(solution)/shard_map/first_step/pallas_call | solution.py:615
  52.4 1.7 %collective-permute-start.4 = (f32[2,18,8,128]{3,2,1,0:T(8,128)S(1)}, f32[2,18,8,128]{3,2,1,0:T(8,128)S(1)}, u32[]{:S(2)}, u32[]{:S(2)}) collective-permute-start(f32[2,18,8,128]{3,2,1,0:T(8,128)S(1)} %get-tuple-element.51), channel_id=1, source_target_pairs={{0,16},{16,32},{32,48},{48,64},{64,80},{80,96},{96,112},{112,0},{1... | collective-permute-start | bytes 442376 | tf_op jit(solution)/shard_map/ppermute | solution.py:632
  54.1 4.0 %collective-permute-start.5 = (f32[2,18,8,128]{3,2,1,0:T(8,128)S(1)}, f32[2,18,8,128]{3,2,1,0:T(8,128)S(1)}, u32[]{:S(2)}, u32[]{:S(2)}) collective-permute-start(f32[2,18,8,128]{3,2,1,0:T(8,128)S(1)} %get-tuple-element.52.order), channel_id=1, source_target_pairs={{16,0},{32,16},{48,32},{64,48},{80,64},{96,80},{112,96},{0,112},{1... | collective-permute-start | bytes 442376 | tf_op jit(solution)/shard_map/ppermute | solution.py:632
  58.1 5.3 %source.3 = (f32[2,128,8,128]{3,2,1,0:T(8,128)S(1)}, f32[8,128]{1,0:T(8,128)}) custom-call(f32[256,128]{1,0:T(8,128)S(1)} %bitcast.22, f32[2,18,8,128]{3,2,1,0:T(8,128)S(1)} %get-tuple-element.52.order), custom_call_target="tpu_custom_call" | custom-call | flops 4000000000 | bytes 4000000 | tf_op jit(solution)/shard_map/source/pallas_call | solution.py:615
  63.4 0.0 collective-permute-done.4.below
  63.4 0.0 collective-permute-done.5.above
  63.4 1.0 %advance.1 = (f32[2,125,8,128]{3,2,1,0:T(8,128)S(1)}, f32[2,125,8,128]{3,2,1,0:T(8,128)S(1)}, f32[2,20,8,128]{3,2,1,0:T(8,128)S(1)}, f32[2,20,8,128]{3,2,1,0:T(8,128)S(1)}) custom-call(s32[5]{0:T(128)S(1)} %convert_element_type.3.flags, f32[2,125,8,128]{3,2,1,0:T(8,128)S(1)} %get-tuple-element.50.f, f32[2,18,8,128]{3,2,1,0:T(8,128)S(1)} %collective-permute-done.4.below, ...), custom_call_target="tpu_custom_call" | custom-call | flops 10000000 | bytes 4000000 | tf_op jit(solution)/shard_map/advance/pallas_call | solution.py:615
  64.4 0.1 collective-permute-start.6
  64.5 1.4 %collective-permute-start.7 = (f32[2,20,8,128]{3,2,1,0:T(8,128)S(1)}, f32[2,20,8,128]{3,2,1,0:T(8,128)S(1)}, u32[]{:S(2)}, u32[]{:S(2)}) collective-permute-start(f32[2,20,8,128]{3,2,1,0:T(8,128)S(1)} %get-tuple-element.58), channel_id=1, source_target_pairs={{0,15},{1,2},{2,1},{3,4},{4,3},{5,6},{6,5},{7,8},{8,7},{9,10},{10,... | collective-permute-start | bytes 491528 | tf_op jit(solution)/shard_map/ppermute | solution.py:725
  65.9 0.0 collective-permute-done.6.even
  65.9 5.8 %collective-permute-done.7.odd = f32[2,20,8,128]{3,2,1,0:T(8,128)S(1)} collective-permute-done((f32[2,20,8,128]{3,2,1,0:T(8,128)S(1)}, f32[2,20,8,128]{3,2,1,0:T(8,128)S(1)}, u32[]{:S(2)}, u32[]{:S(2)}) %collective-permute-start.7) | collective-permute-done | bytes 163872 | tf_op jit(solution)/shard_map/ppermute | solution.py:725
  71.7 2.6 %second_step.1 = (f32[2,125,8,128]{3,2,1,0:T(8,128)S(1)}, f32[2,125,8,128]{3,2,1,0:T(8,128)S(1)}, f32[2,125,8,128]{3,2,1,0:T(8,128)S(1)}, f32[2,18,8,128]{3,2,1,0:T(8,128)S(1)}, f32[2,18,8,128]{3,2,1,0:T(8,128)S(1)}) custom-call(s32[5]{0:T(128)S(1)} %convert_element_type.3.flags, f32[2,20,8,128]{3,2,1,0:T(8,128)S(1)} %collective-permute-done.6.even, ...), custom_call_target="tpu_custom_call" | custom-call | flops 100000000 | bytes 4000000 | tf_op jit(solution)/shard_map/second_step/pallas_call | solution.py:615
  74.3 0.6 collective-permute-start.8
  74.9 5.1 %collective-permute-start.9 = (f32[2,18,8,128]{3,2,1,0:T(8,128)S(1)}, f32[2,18,8,128]{3,2,1,0:T(8,128)S(1)}, u32[]{:S(2)}, u32[]{:S(2)}) collective-permute-start(f32[2,18,8,128]{3,2,1,0:T(8,128)S(1)} %get-tuple-element.63), channel_id=1, source_target_pairs={{16,0},{32,16},{48,32},{64,48},{80,64},{96,80},{112,96},{0,112},{1... | collective-permute-start | bytes 442376 | tf_op jit(solution)/shard_map/ppermute | solution.py:632
  80.0 0.0 copy-done.1
  80.0 4.5 %term.1 = (f32[5,40,640]{2,1,0:T(8,128)}, f32[8,128]{1,0:T(8,128)S(1)}) custom-call(f32[2,125,8,128]{3,2,1,0:T(8,128)S(1)} %get-tuple-element.53.d.d1, f32[2,125,8,128]{3,2,1,0:T(8,128)S(1)} %get-tuple-element.65.d2, bf16[2,2,5,40,640]{4,3,2,1,0:T(8,128)(2,1)S(1)} %bitcast.19, f32[125,8,128]{2,1,0:T(8,128)S(1)} %copy-done), custom_call_target="tpu_custom_call" | custom-call | flops 100000000 | bytes 4000000 | tf_op jit(solution)/shard_map/term/pallas_call | solution.py:615
  84.5 0.0 collective-permute-done.8.below
  84.5 0.0 collective-permute-done.9.above
  84.5 1.9 %last.1 = f32[2,5,40,640]{3,2,1,0:T(8,128)} custom-call(s32[5]{0:T(128)S(1)} %convert_element_type.3.flags, f32[2,125,8,128]{3,2,1,0:T(8,128)S(1)} %get-tuple-element.61.f, f32[2,18,8,128]{3,2,1,0:T(8,128)S(1)} %collective-permute-done.8.below, f32[2,18,8,128]{3,2,1,0:T(8,128)S(1)} %collective-permute-done.9.above, ...), custom_call_target="tpu_custom_call" | custom-call | flops 1000000 | bytes 4000000 | tf_op jit(solution)/shard_map/last/pallas_call | solution.py:615
  (1 shorter events, 0.0 us)
Async XLA Ops:
  0.6 79.4 %copy-start.1 = (bf16[2,2,1,5,40,640]{5,4,3,2,1,0:T(8,128)(2,1)S(1)}, bf16[2,2,1,5,40,640]{5,4,3,2,1,0:T(8,128)(2,1)}, u32[]{:S(2)}) copy-start(bf16[2,2,1,5,40,640]{5,4,3,2,1,0:T(8,128)(2,1)} %param.12) | copy-start | bytes 3072004
  2.9 20.6 %all-to-all-start = ((f32[128,2,128]{2,1,0:T(2,128)}), f32[128,2,128]{2,1,0:T(2,128)S(1)}, u32[]{:S(2)}, u32[]{:S(2)}) async-start(f32[128,2,128]{2,1,0:T(2,128)} %bitcast.26), calls=%async_computation | async-start | bytes 262144 | tf_op jit(solution)/shard_map/all_to_all | solution.py:669
  18.3 24.0 %copy-start.5 = (f32[2,25,8,128]{3,2,1,0:T(8,128)S(1)}, f32[2,25,8,128]{3,2,1,0:T(8,128)}, u32[]{:S(2)}) copy-start(f32[2,25,8,128]{3,2,1,0:T(8,128)} %get-tuple-element.41.wm_rim) | copy-start | bytes 614404
  18.3 31.6 %copy-start = (f32[125,8,128]{2,1,0:T(8,128)S(1)}, f32[125,8,128]{2,1,0:T(8,128)}, u32[]{:S(2)}) copy-start(f32[125,8,128]{2,1,0:T(8,128)} %get-tuple-element.48.wm) | copy-start | bytes 1536004
  18.3 31.6 %copy-start.2 = (f32[2,125,8,128]{3,2,1,0:T(8,128)S(1)}, f32[2,125,8,128]{3,2,1,0:T(8,128)}, u32[]{:S(2)}) copy-start(f32[2,125,8,128]{3,2,1,0:T(8,128)} %get-tuple-element.45.d) | copy-start | bytes 3072004
  18.3 31.5 %copy-start.4 = (f32[125,8,128]{2,1,0:T(8,128)S(1)}, f32[125,8,128]{2,1,0:T(8,128)}, u32[]{:S(2)}) copy-start(f32[125,8,128]{2,1,0:T(8,128)} %get-tuple-element.49.mass) | copy-start | bytes 1536004
  23.5 26.4 %copy-start.3 = (f32[2,125,8,128]{3,2,1,0:T(8,128)S(1)}, f32[2,125,8,128]{3,2,1,0:T(8,128)}, u32[]{:S(2)}) copy-start(f32[2,125,8,128]{3,2,1,0:T(8,128)} %get-tuple-element.46.q) | copy-start | bytes 3072004
  28.6 12.0 %collective-permute-start = (f32[3,18,8,128]{3,2,1,0:T(8,128)S(1)}, f32[3,18,8,128]{3,2,1,0:T(8,128)S(1)}, u32[]{:S(2)}, u32[]{:S(2)}) collective-permute-start(f32[3,18,8,128]{3,2,1,0:T(8,128)S(1)} %get-tuple-element.37), channel_id=1, source_target_pairs={{0,16},{16,32},{32,48},{48,64},{64,80},{80,96},{96,112},{112,0},{1... | collective-permute-start | bytes 663560 | tf_op jit(solution)/shard_map/ppermute | solution.py:632
  29.9 12.3 %collective-permute-start.1 = (f32[3,18,8,128]{3,2,1,0:T(8,128)S(1)}, f32[3,18,8,128]{3,2,1,0:T(8,128)S(1)}, u32[]{:S(2)}, u32[]{:S(2)}) collective-permute-start(f32[3,18,8,128]{3,2,1,0:T(8,128)S(1)} %get-tuple-element.38), channel_id=1, source_target_pairs={{16,0},{32,16},{48,32},{64,48},{80,64},{96,80},{112,96},{0,112},{1... | collective-permute-start | bytes 663560 | tf_op jit(solution)/shard_map/ppermute | solution.py:632
  42.8 1.8 %collective-permute-start.2 = (f32[40,8,128]{2,1,0:T(8,128)S(1)}, f32[40,8,128]{2,1,0:T(8,128)S(1)}, u32[]{:S(2)}, u32[]{:S(2)}) collective-permute-start(f32[40,8,128]{2,1,0:T(8,128)S(1)} %get-tuple-element.43), channel_id=1, source_target_pairs={{0,1},{1,0},{2,3},{3,2},{4,5},{5,4},{6,7},{7,6},{8,9},{9,8},{10,11... | collective-permute-start | bytes 491528 | tf_op jit(solution)/shard_map/ppermute | solution.py:725
  42.9 6.9 %collective-permute-start.3 = (f32[40,8,128]{2,1,0:T(8,128)S(1)}, f32[40,8,128]{2,1,0:T(8,128)S(1)}, u32[]{:S(2)}, u32[]{:S(2)}) collective-permute-start(f32[40,8,128]{2,1,0:T(8,128)S(1)} %get-tuple-element.44), channel_id=1, source_target_pairs={{0,15},{1,2},{2,1},{3,4},{4,3},{5,6},{6,5},{7,8},{8,7},{9,10},{10,... | collective-permute-start | bytes 491528 | tf_op jit(solution)/shard_map/ppermute | solution.py:725
  52.4 11.0 %collective-permute-start.4 = (f32[2,18,8,128]{3,2,1,0:T(8,128)S(1)}, f32[2,18,8,128]{3,2,1,0:T(8,128)S(1)}, u32[]{:S(2)}, u32[]{:S(2)}) collective-permute-start(f32[2,18,8,128]{3,2,1,0:T(8,128)S(1)} %get-tuple-element.51), channel_id=1, source_target_pairs={{0,16},{16,32},{32,48},{48,64},{64,80},{80,96},{96,112},{112,0},{1... | collective-permute-start | bytes 442376 | tf_op jit(solution)/shard_map/ppermute | solution.py:632
  54.1 9.3 %collective-permute-start.5 = (f32[2,18,8,128]{3,2,1,0:T(8,128)S(1)}, f32[2,18,8,128]{3,2,1,0:T(8,128)S(1)}, u32[]{:S(2)}, u32[]{:S(2)}) collective-permute-start(f32[2,18,8,128]{3,2,1,0:T(8,128)S(1)} %get-tuple-element.52.order), channel_id=1, source_target_pairs={{16,0},{32,16},{48,32},{64,48},{80,64},{96,80},{112,96},{0,112},{1... | collective-permute-start | bytes 442376 | tf_op jit(solution)/shard_map/ppermute | solution.py:632
  64.4 1.5 %collective-permute-start.6 = (f32[2,20,8,128]{3,2,1,0:T(8,128)S(1)}, f32[2,20,8,128]{3,2,1,0:T(8,128)S(1)}, u32[]{:S(2)}, u32[]{:S(2)}) collective-permute-start(f32[2,20,8,128]{3,2,1,0:T(8,128)S(1)} %get-tuple-element.57), channel_id=1, source_target_pairs={{0,1},{1,0},{2,3},{3,2},{4,5},{5,4},{6,7},{7,6},{8,9},{9,8},{10,11... | collective-permute-start | bytes 491528 | tf_op jit(solution)/shard_map/ppermute | solution.py:725
  64.5 7.2 %collective-permute-start.7 = (f32[2,20,8,128]{3,2,1,0:T(8,128)S(1)}, f32[2,20,8,128]{3,2,1,0:T(8,128)S(1)}, u32[]{:S(2)}, u32[]{:S(2)}) collective-permute-start(f32[2,20,8,128]{3,2,1,0:T(8,128)S(1)} %get-tuple-element.58), channel_id=1, source_target_pairs={{0,15},{1,2},{2,1},{3,4},{4,3},{5,6},{6,5},{7,8},{8,7},{9,10},{10,... | collective-permute-start | bytes 491528 | tf_op jit(solution)/shard_map/ppermute | solution.py:725
  74.3 10.2 %collective-permute-start.8 = (f32[2,18,8,128]{3,2,1,0:T(8,128)S(1)}, f32[2,18,8,128]{3,2,1,0:T(8,128)S(1)}, u32[]{:S(2)}, u32[]{:S(2)}) collective-permute-start(f32[2,18,8,128]{3,2,1,0:T(8,128)S(1)} %get-tuple-element.62), channel_id=1, source_target_pairs={{0,16},{16,32},{32,48},{48,64},{64,80},{80,96},{96,112},{112,0},{1... | collective-permute-start | bytes 442376 | tf_op jit(solution)/shard_map/ppermute | solution.py:632
  74.9 9.5 %collective-permute-start.9 = (f32[2,18,8,128]{3,2,1,0:T(8,128)S(1)}, f32[2,18,8,128]{3,2,1,0:T(8,128)S(1)}, u32[]{:S(2)}, u32[]{:S(2)}) collective-permute-start(f32[2,18,8,128]{3,2,1,0:T(8,128)S(1)} %get-tuple-element.63), channel_id=1, source_target_pairs={{16,0},{32,16},{48,32},{64,48},{80,64},{96,80},{112,96},{0,112},{1... | collective-permute-start | bytes 442376 | tf_op jit(solution)/shard_map/ppermute | solution.py:632

commit v4 on v3

--- a/solution.py
+++ b/solution.py
@@ -112,9 +112,20 @@
             put_plane(i, k, wide[i, k])
 
 
-def force(d, f, e, wm, source):
+def edge_slot(n):
+    return n // 25 * 10 + (5 if n // 5 % 5 else 0) + n % 5
+
+
+def patched(base, edge, *lead):
+    def get(n):
+        return edge[lead + (edge_slot(n),)] if n // 5 % 5 in (0, 4) else base[lead + (n,)]
+
+    return get
+
+
+def force(get, f, e, wm, source):
     def line(index, before):
-        g = apply5(derivative, [d[e, n] for n in index])
+        g = apply5(derivative, [get(n) for n in index])
         r = apply5(transposed, [g[a] * wm[index[a]] for a in range(5)])
         for a in range(5):
             f[e, index[a]] = before(index[a]) - r[a]
@@ -161,7 +172,7 @@
         row_high[lead + (i,)] = high
 
 
-def complete(get, i, c, flags, from_below, from_above, left=None, right=None):
+def complete(get, i, c, flags, from_below, from_above):
     sub, ln = sublane(), lane()
     v = [[get(at(i, j, k)) for k in range(5)] for j in range(5)]
     if i in (0, 4):
@@ -175,10 +186,6 @@
             v[4][k] = v[4][k] + jnp.where((sub == 7) & keep, row_of(last_row, k), 0.0)
         for j in range(4):
             v[j][4] = v[j][4] + jnp.where((ln == 127) & keep, column_of(last_column, j), 0.0)
-    if left is not None:
-        for k in range(5):
-            v[0][k] = v[0][k] + jnp.where((sub == 0) & (flags[2] > 0), row_of(left, k), 0.0)
-            v[4][k] = v[4][k] + jnp.where((sub == 7) & (flags[3] > 0), row_of(right, k), 0.0)
     for k in range(5):
         v[4][k] = jnp.where(sub == 7, v[4][k], pltpu.roll(v[0][k], 7, 0))
     for j in range(5):
@@ -342,7 +349,7 @@
         loads[1 + e].wait()
         to_tiles(lambda i, e=e: d0[e, i], put_d, wide)
         copy(d.at[e], d_out.at[e])
-        force(d, kd, e, wm, lambda n: 0.0)
+        force(lambda n, e=e: d[e, n], kd, e, wm, lambda n: 0.0)
         copy(kd.at[e], kept.at[e * points : e * points + points])
     loads[3].wait()
     to_tiles(lambda i: density[i].astype(f32), weighted(mass), wide)
@@ -410,8 +417,10 @@
     scatter(first[64:96], values, *scratch, store)
 
 
-def rows_kernel(flags, from_below, from_above, row_low, row_high, wm_rim, order, even_out, odd_out):
+def rows_kernel(flags, from_below, from_above, row_low, row_high, wm_rim, order, even_out, odd_out, own):
     sub, ln = sublane(), lane()
+    low_tiles = [wm_rim[0, n] for n in range(25)]
+    high_tiles = [wm_rim[1, n] for n in range(25)]
     for c in range(row_low.shape[0]):
         for i in range(5):
             low, high = row_low[c, i], row_high[c, i]
@@ -423,51 +432,131 @@
                 extra = jnp.where((sub == 4) & (ln == 127), corner, extra)
                 low = low + jnp.where(keep, extra, 0.0)
                 high = high + jnp.where(keep, face[c, 16], 0.0)
-            send_sides(flags, even_out, odd_out, c * 5 + i, low, high)
+            shared = (sub == 4) & (ln < 127)
+            low = jnp.where(shared, pltpu.roll(row_of(low, 0), 127, 1), low)
+            high = jnp.where(shared, pltpu.roll(row_of(high, 0), 127, 1), high)
+            own[0, c * 5 + i] = low
+            own[1, c * 5 + i] = high
+            for k in range(5):
+                tile, where = packed_row(c, i, k)
+                low_tiles[tile] = jnp.where(sub == where, row_of(low, k), low_tiles[tile])
+                high_tiles[tile] = jnp.where(sub == where, row_of(high, k), high_tiles[tile])
     for n in range(25):
-        send_sides(flags, even_out, odd_out, 15 + n, wm_rim[0, n], wm_rim[1, n])
-
-
-def first_step_kernel(flags, f, below, above, even, odd, d, q, source, wm, mass, *refs):
-    d_out, q_out, inverse, f_out, face_low, face_high = refs
+        send_sides(flags, even_out, odd_out, n, low_tiles[n], high_tiles[n])
+
+
+def packed_row(c, i, k):
+    row = (c * 5 + i) * 5 + k
+    return row // 3, 5 + row % 3
+
+
+def first_guess_kernel(flags, f, below, above, d, q, source, wm, mass, order, d_out, q_out, inverse, f_out):
     for i in range(5):
-        v = complete(lambda n: mass[n], i, 2, flags, below, above, *sides(flags, even, odd, 10 + i))
+        v = complete(lambda n: mass[n], i, 2, flags, below, above)
         for j in range(5):
             for k in range(5):
                 inverse[at(i, j, k)] = 1.0 / v[j][k]
 
     def event(e, carry):
         for i in range(5):
-            v = complete(lambda n: f[e, n], i, e, flags, below, above, *sides(flags, even, odd, e * 5 + i))
+            v = complete(lambda n: f[e, n], i, e, flags, below, above)
             for j in range(5):
                 for k in range(5):
                     n = at(i, j, k)
                     q_new = q[e, n] + 0.5 * time_step * (v[j][k] * inverse[n])
                     q_out[e, n] = q_new
                     d_out[e, n] = d[e, n] + time_step * q_new
-        force(d_out, f_out, e, wm, lambda n: source[e, n])
-
-        def put(n, value):
-            f_out[e, n] = value
-
-        fold(lambda n: f_out[e, n], put)
-        emit_faces(lambda n: f_out[e, n], e, face_low, face_high)
+        force(lambda n: d_out[e, n], f_out, e, wm, lambda n: source[e, n])
         return carry
 
     lax.fori_loop(0, 2, event, 0)
 
 
-def advance_kernel(flags, f, below, above, d, q, inverse, source, d_out, q_out, even_out, odd_out):
+def add_row(tile, edge, rows, k):
+    return tile + jnp.where(sublane() == edge, row_of(rows, k), 0.0)
+
+
+def row_change_force(change, wm, row):
+    out = [[None] * 5 for _ in range(5)]
+    gx = apply5(derivative, change)
+    rx = apply5(transposed, [gx[i] * wm[i][row] for i in range(5)])
+    for i in range(5):
+        out[i] = apply5(transposed, [float(derivative[b, row]) * change[i] * wm[i][b] for b in range(5)])
+        gz = along_sublanes(derivative, change[i])
+        out[i][row] = out[i][row] + rx[i] + along_sublanes(transposed, gz * wm[i][row])
+    return out
+
+
+def fold_with_rims(f, e, change, f_out, face_low, face_high):
+    sub = sublane()
+
+    def get(n):
+        i, j, k = n // 25, n // 5 % 5, n % 5
+        both = jnp.where(sub == 0, row_of(change[0, i * 5 + j], k), 0.0)
+        return f[e, n] - jnp.where(sub == 7, row_of(change[1, i * 5 + j], k), both)
+
+    def put(n, value):
+        f_out[e, n] = value
+
+    fold(get, put, every=True)
+    emit_faces(lambda n: f_out[e, n], e, face_low, face_high)
+
+
+def first_fix_kernel(flags, even, odd, own, wm_rim, d, q, inverse, f, *refs):
+    d_edge, q_edge, inverse_edge, inverse_rim, f_out, face_low, face_high, change = refs
+    sub = sublane()
+    message = [sides(flags, even, odd, n) for n in range(25)]
+
+    def received(side, c, i):
+        tile = jnp.zeros((8, 128), f32)
+        for k in range(5):
+            n, where = packed_row(c, i, k)
+            tile = jnp.where(sub == k, row_of(message[n][side], where), tile)
+        return jnp.where(flags[2 + side] > 0, tile, 0.0)
+
+    for side in range(2):
+        for i in range(5):
+            mass = jnp.where(sub < 5, own[side, 10 + i] + received(side, 2, i), 1.0)
+            inverse_rim[side, i] = 1.0 / mass
+            for k in range(5):
+                n = at(i, 4 * side, k)
+                inverse_edge[edge_slot(n)] = jnp.where(sub == 7 * side, row_of(inverse_rim[side, i], k), inverse[n])
+    for e in range(2):
+        for side in range(2):
+            shift = []
+            for i in range(5):
+                mine = own[side, e * 5 + i]
+                before = mine * (1.0 / jnp.where(sub < 5, own[side, 10 + i], 1.0))
+                after = (mine + received(side, e, i)) * inverse_rim[side, i]
+                q_change = 0.5 * time_step * (after - before)
+                shift.append(time_step * q_change)
+                for k in range(5):
+                    n = at(i, 4 * side, k)
+                    q_edge[e, edge_slot(n)] = add_row(q[e, n], 7 * side, q_change, k)
+                    d_edge[e, edge_slot(n)] = add_row(d[e, n], 7 * side, shift[i], k)
+            w = [[wm_rim[side, i * 5 + j] for j in range(5)] for i in range(5)]
+            r = row_change_force(shift, w, 4 * side)
+            for i in range(5):
+                for j in range(5):
+                    change[side, i * 5 + j] = r[i][j]
+        fold_with_rims(f, e, change, f_out, face_low, face_high)
+
+
+def advance_kernel(flags, f, below, above, d, d_edge, q, q_edge, inverse, inverse_edge, source, *refs):
+    d_out, q_out, even_out, odd_out = refs
+    get_inverse = patched(inverse, inverse_edge)
+
     def event(e, carry):
+        get_d, get_q = patched(d, d_edge, e), patched(q, q_edge, e)
         for i in range(5):
             v = complete(lambda n: f[e, n], i, e, flags, below, above)
             new = [[None] * 5 for _ in range(5)]
             for j in range(5):
                 for k in range(5):
                     n = at(i, j, k)
-                    q_new = q[e, n] + time_step * (v[j][k] * inverse[n])
+                    q_new = get_q(n) + time_step * (v[j][k] * get_inverse(n))
                     q_out[e, n] = q_new
-                    new[j][k] = d[e, n] + time_step * q_new
+                    new[j][k] = get_d(n) + time_step * q_new
                     d_out[e, n] = new[j][k]
             for m in range(4):
                 low = stack_rows([(new[m + 1][k], 0) for k in range(5)])
@@ -485,6 +574,14 @@
     lax.fori_loop(0, 2, event, 0)
 
 
+def second_guess_kernel(d, source, wm, order, f_out):
+    def event(e, carry):
+        force(lambda n: d[e, n], f_out, e, wm, lambda n: source[e, n])
+        return carry
+
+    lax.fori_loop(0, 2, event, 0)
+
+
 def along_sublanes(matrix, tile):
     sub = sublane()
     total = None
@@ -510,78 +607,76 @@
     return out
 
 
-def second_step_kernel(flags, even, odd, wm_even, wm_odd, d, q, inverse, source, wm, *refs):
-    d_out, q_out, f_out, face_low, face_high = refs
+def second_fix_kernel(flags, even, odd, wm_even, wm_odd, wm_rim, inverse_rim, d, q, f, order, *refs):
+    d_edge, q_edge, f_out, face_low, face_high, change = refs
     sub = sublane()
-
-    def event(e, carry):
-        for i in range(5):
-            message = [sides(flags, even, odd, e, i * 4 + m) for m in range(4)]
-            for j in range(5):
+    wm_sides = [sides(flags, wm_even, wm_odd, n) for n in range(25)]
+    for e in range(2):
+        for side in range(2):
+            keep = flags[2 + side] > 0
+            shared, shift, u, w, sources = [], [], [], [], []
+            for i in range(5):
+                m = [sides(flags, even, odd, e, i * 4 + n)[side] for n in range(4)]
+                forces = jnp.where(sub < 3, pltpu.roll(m[0], 3, 0), pltpu.roll(m[1], 6, 0))
+                sources.append(jnp.where(sub < 3, pltpu.roll(m[2], 3, 0), pltpu.roll(m[3], 6, 0)))
+                q_change = time_step * (jnp.where(keep & (sub < 5), forces, 0.0) * inverse_rim[side, i])
+                shift.append(time_step * q_change)
                 for k in range(5):
-                    n = at(i, j, k)
-                    d_new, q_new = d[e, n], q[e, n]
-                    if j in (0, 4):
-                        side = 0 if j == 0 else 1
-                        row = row_of(message[0][side], 5 + k) if k < 3 else row_of(message[1][side], 2 + k)
-                        mine = (sub == (0 if j == 0 else 7)) & (flags[2 + side] > 0)
-                        change = time_step * (jnp.where(mine, row, 0.0) * inverse[n])
-                        q_new = q_new + change
-                        d_new = d_new + time_step * change
-                    d_out[e, n] = d_new
-                    q_out[e, n] = q_new
-        force(d_out, f_out, e, wm, lambda n: source[e, n])
-        for side in range(2):
-            j, edge = (0, 0) if side == 0 else (4, 7)
-            near = 4 - j
-            u, w, message = [], [], []
+                    n = at(i, 4 * side, k)
+                    q_edge[e, edge_slot(n)] = add_row(q[e, n], 7 * side, q_change, k)
+                    d_edge[e, edge_slot(n)] = add_row(d[e, n], 7 * side, shift[i], k)
+                here = stack_rows([(d_edge[e, edge_slot(at(i, 4 * side, k))], 7 * side) for k in range(5)])
+                u.append([here] + m if side else m + [here])
+                w.append([wm_sides[i * 5 + j][side] for j in range(5)])
+            beyond = rim_force(u, w, 4 - 4 * side)
+            w = [[wm_rim[side, i * 5 + j] for j in range(5)] for i in range(5)]
+            r = row_change_force(shift, w, 4 * side)
             for i in range(5):
-                message.append([sides(flags, even, odd, e, i * 4 + m)[side] for m in range(4)])
-                shared = stack_rows([(d_out[e, at(i, j, k)], edge) for k in range(5)])
-                u.append(message[i] + [shared] if near == 4 else [shared] + message[i])
-                w.append([sides(flags, wm_even, wm_odd, 15 + i * 5 + m)[side] for m in range(5)])
-            r = rim_force(u, w, near)
-            mine = (sub == edge) & (flags[2 + side] > 0)
-            for i in range(5):
-                for k in range(5):
-                    row = row_of(message[i][2], 5 + k) if k < 3 else row_of(message[i][3], 2 + k)
-                    n = at(i, j, k)
-                    f_out[e, n] = f_out[e, n] + jnp.where(mine, row - row_of(r[i], k), 0.0)
-
-        def put(n, value):
-            f_out[e, n] = value
-
-        fold(lambda n: f_out[e, n], put)
-        emit_faces(lambda n: f_out[e, n], e, face_low, face_high)
-        return carry
-
-    lax.fori_loop(0, 2, event, 0)
-
-
-def last_kernel(flags, f, below, above, q, inverse, order, velocity, wide):
-    def event(e, carry):
-        for i in range(5):
+                r[i][4 * side] = r[i][4 * side] + jnp.where(keep, beyond[i] - sources[i], 0.0)
+                for j in range(5):
+                    change[side, i * 5 + j] = r[i][j]
+        fold_with_rims(f, e, change, f_out, face_low, face_high)
+
+
+def write_velocity(planes, flags, f, below, above, q, q_edge, inverse, inverse_edge, velocity, wide, rows, sems):
+    get_inverse = patched(inverse, inverse_edge)
+    copies = []
+    for e in range(2):
+        get_q = patched(q, q_edge, e)
+        for m, i in enumerate(planes):
             v = complete(lambda n: f[e, n], i, e, flags, below, above)
             for j in range(5):
                 for k in range(5):
                     n = at(i, j, k)
-                    wide[i, k, pl.ds(j, 8, stride=5), :] = q[e, n] + 0.5 * time_step * (v[j][k] * inverse[n])
+                    wide[i, k, pl.ds(j, 8, stride=5), :] = get_q(n) + 0.5 * time_step * (v[j][k] * get_inverse(n))
             for k in range(5):
-                velocity[e, i, :, k * 128 : (k + 1) * 128] = wide[i, k]
-        return carry
-
-    lax.fori_loop(0, 2, event, 0)
-
-
-def correlate(d, forward, step, total, wide, tiles):
+                rows[e, m, :, k * 128 : (k + 1) * 128] = wide[i, k]
+            copies.append(pltpu.make_async_copy(rows.at[e, m], velocity.at[e, i], sems.at[len(copies)]))
+            copies[-1].start()
+    for copy in copies:
+        copy.wait()
+
+
+def inner_velocity_kernel(f, q, q_edge, inverse, inverse_edge, order, velocity, token, *scratch):
+    token[...] = jnp.zeros_like(token)
+    write_velocity((1, 2, 3), None, f, None, None, q, q_edge, inverse, inverse_edge, velocity, *scratch)
+
+
+def outer_velocity_kernel(flags, f, below, above, q, q_edge, inverse, inverse_edge, inner, order, velocity, *scratch):
+    write_velocity((0, 4), flags, f, below, above, q, q_edge, inverse, inverse_edge, velocity, *scratch)
+
+
+def correlate(d, d_edge, forward, step, total, wide, tiles):
     def event(e, carry):
         def put(n, value):
             tiles[n] = value
 
         to_tiles(lambda i: forward[step, e, i].astype(f32), put, wide)
 
+        get_d = patched(d, d_edge, e)
+
         def line(index):
-            g = apply5(derivative, [d[e, n] for n in index])
+            g = apply5(derivative, [get_d(n) for n in index])
             h = apply5(derivative, [tiles[n] for n in index])
             for a in range(5):
                 total[index[a]] = total[index[a]] + g[a] * h[a]
@@ -592,14 +687,23 @@
     lax.fori_loop(0, 2, event, 0)
 
 
-def term_kernel(d1, d2, forward, wm, out, token, total, wide, tiles):
+def first_term_kernel(d, d_edge, forward, order, total, token, wide, tiles):
     def clear(n, carry):
         total[n] = jnp.zeros((8, 128), f32)
         return carry
 
     lax.fori_loop(0, points, clear, 0)
-    correlate(d1, forward, 0, total, wide, tiles)
-    correlate(d2, forward, 1, total, wide, tiles)
+    correlate(d, d_edge, forward, 0, total, wide, tiles)
+    token[...] = jnp.zeros_like(token)
+
+
+def last_term_kernel(d, d_edge, forward, before, wm, out, token, total, wide, tiles):
+    def copy(n, carry):
+        total[n] = before[n]
+        return carry
+
+    lax.fori_loop(0, points, copy, 0)
+    correlate(d, d_edge, forward, 1, total, wide, tiles)
     token[...] = jnp.zeros_like(token)
 
     def tile(i, j, k):
@@ -725,56 +829,103 @@
         return lax.ppermute(even, "lon", pairs), lax.ppermute(odd, "lon", between)
 
     face_low, face_high, row_low, row_high = edges
+    rim_fields = [(2, 50, 8, 128)] * 2
     s1, order = source(1, row_low)
     beside = swap(face_low, face_high, "lat")
-    first_message = call(
+    *message, own = call(
         rows_kernel,
         "rows",
-        [(40, 8, 128)] * 2,
+        [(25, 8, 128)] * 2 + [(2, 15, 8, 128)],
         (flags, *beside, row_low, row_high, wm_rim, order),
         specs=[SMEM] + [VMEM] * 5 + [ANY],
         moved=4 * 10**5,
         vmem=4,
     )
-    first_message = trade(*first_message)
-    d1, q, inverse, f, *edges = call(
-        first_step_kernel,
-        "first_step",
-        [field, field, one, field] + faces(2),
-        (flags, f, *beside, *first_message, d, q, s1, wm, mass),
-        specs=[SMEM] + [VMEM] * 10,
+    first_message = trade(*message)
+    d1, q1, inverse, f = call(
+        first_guess_kernel,
+        "first_guess",
+        [field, field, one, field],
+        (flags, f, *beside, d, q, s1, wm, mass, message[0]),
+        specs=[SMEM] + [VMEM] * 8 + [ANY],
         flops=10**8,
+    )
+    d1_edge, q1_edge, inverse_edge, inverse_rim, f, *edges = call(
+        first_fix_kernel,
+        "first_fix",
+        rim_fields + [(50, 8, 128), (2, 5, 8, 128), field] + faces(2),
+        (flags, *first_message, own, wm_rim, d1, q1, inverse, f),
+        [pltpu.VMEM((2, 25, 8, 128), f32)],
+        [SMEM] + [VMEM] * 8,
+        flops=10**7,
     )
     s2, unused = source(2, edges[0])
     beside = swap(*edges, "lat")
-    d2, q, *second_message = call(
+    d2, q2, *message = call(
         advance_kernel,
         "advance",
         [field, field] + [(2, 20, 8, 128)] * 2,
-        (flags, f, *beside, d1, q, inverse, s2),
-        specs=[SMEM] + [VMEM] * 7,
+        (flags, f, *beside, d1, d1_edge, q1, q1_edge, inverse, inverse_edge, s2),
+        specs=[SMEM] + [VMEM] * 10,
         flops=10**7,
     )
-    second_message = trade(*second_message)
-    d2, q, f, *edges = call(
-        second_step_kernel,
-        "second_step",
-        [field, field, field] + faces(2),
-        (flags, *second_message, *first_message, d2, q, inverse, s2, wm),
-        specs=[SMEM] + [VMEM] * 9,
+    second_message = trade(*message)
+    (f,) = call(
+        second_guess_kernel,
+        "second_guess",
+        [field],
+        (d2, s2, wm, message[0]),
+        specs=[VMEM] * 3 + [ANY],
         flops=10**8,
     )
+    term, order = call(
+        first_term_kernel,
+        "first_term",
+        [one, token],
+        (d1, d1_edge, forward, message[0]),
+        [wide, tiles],
+        [VMEM] * 3 + [ANY],
+        flops=10**8,
+    )
+    d2_edge, q2_edge, f, *edges = call(
+        second_fix_kernel,
+        "second_fix",
+        rim_fields + [field] + faces(2),
+        (flags, *second_message, *first_message, wm_rim, inverse_rim, d2, q2, f, order),
+        [pltpu.VMEM((2, 25, 8, 128), f32)],
+        [SMEM] + [VMEM] * 9 + [ANY],
+        flops=10**7,
+    )
+    beside = swap(*edges, "lat")
     kernel, order = call(
-        term_kernel, "term", [(5, 40, 640), token], (d1, d2, forward, wm), [tiles, wide, tiles], flops=10**8
-    )
-    beside = swap(*edges, "lat")
+        last_term_kernel,
+        "last_term",
+        [(5, 40, 640), token],
+        (d2, d2_edge, forward, term, wm),
+        [tiles, wide, tiles],
+        flops=10**8,
+    )
+    fields = (q2, q2_edge, inverse, inverse_edge)
+    velocity, order_too = call(
+        inner_velocity_kernel,
+        "inner_velocity",
+        [(2, 5, 40, 640), token],
+        (f, *fields, order),
+        [wide, pltpu.VMEM((2, 3, 40, 640), f32), pltpu.SemaphoreType.DMA((6,))],
+        [VMEM] * 5 + [ANY],
+        [HBM, VMEM],
+        flops=10**7,
+    )
     (velocity,) = call(
-        last_kernel,
-        "last",
+        outer_velocity_kernel,
+        "outer_velocity",
         [(2, 5, 40, 640)],
-        (flags, f, *beside, q, inverse, order),
-        [wide],
-        [SMEM] + [VMEM] * 5 + [ANY],
+        (flags, f, *beside, *fields, velocity, order_too),
+        [wide, pltpu.VMEM((2, 2, 40, 640), f32), pltpu.SemaphoreType.DMA((4,))],
+        [SMEM] + [VMEM] * 7 + [HBM, ANY],
+        [HBM],
+        flops=10**7,
+        input_output_aliases={8: 0},
     )
     return velocity.reshape(native), kernel.reshape(kernel_shape)
 

time: 86.5 us -> 82.4 us (0.953)
  waiting for transfers between devices: 19.3 us -> 14.7 us
  Pallas kernels: 34.6 us -> 37.1 us
  starting transfers between devices: 31.5 us -> 29.3 us
    ppermute x4, waiting for transfers between devices: 11 us -> 6.43 us  [trade(): return (lax.ppermute(even, 'lon', pairs), lax.ppermute(odd, 'lon', between))]
    pallas_call x11 -> x15, Pallas kernels: 34.6 us -> 37.1 us  [call(): pl.pallas_call(kernel, name=name, out_shape=[s if hasattr(s, 'dtype') els...]
    ppermute x4, starting transfers between devices: 3.24 us -> 1 us  [trade(): return (lax.ppermute(even, 'lon', pairs), lax.ppermute(odd, 'lon', between))]
  transfers between devices with their start and end apart: 11 -> 11, of which waited for: 5 -> 5; matrix products, arithmetic and copies ran while one was open for 0% -> 0% of each run, Pallas kernels for 22% -> 29%
where the time goes in v4:
time: 82.4 us; the launch traced here: 82.2 us
  Pallas kernels  37.1 us (45%)
  starting transfers between devices  29.3 us (36%)
  waiting for transfers between devices  14.7 us (18%)
  between operations  1.01 us (1%)
    pallas_call x15, Pallas kernels, call(): pl.pallas_call(kernel, name=name, out_shape=[s if hasattr(s, 'dtype') els...  37.1 us
    ppermute x6, starting transfers between devices, swap(): return (lax.ppermute(high, axis, up), lax.ppermute(low, axis, down))  17.1 us
    all_to_all x1, starting transfers between devices, on_device(): lax.all_to_all(packed.reshape(devices, 2, 128), ('lat', 'lon'), 0, 0, til...  11.1 us
    ppermute x4, waiting for transfers between devices, trade(): return (lax.ppermute(even, 'lon', pairs), lax.ppermute(odd, 'lon', between))  6.43 us
    all_to_all x1, waiting for transfers between devices, on_device(): lax.all_to_all(packed.reshape(devices, 2, 128), ('lat', 'lon'), 0, 0, til...  5.16 us
    ppermute x6, waiting for transfers between devices, swap(): return (lax.ppermute(high, axis, up), lax.ppermute(low, axis, down))  3.09 us
  transfers between devices with their start and end apart: 11, of which 5 were waited for; matrix products, arithmetic and copies ran while one was open for 0% of the time, Pallas kernels for 29%

profile of v4, /device:TPU:0, one launch (start us, length us, event | category | flops | bytes accessed | tf_op | source)
XLA Modules:
  0.0 82.2 jit_solution(5898571041624025187)
XLA Ops:
  0.6 0.0 copy-start.1
  0.6 2.3 %pack.1 = f32[256,128]{1,0:T(8,128)} custom-call(f32[3,2,1024]{2,1,0:T(2,128)} %bitcast.30, s32[1,1024]{1,0:T(1,128)} %bitcast.31, s32[1,1024]{1,0:T(1,128)} %bitcast.32), custom_call_target="tpu_custom_call" | custom-call | flops 1000000 | bytes 4000000 | tf_op jit(solution)/shard_map/pack/pallas_call | solution.py:719
  2.9 11.1 %all-to-all-start = ((f32[128,2,128]{2,1,0:T(2,128)}), f32[128,2,128]{2,1,0:T(2,128)S(1)}, u32[]{:S(2)}, u32[]{:S(2)}) async-start(f32[128,2,128]{2,1,0:T(2,128)} %bitcast.27), calls=%async_computation | async-start | bytes 262144 | tf_op jit(solution)/shard_map/all_to_all | solution.py:773
  14.1 0.1 stack.23
  14.2 4.1 %start.1 = (f32[2,125,8,128]{3,2,1,0:T(8,128)}, f32[2,125,8,128]{3,2,1,0:T(8,128)}, f32[125,8,128]{2,1,0:T(8,128)}, f32[125,8,128]{2,1,0:T(8,128)}, f32[2,25,8,128]{3,2,1,0:T(8,128)}, /*index=5*/f32[12288,8,128]{2,1,0:T(8,128)}) custom-call(f32[2,5,40,640]{3,2,1,0:T(8,128)} %bitcast.24, f32[2,5,40,640]{3,2,1,0:T(8,128)} %bitcast.25, ...), custom_call_target="tpu_custom_call" | custom-call | flops 100000000 | bytes 4000000 | tf_op jit(solution)/shard_map/start/pallas_call | solution.py:719
  18.3 0.0 copy-start.2
  18.3 0.0 copy-start
  18.3 0.0 copy-start.3
  18.3 0.0 copy-start.5
  18.3 5.2 %all-to-all-done = f32[128,2,128]{2,1,0:T(2,128)S(1)} async-done(((f32[128,2,128]{2,1,0:T(2,128)}), f32[128,2,128]{2,1,0:T(2,128)S(1)}, u32[]{:S(2)}, u32[]{:S(2)}) %all-to-all-start) | async-done | bytes 131104 | tf_op jit(solution)/shard_map/all_to_all | solution.py:773
  23.5 5.1 %first_force.1 = (f32[2,125,8,128]{3,2,1,0:T(8,128)S(1)}, f32[3,18,8,128]{3,2,1,0:T(8,128)S(1)}, f32[3,18,8,128]{3,2,1,0:T(8,128)S(1)}, f32[3,5,8,128]{3,2,1,0:T(8,128)S(1)}, f32[3,5,8,128]{3,2,1,0:T(8,128)S(1)}) custom-call(f32[256,128]{1,0:T(8,128)S(1)} %bitcast.21, f32[12288,8,128]{2,1,0:T(8,128)} %get-tuple-element.45.kept), custom_call_target="tpu_custom_call" | custom-call | flops 4000000000 | bytes 4000000 | tf_op jit(solution)/shard_map/first_force/pallas_call | solution.py:719
  28.6 1.3 %collective-permute-start = (f32[3,18,8,128]{3,2,1,0:T(8,128)S(1)}, f32[3,18,8,128]{3,2,1,0:T(8,128)S(1)}, u32[]{:S(2)}, u32[]{:S(2)}) collective-permute-start(f32[3,18,8,128]{3,2,1,0:T(8,128)S(1)} %get-tuple-element.46), channel_id=1, source_target_pairs={{0,16},{16,32},{32,48},{48,64},{64,80},{80,96},{96,112},{112,0},{1... | collective-permute-start | bytes 663560 | tf_op jit(solution)/shard_map/ppermute | solution.py:736
  29.9 4.4 %collective-permute-start.1 = (f32[3,18,8,128]{3,2,1,0:T(8,128)S(1)}, f32[3,18,8,128]{3,2,1,0:T(8,128)S(1)}, u32[]{:S(2)}, u32[]{:S(2)}) collective-permute-start(f32[3,18,8,128]{3,2,1,0:T(8,128)S(1)} %get-tuple-element.47), channel_id=1, source_target_pairs={{16,0},{32,16},{48,32},{64,48},{80,64},{96,80},{112,96},{0,112},{1... | collective-permute-start | bytes 663560 | tf_op jit(solution)/shard_map/ppermute | solution.py:736
  34.4 4.8 %source.2 = (f32[2,128,8,128]{3,2,1,0:T(8,128)S(1)}, f32[8,128]{1,0:T(8,128)S(1)}) custom-call(f32[256,128]{1,0:T(8,128)S(1)} %bitcast.22, f32[3,5,8,128]{3,2,1,0:T(8,128)S(1)} %get-tuple-element.48.order.row_low), custom_call_target="tpu_custom_call" | custom-call | flops 4000000000 | bytes 4000000 | tf_op jit(solution)/shard_map/source/pallas_call | solution.py:719
  39.2 1.5 %collective-permute-done.from_below.below = f32[3,18,8,128]{3,2,1,0:T(8,128)S(1)} collective-permute-done((f32[3,18,8,128]{3,2,1,0:T(8,128)S(1)}, f32[3,18,8,128]{3,2,1,0:T(8,128)S(1)}, u32[]{:S(2)}, u32[]{:S(2)}) %collective-permute-start) | collective-permute-done | bytes 221216 | tf_op jit(solution)/shard_map/ppermute | solution.py:736
  40.6 1.6 %collective-permute-done.1.from_above.above = f32[3,18,8,128]{3,2,1,0:T(8,128)S(1)} collective-permute-done((f32[3,18,8,128]{3,2,1,0:T(8,128)S(1)}, f32[3,18,8,128]{3,2,1,0:T(8,128)S(1)}, u32[]{:S(2)}, u32[]{:S(2)}) %collective-permute-start.1) | collective-permute-done | bytes 221216 | tf_op jit(solution)/shard_map/ppermute | solution.py:736
  42.2 0.0 copy-done.2
  42.2 0.7 rows.1
  42.9 0.6 collective-permute-start.3
  43.5 0.3 collective-permute-start.2
  43.8 0.0 copy-done
  43.8 0.0 copy-done.3
  43.8 0.0 copy-done.5
  43.8 0.0 copy-done.4
  43.8 2.3 %first_guess.1 = (f32[2,125,8,128]{3,2,1,0:T(8,128)S(1)}, f32[2,125,8,128]{3,2,1,0:T(8,128)S(1)}, f32[125,8,128]{2,1,0:T(8,128)S(1)}, f32[2,125,8,128]{3,2,1,0:T(8,128)S(1)}) custom-call(s32[5]{0:T(128)S(1)} %convert_element_type.3.flags, f32[2,125,8,128]{3,2,1,0:T(8,128)S(1)} %get-tuple-element.55.f, ...), custom_call_target="tpu_custom_call" | custom-call | flops 100000000 | bytes 4000000 | tf_op jit(solution)/shard_map/first_guess/pallas_call | solution.py:719
  46.1 3.1 %collective-permute-done.3.odd.wm_odd = f32[25,8,128]{2,1,0:T(8,128)S(1)} collective-permute-done((f32[25,8,128]{2,1,0:T(8,128)S(1)}, f32[25,8,128]{2,1,0:T(8,128)S(1)}, u32[]{:S(2)}, u32[]{:S(2)}) %collective-permute-start.3) | collective-permute-done | bytes 102432 | tf_op jit(solution)/shard_map/ppermute | solution.py:829
  49.2 0.0 collective-permute-done.2.even.wm_even
  49.2 1.2 %first_fix.1 = (f32[2,50,8,128]{3,2,1,0:T(8,128)S(1)}, f32[2,50,8,128]{3,2,1,0:T(8,128)S(1)}, f32[50,8,128]{2,1,0:T(8,128)S(1)}, f32[2,5,8,128]{3,2,1,0:T(8,128)...) custom-call(s32[5]{0:T(128)S(1)} %convert_element_type.3.flags, ...), custom_call_target="tpu_custom_call" | custom-call | flops 10000000 | bytes 4000000 | tf_op jit(solution)/shard_map/first_fix/pallas_call | solution.py:719
  50.4 1.7 %collective-permute-start.4 = (f32[2,18,8,128]{3,2,1,0:T(8,128)S(1)}, f32[2,18,8,128]{3,2,1,0:T(8,128)S(1)}, u32[]{:S(2)}, u32[]{:S(2)}) collective-permute-start(f32[2,18,8,128]{3,2,1,0:T(8,128)S(1)} %get-tuple-element.66), channel_id=1, source_target_pairs={{0,16},{16,32},{32,48},{48,64},{64,80},{80,96},{96,112},{112,0},{1... | collective-permute-start | bytes 442376 | tf_op jit(solution)/shard_map/ppermute | solution.py:736
  52.2 4.0 %collective-permute-start.5 = (f32[2,18,8,128]{3,2,1,0:T(8,128)S(1)}, f32[2,18,8,128]{3,2,1,0:T(8,128)S(1)}, u32[]{:S(2)}, u32[]{:S(2)}) collective-permute-start(f32[2,18,8,128]{3,2,1,0:T(8,128)S(1)} %get-tuple-element.67.order), channel_id=1, source_target_pairs={{16,0},{32,16},{48,32},{64,48},{80,64},{96,80},{112,96},{0,112},{1... | collective-permute-start | bytes 442376 | tf_op jit(solution)/shard_map/ppermute | solution.py:736
  56.1 5.3 %source.3 = (f32[2,128,8,128]{3,2,1,0:T(8,128)S(1)}, f32[8,128]{1,0:T(8,128)}) custom-call(f32[256,128]{1,0:T(8,128)S(1)} %bitcast.23, f32[2,18,8,128]{3,2,1,0:T(8,128)S(1)} %get-tuple-element.67.order), custom_call_target="tpu_custom_call" | custom-call | flops 4000000000 | bytes 4000000 | tf_op jit(solution)/shard_map/source/pallas_call | solution.py:719
  61.4 0.0 collective-permute-done.4.below
  61.4 0.0 collective-permute-done.5.above
  61.4 1.0 %advance.1 = (f32[2,125,8,128]{3,2,1,0:T(8,128)S(1)}, f32[2,125,8,128]{3,2,1,0:T(8,128)S(1)}, f32[2,20,8,128]{3,2,1,0:T(8,128)S(1)}, f32[2,20,8,128]{3,2,1,0:T(8,128)S(1)}) custom-call(s32[5]{0:T(128)S(1)} %convert_element_type.3.flags, f32[2,125,8,128]{3,2,1,0:T(8,128)S(1)} %get-tuple-element.65.f, f32[2,18,8,128]{3,2,1,0:T(8,128)S(1)} %collective-permute-done.4.below, ...), custom_call_target="tpu_custom_call" | custom-call | flops 10000000 | bytes 4000000 | tf_op jit(solution)/shard_map/advance/pallas_call | solution.py:719
  62.5 0.1 collective-permute-start.7
  62.6 0.1 collective-permute-start.6
  62.7 2.1 %first_term.1 = (f32[125,8,128]{2,1,0:T(8,128)S(1)}, f32[8,128]{1,0:T(8,128)S(1)}) custom-call(f32[2,125,8,128]{3,2,1,0:T(8,128)S(1)} %get-tuple-element.61.d, f32[2,50,8,128]{3,2,1,0:T(8,128)S(1)} %get-tuple-element.68.d_edge, bf16[2,2,5,40,640]{4,3,2,1,0:T(8,128)(2,1)S(1)} %bitcast.19, f32[2,20,8,128]{3,2,1,0:T(8,128)S(1)} %get-tuple-element.72.order), custom_call_target="tpu_custom_call" | custom-call | flops 100000000 | bytes 4000000 | tf_op jit(solution)/shard_map/first_term/pallas_call | solution.py:719
  64.8 1.3 %second_guess.1.f = f32[2,125,8,128]{3,2,1,0:T(8,128)S(1)} custom-call(f32[2,125,8,128]{3,2,1,0:T(8,128)S(1)} %get-tuple-element.75.d, f32[2,128,8,128]{3,2,1,0:T(8,128)S(1)} %get-tuple-element.71.source, f32[125,8,128]{2,1,0:T(8,128)S(1)} %copy-done, f32[2,20,8,128]{3,2,1,0:T(8,128)S(1)} %get-tuple-element.72.order), custom_call_target="tpu_custom_call" | custom-call | flops 100000000 | bytes 4000000 | tf_op jit(solution)/shard_map/second_guess/pallas_call | solution.py:719
  66.1 3.3 %collective-permute-done.7.odd = f32[2,20,8,128]{3,2,1,0:T(8,128)S(1)} collective-permute-done((f32[2,20,8,128]{3,2,1,0:T(8,128)S(1)}, f32[2,20,8,128]{3,2,1,0:T(8,128)S(1)}, u32[]{:S(2)}, u32[]{:S(2)}) %collective-permute-start.7) | collective-permute-done | bytes 163872 | tf_op jit(solution)/shard_map/ppermute | solution.py:829
  69.4 0.0 collective-permute-done.6.even
  69.4 1.4 %second_fix.1 = (f32[2,50,8,128]{3,2,1,0:T(8,128)S(1)}, f32[2,50,8,128]{3,2,1,0:T(8,128)S(1)}, f32[2,125,8,128]{3,2,1,0:T(8,128)S(1)}, f32[2,18,8,128]{3,2,1,0:T(8,128)S(1)}, f32[2,18,8,128]{3,2,1,0:T(8,128)S(1)}) custom-call(s32[5]{0:T(128)S(1)} %convert_element_type.3.flags, f32[2,20,8,128]{3,2,1,0:T(8,128)S(1)} %collective-permute-done.6.even, ...), custom_call_target="tpu_custom_call" | custom-call | flops 10000000 | bytes 4000000 | tf_op jit(solution)/shard_map/second_fix/pallas_call | solution.py:719
  70.8 0.6 collective-permute-start.8
  71.5 5.1 %collective-permute-start.9 = (f32[2,18,8,128]{3,2,1,0:T(8,128)S(1)}, f32[2,18,8,128]{3,2,1,0:T(8,128)S(1)}, u32[]{:S(2)}, u32[]{:S(2)}) collective-permute-start(f32[2,18,8,128]{3,2,1,0:T(8,128)S(1)} %get-tuple-element.80), channel_id=1, source_target_pairs={{16,0},{32,16},{48,32},{64,48},{80,64},{96,80},{112,96},{0,112},{1... | collective-permute-start | bytes 442376 | tf_op jit(solution)/shard_map/ppermute | solution.py:736
  76.5 3.0 %last_term.1 = (f32[5,40,640]{2,1,0:T(8,128)}, f32[8,128]{1,0:T(8,128)S(1)}) custom-call(f32[2,125,8,128]{3,2,1,0:T(8,128)S(1)} %get-tuple-element.75.d, f32[2,50,8,128]{3,2,1,0:T(8,128)S(1)} %get-tuple-element.82.d_edge, bf16[2,2,5,40,640]{4,3,2,1,0:T(8,128)(2,1)S(1)} %bitcast.20, f32[125,8,128]{2,1,0:T(8,128)S(1)} %get-tuple-element.83.before, ...), custom_call_target="tpu_custom_call" | custom-call | flops 100000000 | bytes 4000000 | tf_op jit(solution)/shard_map/last_term/pallas_call | solution.py:719
  79.6 1.0 %inner_velocity.1 = (f32[2,5,40,640]{3,2,1,0:T(8,128)}, f32[8,128]{1,0:T(8,128)S(1)}) custom-call(f32[2,125,8,128]{3,2,1,0:T(8,128)S(1)} %get-tuple-element.78.f, f32[2,125,8,128]{3,2,1,0:T(8,128)S(1)} %get-tuple-element.76.q, f32[2,50,8,128]{3,2,1,0:T(8,128)S(1)} %get-tuple-element.81.q_edge, f32[125,8,128]{2,1,0:T(8,128)S(1)} %get-tuple-element.63.inverse, ...), custom_call_target="tpu_custom_call" | custom-call | flops 10000000 | bytes 4000000 | tf_op jit(solution)/shard_map/inner_velocity/pallas_call | solution.py:719
  80.6 0.0 collective-permute-done.8.below
  80.6 0.0 collective-permute-done.9.above
  80.6 1.4 %outer_velocity.1 = f32[2,5,40,640]{3,2,1,0:T(8,128)} custom-call(s32[5]{0:T(128)S(1)} %convert_element_type.3.flags, f32[2,125,8,128]{3,2,1,0:T(8,128)S(1)} %get-tuple-element.78.f, f32[2,18,8,128]{3,2,1,0:T(8,128)S(1)} %collective-permute-done.8.below, f32[2,18,8,128]{3,2,1,0:T(8,128)S(1)} %collective-permute-done.9.above, ...), custom_call_target="tpu_custom_call", output_to_operand_aliasing={{}: (8, {})} | custom-call | flops 10000000 | bytes 4000000 | tf_op jit(solution)/shard_map/outer_velocity/pallas_call | solution.py:719
  (3 shorter events, 0.0 us)
Async XLA Ops:
  0.6 62.0 %copy-start.1 = (bf16[2,2,1,5,40,640]{5,4,3,2,1,0:T(8,128)(2,1)S(1)}, bf16[2,2,1,5,40,640]{5,4,3,2,1,0:T(8,128)(2,1)}, u32[]{:S(2)}) copy-start(bf16[2,2,1,5,40,640]{5,4,3,2,1,0:T(8,128)(2,1)} %param.12) | copy-start | bytes 3072004
  2.9 20.6 %all-to-all-start = ((f32[128,2,128]{2,1,0:T(2,128)}), f32[128,2,128]{2,1,0:T(2,128)S(1)}, u32[]{:S(2)}, u32[]{:S(2)}) async-start(f32[128,2,128]{2,1,0:T(2,128)} %bitcast.27), calls=%async_computation | async-start | bytes 262144 | tf_op jit(solution)/shard_map/all_to_all | solution.py:773
  18.3 24.0 %copy-start.2 = (f32[2,25,8,128]{3,2,1,0:T(8,128)S(1)}, f32[2,25,8,128]{3,2,1,0:T(8,128)}, u32[]{:S(2)}) copy-start(f32[2,25,8,128]{3,2,1,0:T(8,128)} %get-tuple-element.50.wm_rim) | copy-start | bytes 614404
  18.3 25.5 %copy-start = (f32[125,8,128]{2,1,0:T(8,128)S(1)}, f32[125,8,128]{2,1,0:T(8,128)}, u32[]{:S(2)}) copy-start(f32[125,8,128]{2,1,0:T(8,128)} %get-tuple-element.59.wm) | copy-start | bytes 1536004
  18.3 25.4 %copy-start.3 = (f32[2,125,8,128]{3,2,1,0:T(8,128)S(1)}, f32[2,125,8,128]{3,2,1,0:T(8,128)}, u32[]{:S(2)}) copy-start(f32[2,125,8,128]{3,2,1,0:T(8,128)} %get-tuple-element.56.d) | copy-start | bytes 3072004
  18.3 25.4 %copy-start.5 = (f32[125,8,128]{2,1,0:T(8,128)S(1)}, f32[125,8,128]{2,1,0:T(8,128)}, u32[]{:S(2)}) copy-start(f32[125,8,128]{2,1,0:T(8,128)} %get-tuple-element.60.mass) | copy-start | bytes 1536004
  23.5 20.3 %copy-start.4 = (f32[2,125,8,128]{3,2,1,0:T(8,128)S(1)}, f32[2,125,8,128]{3,2,1,0:T(8,128)}, u32[]{:S(2)}) copy-start(f32[2,125,8,128]{3,2,1,0:T(8,128)} %get-tuple-element.57.q) | copy-start | bytes 3072004
  28.6 12.0 %collective-permute-start = (f32[3,18,8,128]{3,2,1,0:T(8,128)S(1)}, f32[3,18,8,128]{3,2,1,0:T(8,128)S(1)}, u32[]{:S(2)}, u32[]{:S(2)}) collective-permute-start(f32[3,18,8,128]{3,2,1,0:T(8,128)S(1)} %get-tuple-element.46), channel_id=1, source_target_pairs={{0,16},{16,32},{32,48},{48,64},{64,80},{80,96},{96,112},{112,0},{1... | collective-permute-start | bytes 663560 | tf_op jit(solution)/shard_map/ppermute | solution.py:736
  29.9 12.3 %collective-permute-start.1 = (f32[3,18,8,128]{3,2,1,0:T(8,128)S(1)}, f32[3,18,8,128]{3,2,1,0:T(8,128)S(1)}, u32[]{:S(2)}, u32[]{:S(2)}) collective-permute-start(f32[3,18,8,128]{3,2,1,0:T(8,128)S(1)} %get-tuple-element.47), channel_id=1, source_target_pairs={{16,0},{32,16},{48,32},{64,48},{80,64},{96,80},{112,96},{0,112},{1... | collective-permute-start | bytes 663560 | tf_op jit(solution)/shard_map/ppermute | solution.py:736
  42.9 6.3 %collective-permute-start.3 = (f32[25,8,128]{2,1,0:T(8,128)S(1)}, f32[25,8,128]{2,1,0:T(8,128)S(1)}, u32[]{:S(2)}, u32[]{:S(2)}) collective-permute-start(f32[25,8,128]{2,1,0:T(8,128)S(1)} %get-tuple-element.53), channel_id=1, source_target_pairs={{0,15},{1,2},{2,1},{3,4},{4,3},{5,6},{6,5},{7,8},{8,7},{9,10},{10,... | collective-permute-start | bytes 307208 | tf_op jit(solution)/shard_map/ppermute | solution.py:829
  43.5 5.7 %collective-permute-start.2 = (f32[25,8,128]{2,1,0:T(8,128)S(1)}, f32[25,8,128]{2,1,0:T(8,128)S(1)}, u32[]{:S(2)}, u32[]{:S(2)}) collective-permute-start(f32[25,8,128]{2,1,0:T(8,128)S(1)} %get-tuple-element.52.order), channel_id=1, source_target_pairs={{0,1},{1,0},{2,3},{3,2},{4,5},{5,4},{6,7},{7,6},{8,9},{9,8},{10,11... | collective-permute-start | bytes 307208 | tf_op jit(solution)/shard_map/ppermute | solution.py:829
  50.4 11.0 %collective-permute-start.4 = (f32[2,18,8,128]{3,2,1,0:T(8,128)S(1)}, f32[2,18,8,128]{3,2,1,0:T(8,128)S(1)}, u32[]{:S(2)}, u32[]{:S(2)}) collective-permute-start(f32[2,18,8,128]{3,2,1,0:T(8,128)S(1)} %get-tuple-element.66), channel_id=1, source_target_pairs={{0,16},{16,32},{32,48},{48,64},{64,80},{80,96},{96,112},{112,0},{1... | collective-permute-start | bytes 442376 | tf_op jit(solution)/shard_map/ppermute | solution.py:736
  52.2 9.3 %collective-permute-start.5 = (f32[2,18,8,128]{3,2,1,0:T(8,128)S(1)}, f32[2,18,8,128]{3,2,1,0:T(8,128)S(1)}, u32[]{:S(2)}, u32[]{:S(2)}) collective-permute-start(f32[2,18,8,128]{3,2,1,0:T(8,128)S(1)} %get-tuple-element.67.order), channel_id=1, source_target_pairs={{16,0},{32,16},{48,32},{64,48},{80,64},{96,80},{112,96},{0,112},{1... | collective-permute-start | bytes 442376 | tf_op jit(solution)/shard_map/ppermute | solution.py:736
  62.5 6.9 %collective-permute-start.7 = (f32[2,20,8,128]{3,2,1,0:T(8,128)S(1)}, f32[2,20,8,128]{3,2,1,0:T(8,128)S(1)}, u32[]{:S(2)}, u32[]{:S(2)}) collective-permute-start(f32[2,20,8,128]{3,2,1,0:T(8,128)S(1)} %get-tuple-element.73), channel_id=1, source_target_pairs={{0,15},{1,2},{2,1},{3,4},{4,3},{5,6},{6,5},{7,8},{8,7},{9,10},{10,... | collective-permute-start | bytes 491528 | tf_op jit(solution)/shard_map/ppermute | solution.py:829
  62.6 6.8 %collective-permute-start.6 = (f32[2,20,8,128]{3,2,1,0:T(8,128)S(1)}, f32[2,20,8,128]{3,2,1,0:T(8,128)S(1)}, u32[]{:S(2)}, u32[]{:S(2)}) collective-permute-start(f32[2,20,8,128]{3,2,1,0:T(8,128)S(1)} %get-tuple-element.72.order), channel_id=1, source_target_pairs={{0,1},{1,0},{2,3},{3,2},{4,5},{5,4},{6,7},{7,6},{8,9},{9,8},{10,11... | collective-permute-start | bytes 491528 | tf_op jit(solution)/shard_map/ppermute | solution.py:829
  70.8 9.7 %collective-permute-start.8 = (f32[2,18,8,128]{3,2,1,0:T(8,128)S(1)}, f32[2,18,8,128]{3,2,1,0:T(8,128)S(1)}, u32[]{:S(2)}, u32[]{:S(2)}) collective-permute-start(f32[2,18,8,128]{3,2,1,0:T(8,128)S(1)} %get-tuple-element.79), channel_id=1, source_target_pairs={{0,16},{16,32},{32,48},{48,64},{64,80},{80,96},{96,112},{112,0},{1... | collective-permute-start | bytes 442376 | tf_op jit(solution)/shard_map/ppermute | solution.py:736
  71.5 9.1 %collective-permute-start.9 = (f32[2,18,8,128]{3,2,1,0:T(8,128)S(1)}, f32[2,18,8,128]{3,2,1,0:T(8,128)S(1)}, u32[]{:S(2)}, u32[]{:S(2)}) collective-permute-start(f32[2,18,8,128]{3,2,1,0:T(8,128)S(1)} %get-tuple-element.80), channel_id=1, source_target_pairs={{16,0},{32,16},{48,32},{64,48},{80,64},{96,80},{112,96},{0,112},{1... | collective-permute-start | bytes 442376 | tf_op jit(solution)/shard_map/ppermute | solution.py:736

commit v5 on v4

--- a/solution.py
+++ b/solution.py
@@ -18,7 +18,6 @@
 face_tiles = 18
 kept_tiles = 12288
 VMEM = pl.BlockSpec(memory_space=pltpu.VMEM)
-SMEM = pl.BlockSpec(memory_space=pltpu.SMEM)
 HBM = pl.BlockSpec(memory_space=pltpu.HBM)
 ANY = pl.BlockSpec(memory_space=pl.ANY)
 
@@ -314,8 +313,8 @@
             store(c, m, both[:, :128] + both[:, 128:])
 
 
-def start_kernel(d_in, v_in, k_in, m_in, d_out, v_out, wm_out, mass_out, rim_out, kept, *scratch):
-    d0, v0, modulus, density, d, v, wm, mass, rim, kd, edges, wide, sems = scratch
+def start_kernel(d_in, k_in, m_in, d_out, wm_out, mass_out, rim_out, kept, low_out, high_out, rows_out, *scratch):
+    d0, modulus, density, d, wm, mass, rim, kd, low, high, rows, wide, sems = scratch
     copies = []
 
     def copy(source, target):
@@ -324,7 +323,7 @@
         return copies[-1]
 
     loads = [copy(k_in, modulus), copy(d_in.at[0], d0.at[0]), copy(d_in.at[1], d0.at[1])]
-    loads += [copy(m_in, density), copy(v_in, v0)]
+    loads += [copy(m_in, density)]
 
     def weighted(target):
         def put(n, value):
@@ -359,27 +358,16 @@
 
     fold(lambda n: mass[n], put_mass)
     copy(mass, mass_out)
-    low, high, row_low, row_high = edges.at[0:18], edges.at[18:36], edges.at[36:41], edges.at[41:46]
-    emit_faces(lambda n: mass[n], None, low, high, row_low, row_high)
-    copy(edges, kept.at[2 * points : 2 * points + 46])
-    loads[4].wait()
-    for e in range(2):
-
-        def put_v(n, value, e=e):
-            v[e, n] = value
-
-        to_tiles(lambda i, e=e: v0[e, i], put_v, wide)
-        copy(v.at[e], v_out.at[e])
+    emit_faces(lambda n: mass[n], 0, low, high, rows.at[0:1], rows.at[1:2])
+    copy(low, low_out)
+    copy(high, high_out)
+    copy(rows, rows_out)
     for pending in copies[len(loads) :]:
         pending.wait()
 
 
 def first_force_kernel(got, kept, f, face_low, face_high, row_low, row_high, kd, sems, *scratch):
-    edges = kept.at[2 * points : 2 * points + 46]
-    pairs = ((kept.at[0:points], kd.at[0]), (kept.at[points : 2 * points], kd.at[1]))
-    pairs += ((edges.at[0:18], face_low.at[2]), (edges.at[18:36], face_high.at[2]))
-    pairs += ((edges.at[36:41], row_low.at[2]), (edges.at[41:46], row_high.at[2]))
-    copies = [pltpu.make_async_copy(a, b, sems.at[n]) for n, (a, b) in enumerate(pairs)]
+    copies = [pltpu.make_async_copy(kept.at[e * points : (e + 1) * points], kd.at[e], sems.at[e]) for e in range(2)]
     for copy in copies:
         copy.start()
     devices = got.shape[0] // 2
@@ -417,21 +405,23 @@
     scatter(first[64:96], values, *scratch, store)
 
 
-def rows_kernel(flags, from_below, from_above, row_low, row_high, wm_rim, order, even_out, odd_out, own):
+def rows_kernel(flags, below, above, m_below, m_above, row_low, row_high, m_rows, wm_rim, order, *outs):
+    even_out, odd_out, own = outs
     sub, ln = sublane(), lane()
     low_tiles = [wm_rim[0, n] for n in range(25)]
     high_tiles = [wm_rim[1, n] for n in range(25)]
-    for c in range(row_low.shape[0]):
+    for c in range(3):
         for i in range(5):
-            low, high = row_low[c, i], row_high[c, i]
+            low, high = (row_low[c, i], row_high[c, i]) if c < 2 else (m_rows[0, i], m_rows[1, i])
             if i in (0, 4):
-                face = from_below if i == 0 else from_above
+                face = (below if i == 0 else above) if c < 2 else (m_below if i == 0 else m_above)
+                part = c if c < 2 else 0
                 keep = flags[0 if i == 0 else 1] > 0
-                extra = stack_rows([(face[c, k], 0) for k in range(4)])
-                corner = jnp.broadcast_to(face[c, 17][0:1, 0:1], (8, 128))
+                extra = stack_rows([(face[part, k], 0) for k in range(4)])
+                corner = jnp.broadcast_to(face[part, 17][0:1, 0:1], (8, 128))
                 extra = jnp.where((sub == 4) & (ln == 127), corner, extra)
                 low = low + jnp.where(keep, extra, 0.0)
-                high = high + jnp.where(keep, face[c, 16], 0.0)
+                high = high + jnp.where(keep, face[part, 16], 0.0)
             shared = (sub == 4) & (ln < 127)
             low = jnp.where(shared, pltpu.roll(row_of(low, 0), 127, 1), low)
             high = jnp.where(shared, pltpu.roll(row_of(high, 0), 127, 1), high)
@@ -450,20 +440,25 @@
     return row // 3, 5 + row % 3
 
 
-def first_guess_kernel(flags, f, below, above, d, q, source, wm, mass, order, d_out, q_out, inverse, f_out):
+def first_guess_kernel(flags, f, below, above, m_below, m_above, d, v0, source, wm, mass, order, *outs):
+    d_out, q_out, inverse, f_out, wide = outs
     for i in range(5):
-        v = complete(lambda n: mass[n], i, 2, flags, below, above)
+        v = complete(lambda n: mass[n], i, 0, flags, m_below, m_above)
         for j in range(5):
             for k in range(5):
                 inverse[at(i, j, k)] = 1.0 / v[j][k]
 
     def event(e, carry):
+        def put(n, value):
+            q_out[e, n] = value
+
+        to_tiles(lambda i: v0[e, i], put, wide)
         for i in range(5):
             v = complete(lambda n: f[e, n], i, e, flags, below, above)
             for j in range(5):
                 for k in range(5):
                     n = at(i, j, k)
-                    q_new = q[e, n] + 0.5 * time_step * (v[j][k] * inverse[n])
+                    q_new = q_out[e, n] + 0.5 * time_step * (v[j][k] * inverse[n])
                     q_out[e, n] = q_new
                     d_out[e, n] = d[e, n] + time_step * q_new
         force(lambda n: d_out[e, n], f_out, e, wm, lambda n: source[e, n])
@@ -715,6 +710,15 @@
     from_tiles(tile, put_plane, wide)
 
 
+def placed(kernel):
+    def with_place(*refs):
+        lat, lon = lax.axis_index("lat"), lax.axis_index("lon")
+        lat_count, lon_count = lax.axis_size("lat"), lax.axis_size("lon")
+        kernel((lat, lat_count - 1 - lat, lon, lon_count - 1 - lon, 1 - lon % 2), *refs)
+
+    return with_place
+
+
 def call(kernel, name, out_shapes, args, scratch=(), specs=None, outs=None, flops=10**6, moved=4 * 10**6, vmem=16, **more):
     return pl.pallas_call(
         kernel,
@@ -737,11 +741,8 @@
 
 
 def on_device(d0, v0, modulus, density, forward, traces, owner, point):
-    lat, lon = lax.axis_index("lat"), lax.axis_index("lon")
     lat_count, lon_count = lax.axis_size("lat"), lax.axis_size("lon")
     devices = lat_count * lon_count
-    flags = [lat > 0, lat < lat_count - 1, lon > 0, lon < lon_count - 1, lon % 2 == 0]
-    flags = jnp.stack(flags).astype(jnp.int32)
     field = (2, points, 8, 128)
     one = (points, 8, 128)
     wide_field = (2, padded, 8, 128)
@@ -775,24 +776,24 @@
     wide = pltpu.VMEM((5, 5, 40, 128), f32)
     tiles = pltpu.VMEM(one, f32)
     rim = (2, 25, 8, 128)
-    d, q, wm, mass, wm_rim, kept = call(
+    d, wm, mass, wm_rim, kept, *mass_edges = call(
         start_kernel,
         "start",
-        [field, field, one, one, rim, (kept_tiles, 8, 128)],
-        (d0, v0, modulus, density),
+        [field, one, one, rim, (kept_tiles, 8, 128)] + faces(1) + [(2, 5, 8, 128)],
+        (d0, modulus, density),
         [
             pltpu.VMEM(d0.shape, f32),
-            pltpu.VMEM(v0.shape, f32),
             pltpu.VMEM(modulus.shape, bf16),
             pltpu.VMEM(density.shape, bf16),
         ]
-        + [pltpu.VMEM(s, f32) for s in (field, field, one, one, rim, field, (46, 8, 128))]
+        + [pltpu.VMEM(s, f32) for s in [field, one, one, rim, field] + faces(1) + [(2, 5, 8, 128)]]
         + [wide, pltpu.SemaphoreType.DMA((16,))],
-        [HBM] * 4,
-        [HBM] * 6,
+        [HBM] * 3,
+        [HBM] * 8,
         flops=10**8,
         vmem=56,
     )
+    mass_beside = swap(*mass_edges[:2], "lat")
     scatter_scratch = [
         pltpu.VMEM((slots, devices), f32),
         pltpu.VMEM((slots, devices), f32),
@@ -803,9 +804,9 @@
     f, *edges = call(
         first_force_kernel,
         "first_force",
-        [field] + faces(3) + [(3, 5, 8, 128)] * 2,
+        [field] + faces(2) + [(2, 5, 8, 128)] * 2,
         (got, kept),
-        [pltpu.VMEM(field, f32), pltpu.SemaphoreType.DMA((6,))] + scatter_scratch,
+        [pltpu.VMEM(field, f32), pltpu.SemaphoreType.DMA((2,))] + scatter_scratch,
         [VMEM, HBM],
         flops=4 * 10**9,
         vmem=18,
@@ -833,40 +834,41 @@
     s1, order = source(1, row_low)
     beside = swap(face_low, face_high, "lat")
     *message, own = call(
-        rows_kernel,
+        placed(rows_kernel),
         "rows",
         [(25, 8, 128)] * 2 + [(2, 15, 8, 128)],
-        (flags, *beside, row_low, row_high, wm_rim, order),
-        specs=[SMEM] + [VMEM] * 5 + [ANY],
+        (*beside, *mass_beside, row_low, row_high, mass_edges[2], wm_rim, order),
+        specs=[VMEM] * 8 + [ANY],
         moved=4 * 10**5,
         vmem=4,
     )
     first_message = trade(*message)
     d1, q1, inverse, f = call(
-        first_guess_kernel,
+        placed(first_guess_kernel),
         "first_guess",
         [field, field, one, field],
-        (flags, f, *beside, d, q, s1, wm, mass, message[0]),
-        specs=[SMEM] + [VMEM] * 8 + [ANY],
+        (f, *beside, *mass_beside, d, v0, s1, wm, mass, message[0]),
+        [wide],
+        [VMEM] * 10 + [ANY],
         flops=10**8,
     )
     d1_edge, q1_edge, inverse_edge, inverse_rim, f, *edges = call(
-        first_fix_kernel,
+        placed(first_fix_kernel),
         "first_fix",
         rim_fields + [(50, 8, 128), (2, 5, 8, 128), field] + faces(2),
-        (flags, *first_message, own, wm_rim, d1, q1, inverse, f),
+        (*first_message, own, wm_rim, d1, q1, inverse, f),
         [pltpu.VMEM((2, 25, 8, 128), f32)],
-        [SMEM] + [VMEM] * 8,
+        [VMEM] * 8,
         flops=10**7,
     )
     s2, unused = source(2, edges[0])
     beside = swap(*edges, "lat")
     d2, q2, *message = call(
-        advance_kernel,
+        placed(advance_kernel),
         "advance",
         [field, field] + [(2, 20, 8, 128)] * 2,
-        (flags, f, *beside, d1, d1_edge, q1, q1_edge, inverse, inverse_edge, s2),
-        specs=[SMEM] + [VMEM] * 10,
+        (f, *beside, d1, d1_edge, q1, q1_edge, inverse, inverse_edge, s2),
+        specs=[VMEM] * 10,
         flops=10**7,
     )
     second_message = trade(*message)
@@ -888,12 +890,12 @@
         flops=10**8,
     )
     d2_edge, q2_edge, f, *edges = call(
-        second_fix_kernel,
+        placed(second_fix_kernel),
         "second_fix",
         rim_fields + [field] + faces(2),
-        (flags, *second_message, *first_message, wm_rim, inverse_rim, d2, q2, f, order),
+        (*second_message, *first_message, wm_rim, inverse_rim, d2, q2, f, order),
         [pltpu.VMEM((2, 25, 8, 128), f32)],
-        [SMEM] + [VMEM] * 9 + [ANY],
+        [VMEM] * 9 + [ANY],
         flops=10**7,
     )
     beside = swap(*edges, "lat")
@@ -917,15 +919,15 @@
         flops=10**7,
     )
     (velocity,) = call(
-        outer_velocity_kernel,
+        placed(outer_velocity_kernel),
         "outer_velocity",
         [(2, 5, 40, 640)],
-        (flags, f, *beside, *fields, velocity, order_too),
+        (f, *beside, *fields, velocity, order_too),
         [wide, pltpu.VMEM((2, 2, 40, 640), f32), pltpu.SemaphoreType.DMA((4,))],
-        [SMEM] + [VMEM] * 7 + [HBM, ANY],
+        [VMEM] * 7 + [HBM, ANY],
         [HBM],
         flops=10**7,
-        input_output_aliases={8: 0},
+        input_output_aliases={7: 0},
     )
     return velocity.reshape(native), kernel.reshape(kernel_shape)
 

time: 82.4 us -> 77.6 us (0.942)
  waiting for transfers between devices: 14.7 us -> 5.03 us
  starting transfers between devices: 29.3 us -> 37.4 us
  Pallas kernels: 37.1 us -> 33.7 us
    ppermute x6 -> x8, starting transfers between devices: 17.1 us -> 22.8 us  [swap(): return (lax.ppermute(high, axis, up), lax.ppermute(low, axis, down))]
    all_to_all x1, waiting for transfers between devices: 5.16 us -> 0.01 us  [on_device(): lax.all_to_all(packed.reshape(devices, 2, 128), ('lat', 'lon'), 0, 0, til...]
    pallas_call x15, Pallas kernels: 37.1 us -> 33.7 us  [call(): pl.pallas_call(kernel, name=name, out_shape=[s if hasattr(s, 'dtype') els...]
    ppermute x6 -> x8, waiting for transfers between devices: 3.09 us -> 0.65 us  [swap(): return (lax.ppermute(high, axis, up), lax.ppermute(low, axis, down))]
    ppermute x4, starting transfers between devices: 1 us -> 3.41 us  [trade(): return (lax.ppermute(even, 'lon', pairs), lax.ppermute(odd, 'lon', between))]
    ppermute x4, waiting for transfers between devices: 6.43 us -> 4.37 us  [trade(): return (lax.ppermute(even, 'lon', pairs), lax.ppermute(odd, 'lon', between))]
  transfers between devices with their start and end apart: 11 -> 13, of which waited for: 5 -> 3; matrix products, arithmetic and copies ran while one was open for 0% -> 0% of each run, Pallas kernels for 29% -> 37%
where the time goes in v5:
time: 77.6 us; the launch traced here: 77.2 us
  starting transfers between devices  37.4 us (48%)
  Pallas kernels  33.7 us (43%)
  waiting for transfers between devices  5.03 us (6%)
  between operations  1.01 us (1%)
    pallas_call x15, Pallas kernels, call(): pl.pallas_call(kernel, name=name, out_shape=[s if hasattr(s, 'dtype') els...  33.7 us
    ppermute x8, starting transfers between devices, swap(): return (lax.ppermute(high, axis, up), lax.ppermute(low, axis, down))  22.8 us
    all_to_all x1, starting transfers between devices, on_device(): lax.all_to_all(packed.reshape(devices, 2, 128), ('lat', 'lon'), 0, 0, til...  11.1 us
    ppermute x4, waiting for transfers between devices, trade(): return (lax.ppermute(even, 'lon', pairs), lax.ppermute(odd, 'lon', between))  4.37 us
    ppermute x4, starting transfers between devices, trade(): return (lax.ppermute(even, 'lon', pairs), lax.ppermute(odd, 'lon', between))  3.41 us
  transfers between devices with their start and end apart: 13, of which 3 were waited for; matrix products, arithmetic and copies ran while one was open for 0% of the time, Pallas kernels for 37%

profile of v5, /device:TPU:0, one launch (start us, length us, event | category | flops | bytes accessed | tf_op | source)
XLA Modules:
  0.0 77.2 jit_solution(6932284337288547954)
XLA Ops:
  0.6 0.0 copy-start.3
  0.6 0.0 copy-start.1
  0.7 2.3 %pack.1 = f32[256,128]{1,0:T(8,128)} custom-call(f32[3,2,1024]{2,1,0:T(2,128)} %bitcast.25, s32[1,1024]{1,0:T(1,128)} %bitcast.26, s32[1,1024]{1,0:T(1,128)} %bitcast.27), custom_call_target="tpu_custom_call" | custom-call | flops 1000000 | bytes 4000000 | tf_op jit(solution)/shard_map/pack/pallas_call | solution.py:723
  3.0 11.1 %all-to-all-start = ((f32[128,2,128]{2,1,0:T(2,128)}), f32[128,2,128]{2,1,0:T(2,128)S(1)}, u32[]{:S(2)}, u32[]{:S(2)}) async-start(f32[128,2,128]{2,1,0:T(2,128)} %bitcast.22), calls=%async_computation | async-start | bytes 262144 | tf_op jit(solution)/shard_map/all_to_all | solution.py:774
  14.1 3.7 %start.1 = (f32[2,125,8,128]{3,2,1,0:T(8,128)}, f32[125,8,128]{2,1,0:T(8,128)}, f32[125,8,128]{2,1,0:T(8,128)}, f32[2,25,8,128]{3,2,1,0:T(8,128)}, f32[12288,8,1...) custom-call(f32[2,5,40,640]{3,2,1,0:T(8,128)} %bitcast.20, ...), custom_call_target="tpu_custom_call" | custom-call | flops 100000000 | bytes 4000000 | tf_op jit(solution)/shard_map/start/pallas_call | solution.py:723
  17.9 0.0 copy-start.2
  17.9 0.0 copy-start
  17.9 0.0 copy-start.5
  17.9 2.5 %collective-permute-start.2 = (f32[1,18,8,128]{3,2,1,0:T(8,128)}, f32[1,18,8,128]{3,2,1,0:T(8,128)S(1)}, u32[]{:S(2)}, u32[]{:S(2)}) collective-permute-start(f32[1,18,8,128]{3,2,1,0:T(8,128)} %get-tuple-element.50), channel_id=1, source_target_pairs={{0,16},{16,32},{32,48},{48,64},{64,80},{80,96},{96,112},{112,0},{1... | collective-permute-start | bytes 221192 | tf_op jit(solution)/shard_map/ppermute | solution.py:740
  20.4 3.2 %collective-permute-start.3 = (f32[1,18,8,128]{3,2,1,0:T(8,128)}, f32[1,18,8,128]{3,2,1,0:T(8,128)S(1)}, u32[]{:S(2)}, u32[]{:S(2)}) collective-permute-start(f32[1,18,8,128]{3,2,1,0:T(8,128)} %get-tuple-element.51), channel_id=1, source_target_pairs={{16,0},{32,16},{48,32},{64,48},{80,64},{96,80},{112,96},{0,112},{1... | collective-permute-start | bytes 221192 | tf_op jit(solution)/shard_map/ppermute | solution.py:740
  23.6 0.0 all-to-all-done
  23.6 5.1 %first_force.1 = (f32[2,125,8,128]{3,2,1,0:T(8,128)S(1)}, f32[2,18,8,128]{3,2,1,0:T(8,128)S(1)}, f32[2,18,8,128]{3,2,1,0:T(8,128)S(1)}, f32[2,5,8,128]{3,2,1,0:T(8,128)S(1)}, f32[2,5,8,128]{3,2,1,0:T(8,128)S(1)}) custom-call(f32[256,128]{1,0:T(8,128)S(1)} %bitcast.17, f32[12288,8,128]{2,1,0:T(8,128)} %get-tuple-element.47.kept), custom_call_target="tpu_custom_call" | custom-call | flops 4000000000 | bytes 4000000 | tf_op jit(solution)/shard_map/first_force/pallas_call | solution.py:723
  28.7 1.2 %collective-permute-start = (f32[2,18,8,128]{3,2,1,0:T(8,128)S(1)}, f32[2,18,8,128]{3,2,1,0:T(8,128)S(1)}, u32[]{:S(2)}, u32[]{:S(2)}) collective-permute-start(f32[2,18,8,128]{3,2,1,0:T(8,128)S(1)} %get-tuple-element.48), channel_id=1, source_target_pairs={{0,16},{16,32},{32,48},{48,64},{64,80},{80,96},{96,112},{112,0},{1... | collective-permute-start | bytes 442376 | tf_op jit(solution)/shard_map/ppermute | solution.py:740
  30.0 4.5 %collective-permute-start.1 = (f32[2,18,8,128]{3,2,1,0:T(8,128)S(1)}, f32[2,18,8,128]{3,2,1,0:T(8,128)S(1)}, u32[]{:S(2)}, u32[]{:S(2)}) collective-permute-start(f32[2,18,8,128]{3,2,1,0:T(8,128)S(1)} %get-tuple-element.49), channel_id=1, source_target_pairs={{16,0},{32,16},{48,32},{64,48},{80,64},{96,80},{112,96},{0,112},{1... | collective-permute-start | bytes 442376 | tf_op jit(solution)/shard_map/ppermute | solution.py:740
  34.4 4.8 %source.2 = (f32[2,128,8,128]{3,2,1,0:T(8,128)S(1)}, f32[8,128]{1,0:T(8,128)S(1)}) custom-call(f32[256,128]{1,0:T(8,128)S(1)} %bitcast.18, f32[2,5,8,128]{3,2,1,0:T(8,128)S(1)} %get-tuple-element.52.order.refs_4_), custom_call_target="tpu_custom_call" | custom-call | flops 4000000000 | bytes 4000000 | tf_op jit(solution)/shard_map/source/pallas_call | solution.py:723
  39.3 0.0 collective-permute-done.2.refs_2_.refs_3_
  39.3 0.0 collective-permute-done.3.refs_3_.refs_4_
  39.3 0.0 collective-permute-done.refs_0_.refs_1_
  39.3 0.0 collective-permute-done.1.refs_1_.refs_2_
  39.3 0.0 copy-done.2
  39.3 0.1 rows.1
  39.5 1.9 %collective-permute-start.5 = (f32[25,8,128]{2,1,0:T(8,128)S(1)}, f32[25,8,128]{2,1,0:T(8,128)S(1)}, u32[]{:S(2)}, u32[]{:S(2)}) collective-permute-start(f32[25,8,128]{2,1,0:T(8,128)S(1)} %get-tuple-element.58), channel_id=1, source_target_pairs={{0,15},{1,2},{2,1},{3,4},{4,3},{5,6},{6,5},{7,8},{8,7},{9,10},{10,... | collective-permute-start | bytes 307208 | tf_op jit(solution)/shard_map/ppermute | solution.py:830
  41.3 0.0 collective-permute-start.4
  41.3 0.0 copy-done
  41.3 2.0 %first_guess.1 = (f32[2,125,8,128]{3,2,1,0:T(8,128)S(1)}, f32[2,125,8,128]{3,2,1,0:T(8,128)S(1)}, f32[125,8,128]{2,1,0:T(8,128)S(1)}, f32[2,125,8,128]{3,2,1,0:T(8,128)S(1)}) custom-call(f32[2,125,8,128]{3,2,1,0:T(8,128)S(1)} %get-tuple-element.60.refs_0_, f32[2,18,8,128]{3,2,1,0:T(8,128)S(1)} %collective-permute-done.refs_0_.refs_1_, ...), custom_call_target="tpu_custom_call" | custom-call | flops 100000000 | bytes 4000000 | tf_op jit(solution)/shard_map/first_guess/pallas_call | solution.py:723
  43.3 2.4 %collective-permute-done.5.refs_1_.refs_3_ = f32[25,8,128]{2,1,0:T(8,128)S(1)} collective-permute-done((f32[25,8,128]{2,1,0:T(8,128)S(1)}, f32[25,8,128]{2,1,0:T(8,128)S(1)}, u32[]{:S(2)}, u32[]{:S(2)}) %collective-permute-start.5) | collective-permute-done | bytes 102432 | tf_op jit(solution)/shard_map/ppermute | solution.py:830
  45.7 0.0 collective-permute-done.4.refs_0_.refs_2_
  45.7 0.7 first_fix.1
  46.4 1.5 %collective-permute-start.6 = (f32[2,18,8,128]{3,2,1,0:T(8,128)S(1)}, f32[2,18,8,128]{3,2,1,0:T(8,128)S(1)}, u32[]{:S(2)}, u32[]{:S(2)}) collective-permute-start(f32[2,18,8,128]{3,2,1,0:T(8,128)S(1)} %get-tuple-element.70), channel_id=1, source_target_pairs={{0,16},{16,32},{32,48},{48,64},{64,80},{80,96},{96,112},{112,0},{1... | collective-permute-start | bytes 442376 | tf_op jit(solution)/shard_map/ppermute | solution.py:740
  47.9 4.2 %collective-permute-start.7 = (f32[2,18,8,128]{3,2,1,0:T(8,128)S(1)}, f32[2,18,8,128]{3,2,1,0:T(8,128)S(1)}, u32[]{:S(2)}, u32[]{:S(2)}) collective-permute-start(f32[2,18,8,128]{3,2,1,0:T(8,128)S(1)} %get-tuple-element.71.order), channel_id=1, source_target_pairs={{16,0},{32,16},{48,32},{64,48},{80,64},{96,80},{112,96},{0,112},{1... | collective-permute-start | bytes 442376 | tf_op jit(solution)/shard_map/ppermute | solution.py:740
  52.1 5.3 %source.3 = (f32[2,128,8,128]{3,2,1,0:T(8,128)S(1)}, f32[8,128]{1,0:T(8,128)}) custom-call(f32[256,128]{1,0:T(8,128)S(1)} %bitcast.19, f32[2,18,8,128]{3,2,1,0:T(8,128)S(1)} %get-tuple-element.71.order), custom_call_target="tpu_custom_call" | custom-call | flops 4000000000 | bytes 4000000 | tf_op jit(solution)/shard_map/source/pallas_call | solution.py:723
  57.4 0.0 collective-permute-done.6.refs_1_
  57.4 0.0 collective-permute-done.7.refs_2_
  57.4 0.5 advance.1
  57.9 1.5 %collective-permute-start.9 = (f32[2,20,8,128]{3,2,1,0:T(8,128)S(1)}, f32[2,20,8,128]{3,2,1,0:T(8,128)S(1)}, u32[]{:S(2)}, u32[]{:S(2)}) collective-permute-start(f32[2,20,8,128]{3,2,1,0:T(8,128)S(1)} %get-tuple-element.77), channel_id=1, source_target_pairs={{0,15},{1,2},{2,1},{3,4},{4,3},{5,6},{6,5},{7,8},{8,7},{9,10},{10,... | collective-permute-start | bytes 491528 | tf_op jit(solution)/shard_map/ppermute | solution.py:830
  59.5 0.0 collective-permute-start.8
  59.5 2.1 %first_term.1 = (f32[125,8,128]{2,1,0:T(8,128)S(1)}, f32[8,128]{1,0:T(8,128)S(1)}) custom-call(f32[2,125,8,128]{3,2,1,0:T(8,128)S(1)} %get-tuple-element.65.refs_4_.refs_3_.d, f32[2,50,8,128]{3,2,1,0:T(8,128)S(1)} %get-tuple-element.72.refs_4_.d_edge, bf16[2,2,5,40,640]{4,3,2,1,0:T(8,128)(2,1)S(1)} %bitcast.14, f32[2,20,8,128]{3,2,1,0:T(8,128)S(1)} %get-tuple-element.76.order), custom_call_target="tpu_custom_call" | custom-call | flops 100000000 | bytes 4000000 | tf_op jit(solution)/shard_map/first_term/pallas_call | solution.py:723
  61.6 1.3 %second_guess.1.refs_8_ = f32[2,125,8,128]{3,2,1,0:T(8,128)S(1)} custom-call(f32[2,125,8,128]{3,2,1,0:T(8,128)S(1)} %get-tuple-element.79.d.refs_6_, f32[2,128,8,128]{3,2,1,0:T(8,128)S(1)} %get-tuple-element.75.refs_9_.source, f32[125,8,128]{2,1,0:T(8,128)S(1)} %copy-done, f32[2,20,8,128]{3,2,1,0:T(8,128)S(1)} %get-tuple-element.76.order), custom_call_target="tpu_custom_call" | custom-call | flops 100000000 | bytes 4000000 | tf_op jit(solution)/shard_map/second_guess/pallas_call | solution.py:723
  62.9 2.0 %collective-permute-done.9.refs_1_ = f32[2,20,8,128]{3,2,1,0:T(8,128)S(1)} collective-permute-done((f32[2,20,8,128]{3,2,1,0:T(8,128)S(1)}, f32[2,20,8,128]{3,2,1,0:T(8,128)S(1)}, u32[]{:S(2)}, u32[]{:S(2)}) %collective-permute-start.9) | collective-permute-done | bytes 163872 | tf_op jit(solution)/shard_map/ppermute | solution.py:830
  64.9 0.0 collective-permute-done.8.refs_0_
  64.9 0.9 %second_fix.1 = (f32[2,50,8,128]{3,2,1,0:T(8,128)S(1)}, f32[2,50,8,128]{3,2,1,0:T(8,128)S(1)}, f32[2,125,8,128]{3,2,1,0:T(8,128)S(1)}, f32[2,18,8,128]{3,2,1,0:T(8,128)S(1)}, f32[2,18,8,128]{3,2,1,0:T(8,128)S(1)}) custom-call(f32[2,20,8,128]{3,2,1,0:T(8,128)S(1)} %collective-permute-done.8.refs_0_, f32[2,20,8,128]{3,2,1,0:T(8,128)S(1)} %collective-permute-done.9.refs_1_, ...), custom_call_target="tpu_custom_call" | custom-call | flops 10000000 | bytes 4000000 | tf_op jit(solution)/shard_map/second_fix/pallas_call | solution.py:723
  65.8 0.5 collective-permute-start.10
  66.3 5.2 %collective-permute-start.11 = (f32[2,18,8,128]{3,2,1,0:T(8,128)S(1)}, f32[2,18,8,128]{3,2,1,0:T(8,128)S(1)}, u32[]{:S(2)}, u32[]{:S(2)}) collective-permute-start(f32[2,18,8,128]{3,2,1,0:T(8,128)S(1)} %get-tuple-element.84), channel_id=1, source_target_pairs={{16,0},{32,16},{48,32},{64,48},{80,64},{96,80},{112,96},{0,112},{1... | collective-permute-start | bytes 442376 | tf_op jit(solution)/shard_map/ppermute | solution.py:740
  71.5 3.0 %last_term.1 = (f32[5,40,640]{2,1,0:T(8,128)}, f32[8,128]{1,0:T(8,128)S(1)}) custom-call(f32[2,125,8,128]{3,2,1,0:T(8,128)S(1)} %get-tuple-element.79.d.refs_6_, f32[2,50,8,128]{3,2,1,0:T(8,128)S(1)} %get-tuple-element.86.d_edge, bf16[2,2,5,40,640]{4,3,2,1,0:T(8,128)(2,1)S(1)} %bitcast.15, f32[125,8,128]{2,1,0:T(8,128)S(1)} %get-tuple-element.87.before, ...), custom_call_target="tpu_custom_call" | custom-call | flops 100000000 | bytes 4000000 | tf_op jit(solution)/shard_map/last_term/pallas_call | solution.py:723
  74.5 1.0 %inner_velocity.1 = (f32[2,5,40,640]{3,2,1,0:T(8,128)}, f32[8,128]{1,0:T(8,128)S(1)}) custom-call(f32[2,125,8,128]{3,2,1,0:T(8,128)S(1)} %get-tuple-element.82.f.refs_0_, f32[2,125,8,128]{3,2,1,0:T(8,128)S(1)} %get-tuple-element.80.refs_7_.q.refs_3_, f32[2,50,8,128]{3,2,1,0:T(8,128)S(1)} %get-tuple-element.85.q_edge.refs_4_, ...), custom_call_target="tpu_custom_call" | custom-call | flops 10000000 | bytes 4000000 | tf_op jit(solution)/shard_map/inner_velocity/pallas_call | solution.py:723
  75.5 0.6 collective-permute-done.10.refs_1_
  76.1 0.0 collective-permute-done.11.refs_2_
  76.1 0.9 %outer_velocity.1 = f32[2,5,40,640]{3,2,1,0:T(8,128)} custom-call(f32[2,125,8,128]{3,2,1,0:T(8,128)S(1)} %get-tuple-element.82.f.refs_0_, f32[2,18,8,128]{3,2,1,0:T(8,128)S(1)} %collective-permute-done.10.refs_1_, f32[2,18,8,128]{3,2,1,0:T(8,128)S(1)} %collective-permute-done.11.refs_2_, ...), custom_call_target="tpu_custom_call", output_to_operand_aliasing={{}: (7, {})} | custom-call | flops 10000000 | bytes 4000000 | tf_op jit(solution)/shard_map/outer_velocity/pallas_call | solution.py:723
  (7 shorter events, 0.0 us)
Async XLA Ops:
  0.6 40.7 %copy-start.3 = (f32[2,1,5,40,640]{4,3,2,1,0:T(8,128)S(1)}, f32[2,1,5,40,640]{4,3,2,1,0:T(8,128)}, u32[]{:S(2)}) copy-start(f32[2,1,5,40,640]{4,3,2,1,0:T(8,128)} %param.9) | copy-start | bytes 3072004
  0.6 58.8 %copy-start.1 = (bf16[2,2,1,5,40,640]{5,4,3,2,1,0:T(8,128)(2,1)S(1)}, bf16[2,2,1,5,40,640]{5,4,3,2,1,0:T(8,128)(2,1)}, u32[]{:S(2)}) copy-start(bf16[2,2,1,5,40,640]{5,4,3,2,1,0:T(8,128)(2,1)} %param.12) | copy-start | bytes 3072004
  3.0 20.7 %all-to-all-start = ((f32[128,2,128]{2,1,0:T(2,128)}), f32[128,2,128]{2,1,0:T(2,128)S(1)}, u32[]{:S(2)}, u32[]{:S(2)}) async-start(f32[128,2,128]{2,1,0:T(2,128)} %bitcast.22), calls=%async_computation | async-start | bytes 262144 | tf_op jit(solution)/shard_map/all_to_all | solution.py:774
  17.9 21.4 %copy-start.2 = (f32[2,25,8,128]{3,2,1,0:T(8,128)S(1)}, f32[2,25,8,128]{3,2,1,0:T(8,128)}, u32[]{:S(2)}) copy-start(f32[2,25,8,128]{3,2,1,0:T(8,128)} %get-tuple-element.55.refs_7_.refs_3_.refs_4_) | copy-start | bytes 614404
  17.9 23.4 %copy-start = (f32[125,8,128]{2,1,0:T(8,128)S(1)}, f32[125,8,128]{2,1,0:T(8,128)}, u32[]{:S(2)}) copy-start(f32[125,8,128]{2,1,0:T(8,128)} %get-tuple-element.63.refs_8_.wm) | copy-start | bytes 1536004
  17.9 23.4 %copy-start.5 = (f32[125,8,128]{2,1,0:T(8,128)S(1)}, f32[125,8,128]{2,1,0:T(8,128)}, u32[]{:S(2)}) copy-start(f32[125,8,128]{2,1,0:T(8,128)} %get-tuple-element.64.refs_9_) | copy-start | bytes 1536004
  17.9 21.3 %collective-permute-start.2 = (f32[1,18,8,128]{3,2,1,0:T(8,128)}, f32[1,18,8,128]{3,2,1,0:T(8,128)S(1)}, u32[]{:S(2)}, u32[]{:S(2)}) collective-permute-start(f32[1,18,8,128]{3,2,1,0:T(8,128)} %get-tuple-element.50), channel_id=1, source_target_pairs={{0,16},{16,32},{32,48},{48,64},{64,80},{80,96},{96,112},{112,0},{1... | collective-permute-start | bytes 221192 | tf_op jit(solution)/shard_map/ppermute | solution.py:740
  20.4 18.8 %collective-permute-start.3 = (f32[1,18,8,128]{3,2,1,0:T(8,128)}, f32[1,18,8,128]{3,2,1,0:T(8,128)S(1)}, u32[]{:S(2)}, u32[]{:S(2)}) collective-permute-start(f32[1,18,8,128]{3,2,1,0:T(8,128)} %get-tuple-element.51), channel_id=1, source_target_pairs={{16,0},{32,16},{48,32},{64,48},{80,64},{96,80},{112,96},{0,112},{1... | collective-permute-start | bytes 221192 | tf_op jit(solution)/shard_map/ppermute | solution.py:740
  23.6 15.7 %copy-start.6 = (f32[2,5,8,128]{3,2,1,0:T(8,128)S(1)}, f32[2,5,8,128]{3,2,1,0:T(8,128)}, u32[]{:S(2)}) copy-start(f32[2,5,8,128]{3,2,1,0:T(8,128)} %get-tuple-element.54.refs_6_) | copy-start | bytes 122884
  23.6 17.7 %copy-start.4 = (f32[2,125,8,128]{3,2,1,0:T(8,128)S(1)}, f32[2,125,8,128]{3,2,1,0:T(8,128)}, u32[]{:S(2)}) copy-start(f32[2,125,8,128]{3,2,1,0:T(8,128)} %get-tuple-element.61.refs_5_) | copy-start | bytes 3072004
  28.7 10.5 %collective-permute-start = (f32[2,18,8,128]{3,2,1,0:T(8,128)S(1)}, f32[2,18,8,128]{3,2,1,0:T(8,128)S(1)}, u32[]{:S(2)}, u32[]{:S(2)}) collective-permute-start(f32[2,18,8,128]{3,2,1,0:T(8,128)S(1)} %get-tuple-element.48), channel_id=1, source_target_pairs={{0,16},{16,32},{32,48},{48,64},{64,80},{80,96},{96,112},{112,0},{1... | collective-permute-start | bytes 442376 | tf_op jit(solution)/shard_map/ppermute | solution.py:740
  30.0 9.3 %collective-permute-start.1 = (f32[2,18,8,128]{3,2,1,0:T(8,128)S(1)}, f32[2,18,8,128]{3,2,1,0:T(8,128)S(1)}, u32[]{:S(2)}, u32[]{:S(2)}) collective-permute-start(f32[2,18,8,128]{3,2,1,0:T(8,128)S(1)} %get-tuple-element.49), channel_id=1, source_target_pairs={{16,0},{32,16},{48,32},{64,48},{80,64},{96,80},{112,96},{0,112},{1... | collective-permute-start | bytes 442376 | tf_op jit(solution)/shard_map/ppermute | solution.py:740
  39.5 6.3 %collective-permute-start.5 = (f32[25,8,128]{2,1,0:T(8,128)S(1)}, f32[25,8,128]{2,1,0:T(8,128)S(1)}, u32[]{:S(2)}, u32[]{:S(2)}) collective-permute-start(f32[25,8,128]{2,1,0:T(8,128)S(1)} %get-tuple-element.58), channel_id=1, source_target_pairs={{0,15},{1,2},{2,1},{3,4},{4,3},{5,6},{6,5},{7,8},{8,7},{9,10},{10,... | collective-permute-start | bytes 307208 | tf_op jit(solution)/shard_map/ppermute | solution.py:830
  41.3 4.4 %collective-permute-start.4 = (f32[25,8,128]{2,1,0:T(8,128)S(1)}, f32[25,8,128]{2,1,0:T(8,128)S(1)}, u32[]{:S(2)}, u32[]{:S(2)}) collective-permute-start(f32[25,8,128]{2,1,0:T(8,128)S(1)} %get-tuple-element.57.refs_10_), channel_id=1, source_target_pairs={{0,1},{1,0},{2,3},{3,2},{4,5},{5,4},{6,7},{7,6},{8,9},{9,8},{10,11... | collective-permute-start | bytes 307208 | tf_op jit(solution)/shard_map/ppermute | solution.py:830
  46.4 11.0 %collective-permute-start.6 = (f32[2,18,8,128]{3,2,1,0:T(8,128)S(1)}, f32[2,18,8,128]{3,2,1,0:T(8,128)S(1)}, u32[]{:S(2)}, u32[]{:S(2)}) collective-permute-start(f32[2,18,8,128]{3,2,1,0:T(8,128)S(1)} %get-tuple-element.70), channel_id=1, source_target_pairs={{0,16},{16,32},{32,48},{48,64},{64,80},{80,96},{96,112},{112,0},{1... | collective-permute-start | bytes 442376 | tf_op jit(solution)/shard_map/ppermute | solution.py:740
  47.9 9.5 %collective-permute-start.7 = (f32[2,18,8,128]{3,2,1,0:T(8,128)S(1)}, f32[2,18,8,128]{3,2,1,0:T(8,128)S(1)}, u32[]{:S(2)}, u32[]{:S(2)}) collective-permute-start(f32[2,18,8,128]{3,2,1,0:T(8,128)S(1)} %get-tuple-element.71.order), channel_id=1, source_target_pairs={{16,0},{32,16},{48,32},{64,48},{80,64},{96,80},{112,96},{0,112},{1... | collective-permute-start | bytes 442376 | tf_op jit(solution)/shard_map/ppermute | solution.py:740
  57.9 6.9 %collective-permute-start.9 = (f32[2,20,8,128]{3,2,1,0:T(8,128)S(1)}, f32[2,20,8,128]{3,2,1,0:T(8,128)S(1)}, u32[]{:S(2)}, u32[]{:S(2)}) collective-permute-start(f32[2,20,8,128]{3,2,1,0:T(8,128)S(1)} %get-tuple-element.77), channel_id=1, source_target_pairs={{0,15},{1,2},{2,1},{3,4},{4,3},{5,6},{6,5},{7,8},{8,7},{9,10},{10,... | collective-permute-start | bytes 491528 | tf_op jit(solution)/shard_map/ppermute | solution.py:830
  59.5 5.4 %collective-permute-start.8 = (f32[2,20,8,128]{3,2,1,0:T(8,128)S(1)}, f32[2,20,8,128]{3,2,1,0:T(8,128)S(1)}, u32[]{:S(2)}, u32[]{:S(2)}) collective-permute-start(f32[2,20,8,128]{3,2,1,0:T(8,128)S(1)} %get-tuple-element.76.order), channel_id=1, source_target_pairs={{0,1},{1,0},{2,3},{3,2},{4,5},{5,4},{6,7},{7,6},{8,9},{9,8},{10,11... | collective-permute-start | bytes 491528 | tf_op jit(solution)/shard_map/ppermute | solution.py:830
  65.8 10.3 %collective-permute-start.10 = (f32[2,18,8,128]{3,2,1,0:T(8,128)S(1)}, f32[2,18,8,128]{3,2,1,0:T(8,128)S(1)}, u32[]{:S(2)}, u32[]{:S(2)}) collective-permute-start(f32[2,18,8,128]{3,2,1,0:T(8,128)S(1)} %get-tuple-element.83), channel_id=1, source_target_pairs={{0,16},{16,32},{32,48},{48,64},{64,80},{80,96},{96,112},{112,0},{1... | collective-permute-start | bytes 442376 | tf_op jit(solution)/shard_map/ppermute | solution.py:740
  66.3 9.8 %collective-permute-start.11 = (f32[2,18,8,128]{3,2,1,0:T(8,128)S(1)}, f32[2,18,8,128]{3,2,1,0:T(8,128)S(1)}, u32[]{:S(2)}, u32[]{:S(2)}) collective-permute-start(f32[2,18,8,128]{3,2,1,0:T(8,128)S(1)} %get-tuple-element.84), channel_id=1, source_target_pairs={{16,0},{32,16},{48,32},{64,48},{80,64},{96,80},{112,96},{0,112},{1... | collective-permute-start | bytes 442376 | tf_op jit(solution)/shard_map/ppermute | solution.py:740
